TPU v7x, 32 devices: a whole 2x2x4 slice. The times are simulated.
32 devices in a mesh: tm: 8 (over y, x, core), bl: 4 (over z).
Axes of the slice: x: 2, y: 2, z: 4, core: 2. Of those that a mesh axis runs over, the one named last changes fastest.
Arguments:
- visibilities: bfloat16 [16384, 2, 240], P(('tm', 'bl')), may hold values from -12 to 12
- noise_weight: float32 [16384], P(('tm', 'bl')), may hold values from 0.005 to 0.05
- keep_flag: int32 [16384], P(('tm', 'bl')), may hold values 0 or 1
- station_pairs: int32 [2, 16384], P(None, ('tm', 'bl')), may hold values from 0 to 63, as said below
- tile_owner: int32 [16384, 1], P(('tm', 'bl')), may hold values from 0 to 31; in each aligned block of 512 rows (0 to 511, 512 to 1023, ...) at most 32 rows name the same one
- tile_offset: int32 [16384], P(('tm', 'bl')), may hold values from 0 to 131064
- kernel_taps: float32 [8, 16384], P(None, ('tm', 'bl')), may hold values from 0.1 to 1
- gain_field: float32 [8, 64, 8, 2, 240], P('tm', 'bl'), may hold values from 0.25 to 1.75
- sky_grid: float32 [2, 8, 2, 4194304], P(None, None, None, ('tm', 'bl')), may hold values from -4 to 4
Outputs:
- gain_gradient: float32 [8, 64, 8, 2, 240], P('tm', 'bl')
- grid_gradient: float32 [2, 8, 2, 4194304], P(None, None, None, ('tm', 'bl'))
Inputs may be any that keep to these rules, and one draw needn't show every extreme that they name: `station_pairs`: the two stations of a row differ. `tile_owner`: among the rows of one device no value appears more than 32 times, and in some device one appears exactly 32 times.
All inputs are finite; a program needn't handle non-finite values. No bound on the sum of `keep_flag` on one device may be relied on, other than what follows from the above.
Results may differ from a plain program's by a relative error of at most 0.0003.
Values sent between devices are 32-bit elements; how exact they have to be, the bound alone decides.
No kernel may reach another device: no remote copies, remote signals or barrier semaphores. Data moves between devices by JAX's collectives and lax.ppermute only.
A program may use at most 192 MiB of HBM per device.

v0:
```python
import jax
import jax.numpy as jnp
from jax import lax
from jax.sharding import PartitionSpec as P

smoothness = 4.0


def spectral_table(channels, spectral_terms):
    channel_ramp = 2.0 * jnp.arange(channels, dtype=jnp.float32) / (channels - 1) - 1.0
    powers = jnp.arange(spectral_terms, dtype=jnp.float32)
    return channel_ramp[None, :] ** powers[:, None]


def complex_mul(x_re, x_im, y_re, y_im):
    return (x_re * y_re - x_im * y_im, x_re * y_im + x_im * y_re)


def row_grads(visibilities, noise_weight, keep_flag, station_pairs, gains_all, degrid):
    row_count = visibilities.shape[0]
    stations = gains_all.shape[0]
    facets = gains_all.shape[1]
    channels = gains_all.shape[3]
    spectral_terms = degrid.shape[2]
    spectrum = spectral_table(channels, spectral_terms)
    first_station = station_pairs[0]
    second_station = station_pairs[1]
    observed = visibilities.astype(jnp.float32)
    scaling = (noise_weight * keep_flag.astype(jnp.float32))[:, None, None]
    onehot_first = (
        jnp.arange(stations, dtype=jnp.int32)[:, None] == first_station[None, :]
    ).astype(jnp.float32)
    onehot_second = (
        jnp.arange(stations, dtype=jnp.int32)[:, None] == second_station[None, :]
    ).astype(jnp.float32)

    def facet_parts(facet_index):
        gain_slab = lax.dynamic_index_in_dim(gains_all, facet_index, 1, keepdims=False)
        left_gain = jnp.take(gain_slab, first_station, axis=0)
        right_gain = jnp.take(gain_slab, second_station, axis=0)
        degrid_slab = lax.dynamic_index_in_dim(degrid, facet_index, 1, keepdims=False)
        facet_model = jnp.einsum(
            "xtr,tc->xrc", degrid_slab, spectrum, precision=lax.Precision.HIGHEST
        )
        return (left_gain, right_gain, facet_model)

    def add_model(facet_index, running):
        left_gain, right_gain, facet_model = facet_parts(facet_index)
        pair_re, pair_im = complex_mul(
            left_gain[:, 0], left_gain[:, 1], right_gain[:, 0], -right_gain[:, 1]
        )
        vis_re, vis_im = complex_mul(pair_re, pair_im, facet_model[0], facet_model[1])
        return running + jnp.stack([vis_re, vis_im], axis=1)

    predicted = lax.fori_loop(
        0, facets, add_model, jnp.zeros((row_count, 2, channels), jnp.float32)
    )
    error = scaling * (observed - predicted)
    err_re = error[:, 0]
    err_im = error[:, 1]

    def add_grads(facet_index, accums):
        gain_acc, degrid_acc = accums
        left_gain, right_gain, facet_model = facet_parts(facet_index)
        left_re, left_im = (left_gain[:, 0], left_gain[:, 1])
        right_re, right_im = (right_gain[:, 0], right_gain[:, 1])
        model_re, model_im = (facet_model[0], facet_model[1])
        first_re, first_im = complex_mul(err_re, err_im, right_re, right_im)
        grad_are, grad_aim = complex_mul(first_re, first_im, model_re, -model_im)
        second_re, second_im = complex_mul(err_re, -err_im, left_re, left_im)
        grad_bre, grad_bim = complex_mul(second_re, second_im, model_re, model_im)
        third_re, third_im = complex_mul(err_re, err_im, left_re, -left_im)
        grad_mre, grad_mim = complex_mul(third_re, third_im, right_re, right_im)
        grad_left = -jnp.stack([grad_are, grad_aim], axis=1).reshape(row_count, 2 * channels)
        grad_right = -jnp.stack([grad_bre, grad_bim], axis=1).reshape(row_count, 2 * channels)
        per_station = jnp.dot(onehot_first, grad_left, precision=lax.Precision.HIGHEST)
        per_station = per_station + jnp.dot(
            onehot_second, grad_right, precision=lax.Precision.HIGHEST
        )
        gain_acc = lax.dynamic_update_index_in_dim(
            gain_acc, per_station.reshape(stations, 2, channels), facet_index, 1
        )
        grad_model = -jnp.stack([grad_mre, grad_mim], axis=0)
        grad_degrid = jnp.einsum(
            "xrc,tc->xtr", grad_model, spectrum, precision=lax.Precision.HIGHEST
        )
        degrid_acc = lax.dynamic_update_index_in_dim(degrid_acc, grad_degrid, facet_index, 1)
        return (gain_acc, degrid_acc)

    initial = (
        jnp.zeros((stations, facets, 2, channels), jnp.float32),
        jnp.zeros((2, facets, spectral_terms, row_count), jnp.float32),
    )
    return lax.fori_loop(0, facets, add_grads, initial)


def smooth_grad(gain_block):
    step_diff = gain_block[1:] - gain_block[:-1]
    from_below = jnp.pad(step_diff, ((1, 0), (0, 0), (0, 0), (0, 0), (0, 0)))
    from_above = jnp.pad(step_diff, ((0, 1), (0, 0), (0, 0), (0, 0), (0, 0)))
    return smoothness * (from_below - from_above)


def body(
    visibilities,
    noise_weight,
    keep_flag,
    station_pairs,
    tile_owner,
    tile_offset,
    kernel_taps,
    gain_field,
    sky_grid,
):
    row_count = visibilities.shape[0]
    taps_count = kernel_taps.shape[0]
    time_count = lax.axis_size("tm")
    group_count = lax.axis_size("bl")
    device_count = time_count * group_count
    capacity = max(2, 2 * row_count // device_count)
    slot_count = device_count * capacity
    grid_cells = sky_grid.shape[3]
    grid_planes = sky_grid.shape[0] * sky_grid.shape[1] * sky_grid.shape[2]
    row_owner = tile_owner[:, 0]
    owner_hits = (row_owner[:, None] == jnp.arange(device_count, dtype=jnp.int32)[None, :]).astype(
        jnp.int32
    )
    earlier_hits = jnp.cumsum(owner_hits, axis=0) - owner_hits
    slot_rank = jnp.sum(earlier_hits * owner_hits, axis=1)
    slot_index = row_owner * capacity + slot_rank
    send_offsets = jnp.zeros((slot_count,), jnp.int32).at[slot_index].set(tile_offset)
    send_taps = jnp.zeros((slot_count, taps_count), jnp.float32).at[slot_index].set(kernel_taps.T)
    got_offsets, got_taps = (
        lax.all_to_all(send_offsets, ("tm", "bl"), split_axis=0, concat_axis=0, tiled=True),
        lax.all_to_all(send_taps, ("tm", "bl"), split_axis=0, concat_axis=0, tiled=True),
    )
    grid_flat = sky_grid.reshape(grid_planes, grid_cells)
    cell_index = got_offsets[:, None] + jnp.arange(taps_count, dtype=jnp.int32)[None, :]
    tile_values = jnp.sum(grid_flat[:, cell_index] * got_taps[None], axis=2)
    returned = lax.all_to_all(tile_values, ("tm", "bl"), split_axis=1, concat_axis=1, tiled=True)
    degrid = returned[:, slot_index].reshape(
        sky_grid.shape[0], sky_grid.shape[1], sky_grid.shape[2], row_count
    )
    all_gains = lax.all_gather(gain_field, "bl", axis=1, tiled=True)
    data_gains, grad_degrid = row_grads(
        visibilities, noise_weight, keep_flag, station_pairs, all_gains[0], degrid
    )
    summed_gains = lax.psum(data_gains, "bl")
    owned_count = gain_field.shape[1]
    owned_part = lax.dynamic_slice_in_dim(
        summed_gains, lax.axis_index("bl") * owned_count, owned_count, 0
    )[None]
    by_station = lax.all_to_all(gain_field, "tm", split_axis=4, concat_axis=0, tiled=True)
    prior_block = smooth_grad(by_station)
    prior_here = lax.all_to_all(prior_block, "tm", split_axis=0, concat_axis=4, tiled=True)
    gain_gradient = owned_part + prior_here
    send_grad = (
        jnp.zeros((grid_planes, slot_count), jnp.float32)
        .at[:, slot_index]
        .set(grad_degrid.reshape(grid_planes, row_count))
    )
    got_grad = lax.all_to_all(send_grad, ("tm", "bl"), split_axis=1, concat_axis=1, tiled=True)
    local_grid = (
        jnp.zeros((grid_planes, grid_cells), jnp.float32)
        .at[:, cell_index]
        .add(got_grad[:, :, None] * got_taps[None])
    )
    grid_gradient = local_grid.reshape(sky_grid.shape)
    return (gain_gradient, grid_gradient)


def solution(mesh):
    return jax.shard_map(
        body,
        mesh=mesh,
        in_specs=(
            P(("tm", "bl"), None, None),
            P(("tm", "bl")),
            P(("tm", "bl")),
            P(None, ("tm", "bl")),
            P(("tm", "bl"), None),
            P(("tm", "bl")),
            P(None, ("tm", "bl")),
            P("tm", "bl", None, None, None),
            P(None, None, None, ("tm", "bl")),
        ),
        out_specs=(P("tm", "bl", None, None, None), P(None, None, None, ("tm", "bl"))),
        check_vma=False,
    )
```

profile of v0, /device:TPU:9, one launch (start us, length us, event | category | flops | bytes accessed | tf_op | source)
XLA Modules:
  0.0 744.0 jit_solution(9368706463688109850)
XLA Ops:
  10.8 2.6 scatter_custom_fusion
  14.1 6.4 all-to-all-start
  22.2 20.7 %all_gather.3 = f32[1,64,8,2,240]{4,3,1,2,0:T(2,128)} all-gather(f32[1,16,8,2,240]{4,3,1,2,0:T(2,128)S(1)} %copy.79), channel_id=1, replica_groups=mesh['tm'=8,'bl'=4] {'bl'}, dimensions={1}, use_global_device_ids=true | all-gather | bytes 1228800 | tf_op jit(solution)/shard_map/all_gather | solution.py:144
  48.7 16.7 %reshape.393 = f32[32,131072]{1,0:T(8,128)} reshape(f32[2,8,2,131072]{3,2,1,0:T(2,128)} %param.23) | data formatting | bytes 33554432 | tf_op jit(solution)/shard_map/reshape | solution.py:137
  65.4 35.1 %copy.82 = f32[32,131072]{0,1:T(8,128)} copy(f32[32,131072]{1,0:T(8,128)} %reshape.393) | data formatting | bytes 33554432 | tf_op jit(solution)/shard_map/reshape | solution.py:137
  101.9 7.3 all-to-all-start.1
  110.9 122.2 %gather_fusion.4 = f32[8192,32]{1,0:T(8,128)} fusion(f32[32,131072]{0,1:T(8,128)} %copy.82, s32[8192]{0:T(1024)S(1)} %broadcast_clamp_fusion.1), kind=kCustom, calls=%fused_computation.4 | custom fusion | bytes 2129920 | tf_op jit(solution)/shard_map/gather | solution.py:139
  233.1 4.3 all-to-all-start.3
  239.0 7.3 fusion.48
  247.2 5.7 all-to-all-start.2
  259.8 4.3 all-to-all-start.4
  266.4 82.1 %while.34 = (s32[]{:T(128)}, f32[512,2,240]{0,2,1:T(8,128)}, f32[64,8,2,240]{3,2,0,1:T(2,128)}, s32[512]{0:T(512)S(1)}, s32[512]{0:T(512)S(1)}, /*index=5*/f32[2...) while((s32[]{:T(128)}, f32[512,2,240]{0,2,1:T(8,128)}, ...), condition=%wide.region_7.9_spmd.clone, body=%wide.region_6.8_spmd.clone.sunk | while | flops 8735747 | bytes 30760100 | solution.py:55
  267.4 2.6 gather_fusion
  270.6 2.6 gather_fusion.1
  277.7 2.6 gather_fusion
  280.9 2.6 gather_fusion.1
  287.9 2.6 gather_fusion
  291.1 2.6 gather_fusion.1
  298.2 2.6 gather_fusion
  301.4 2.6 gather_fusion.1
  308.4 2.6 gather_fusion
  311.7 2.6 gather_fusion.1
  318.7 2.6 gather_fusion
  321.9 2.6 gather_fusion.1
  329.0 2.6 gather_fusion
  332.2 2.6 gather_fusion.1
  339.2 2.6 gather_fusion
  342.5 2.6 gather_fusion.1
  351.3 165.5 %while.35 = (s32[]{:T(128)}, f32[64,8,2,240]{3,1,2,0:T(8,128)}, f32[2,8,2,512]{3,2,1,0:T(2,128)}, f32[512,240]{0,1:T(8,128)}, f32[64,8,2,240]{3,2,0,1:T(2,128)},...) while((s32[]{:T(128)}, f32[64,8,2,240]{3,1,2,0:T(8,128)}, ...), condition=%wide.region_9.11_spmd.clone.clone.clone, body=%wide.region_8.10_spmd.clone.clone.clone.sunk | while | flops 396215296 | bytes 45429904 | solution.py:94
  352.6 2.6 gather_fusion.3
  356.4 2.6 gather_fusion.2
  368.3 4.0 dynamic_update_slice.30
  373.3 2.6 gather_fusion.3
  377.0 2.6 gather_fusion.2
  388.9 4.0 dynamic_update_slice.30
  393.9 2.6 gather_fusion.3
  409.5 4.0 dynamic_update_slice.30
  430.2 4.0 dynamic_update_slice.30
  450.8 4.0 dynamic_update_slice.30
  471.5 4.0 dynamic_update_slice.30
  492.1 4.0 dynamic_update_slice.30
  512.7 4.0 dynamic_update_slice.30
  520.7 6.0 all-to-all-start.5
  526.9 5.9 sort
  539.0 5.0 multiply_bitcast_fusion
  544.0 134.2 %scatter_custom_fusion.3 = f32[32,131072]{0,1:T(8,128)} fusion(s32[8192]{0:T(1024)S(1)} %get-tuple-element.632, f32[]{:T(128)} %constant.111.clone.1, f32[8192,32]{1,0:T(8,128)} %multiply_bitcast_fusion, s32[8192]{0:T(1024)S(1)} %broadcast_clamp_fusion), kind=kCustom, calls=%fused_computation.103 | custom fusion | flops 262144 | bytes 16777728 | tf_op jit(solution)/shard_map/scatter-add | solution.py:166
  678.2 40.6 %copy.97 = f32[32,131072]{1,0:T(8,128)} copy(f32[32,131072]{0,1:T(8,128)} %scatter_custom_fusion.3) | data formatting | bytes 33554432 | tf_op jit(solution)/shard_map/scatter-add | solution.py:166
  718.8 16.0 %reshape.397 = f32[2,8,2,131072]{3,2,1,0:T(2,128)} reshape(f32[32,131072]{1,0:T(8,128)} %copy.97) | data formatting | bytes 33554432 | tf_op jit(solution)/shard_map/reshape | solution.py:168
  (465 shorter events, 199.6 us)
Async XLA Ops:
  7.2 38.6 %copy-start.9 = (f32[8,512]{1,0:T(8,128)S(1)}, f32[8,512]{1,0:T(8,128)}, u32[]{:S(2)}) copy-start(f32[8,512]{1,0:T(8,128)} %param.21) | copy-start | bytes 49156
  10.8 54.6 %copy-start.10 = (s32[512,1]{0,1:T(1,128)}, s32[512,1]{0,1:T(1,128)S(1)}, u32[]{:S(2)}) copy-start(s32[512,1]{0,1:T(1,128)S(1)} %compare_select_fusion.5) | copy-start | bytes 6148
  14.1 87.8 %all-to-all-start = ((s32[32,32,1]{1,2,0:T(1,128)}), s32[32,32,1]{1,2,0:T(1,128)S(1)}, u32[]{:S(2)}, u32[]{:S(2)}) async-start(s32[32,32,1]{1,2,0:T(1,128)} %bitcast.8), calls=%async_computation | async-start | bytes 32768 | tf_op jit(solution)/shard_map/all_to_all | solution.py:134
  101.9 131.3 %all-to-all-start.1 = ((f32[32,1,256]{2,1,0:T(1,128)}), f32[32,1,256]{2,1,0:T(1,128)S(1)}, u32[]{:S(2)}, u32[]{:S(2)}) async-start(f32[32,1,256]{2,1,0:T(1,128)} %reshape.528), calls=%async_computation.1 | async-start | bytes 65536 | tf_op jit(solution)/shard_map/all_to_all | solution.py:135
  233.1 14.1 %all-to-all-start.3 = ((f32[8,1,7680]{2,1,0:T(1,128)}), f32[8,1,7680]{2,1,0:T(1,128)S(1)}, u32[]{:S(2)}, u32[]{:S(2)}) async-start(f32[8,1,7680]{2,1,0:T(1,128)} %reshape.524), calls=%async_computation.3 | async-start | bytes 491520 | tf_op jit(solution)/shard_map/all_to_all | solution.py:153
  239.0 15.8 %copy-start.5 = (f32[32,32,8]{2,1,0:T(8,128)}, f32[32,32,8]{2,1,0:T(8,128)S(1)}, u32[]{:S(2)}) copy-start(f32[32,32,8]{2,1,0:T(8,128)S(1)} %copy.99) | copy-start | bytes 98308
  247.2 12.6 %all-to-all-start.2 = ((f32[32,1,1024]{2,1,0:T(1,128)}), f32[32,1,1024]{2,1,0:T(1,128)S(1)}, u32[]{:S(2)}, u32[]{:S(2)}) async-start(f32[32,1,1024]{2,1,0:T(1,128)} %reshape.530), calls=%async_computation.2 | async-start | bytes 262144 | tf_op jit(solution)/shard_map/all_to_all | solution.py:140
  259.8 260.9 %all-to-all-start.4 = ((f32[8,1,7680]{2,1,0:T(1,128)}), f32[8,1,7680]{2,1,0:T(1,128)}, u32[]{:S(2)}, u32[]{:S(2)}) async-start(f32[8,1,7680]{2,1,0:T(1,128)} %reshape.526), calls=%async_computation.4 | async-start | bytes 491520 | tf_op jit(solution)/shard_map/all_to_all | solution.py:155
  351.7 3.5 copy-start.7
  355.7 4.4 copy-start
  360.1 4.6 copy-start.1
  360.2 4.6 copy-start.4
  365.7 6.6 copy-start.8
  372.3 3.5 copy-start.7
  376.4 4.4 copy-start
  380.8 4.6 copy-start.1
  380.8 4.6 copy-start.4
  386.3 6.6 copy-start.8
  392.9 3.5 copy-start.7
  397.0 4.4 copy-start
  401.4 4.6 copy-start.1
  401.4 4.6 copy-start.4
  407.0 6.6 copy-start.8
  413.6 3.5 copy-start.7
  417.6 4.4 copy-start
  422.1 4.6 copy-start.1
  422.1 4.6 copy-start.4
  427.6 6.6 copy-start.8
  434.2 3.5 copy-start.7
  438.3 4.4 copy-start
  442.7 4.7 copy-start.1
  442.7 4.7 copy-start.4
  448.3 6.6 copy-start.8
  458.9 4.4 copy-start
  463.3 4.6 copy-start.1
  463.4 4.6 copy-start.4
  468.9 6.6 copy-start.8
  479.6 4.4 copy-start
  484.0 4.7 copy-start.1
  484.0 4.7 copy-start.4
  489.6 6.6 copy-start.8
  500.2 4.4 copy-start
  504.6 4.6 copy-start.1
  504.6 4.6 copy-start.4
  510.2 6.6 copy-start.8
  519.8 19.3 %copy-start.6 = (f32[32,32,8]{2,1,0:T(8,128)S(1)}, f32[32,32,8]{2,1,0:T(8,128)}, u32[]{:S(2)}) copy-start(f32[32,32,8]{2,1,0:T(8,128)} %copy-done.5) | copy-start | bytes 98308
  520.7 17.2 %all-to-all-start.5 = ((f32[32,1,1024]{2,1,0:T(1,128)}), f32[32,1,1024]{2,1,0:T(1,128)S(1)}, u32[]{:S(2)}, u32[]{:S(2)}) async-start(f32[32,1,1024]{2,1,0:T(1,128)} %reshape.532), calls=%async_computation.5 | async-start | bytes 262144 | tf_op jit(solution)/shard_map/all_to_all | solution.py:162
  526.7 208.1 %all-reduce.4.cloned.1.call-start = ((), (), s32[]{:S(2)}) async-start(), calls=%async_computation.6 | async-start | bytes 2097152 | tf_op jit(solution)/shard_map/psum | solution.py:148
  (19 other events, 31.1 us)
Sparse Core Ops, SparseCore 0:
  533.0 52.0 all-reduce.3
where the time goes:
time: 756 us; the launch traced here: 744 us
  local copies, waits for them, and re-layouts  414 us (55%)
  other arithmetic  209 us (28%)
  matrix products  48 us (6%)
  starting transfers between devices  34.2 us (5%)
  blocking collectives  20.7 us (3%)
  between operations  14.8 us (2%)
    scatter-add x3, other arithmetic, body(): local_grid = jnp.zeros((grid_planes, grid_cells), jnp.float32).at[:, cell...  140 us
    gather x1, local copies, waits for them, and re-layouts, body(): tile_values = jnp.sum(grid_flat[:, cell_index] * got_taps[None], axis=2)  122 us
    reshape x2, local copies, waits for them, and re-layouts, body(): grid_flat = sky_grid.reshape(grid_planes, grid_cells)  51.8 us
    gather x32, local copies, waits for them, and re-layouts, facet_parts(): right_gain = jnp.take(gain_slab, second_station, axis=0)  49.2 us
    gather x32, local copies, waits for them, and re-layouts, facet_parts(): left_gain = jnp.take(gain_slab, first_station, axis=0)  49.2 us
    scatter-add x2, local copies, waits for them, and re-layouts, body(): local_grid = jnp.zeros((grid_planes, grid_cells), jnp.float32).at[:, cell...  40.6 us
    dynamic_update_slice x8, local copies, waits for them, and re-layouts, add_grads(): lax.dynamic_update_index_in_dim(gain_acc, per_station.reshape(stations, 2...  32.3 us
    dot_general x16, matrix products, facet_parts(): jnp.einsum('xtr,tc->xrc', degrid_slab, spectrum, precision=lax.Precision....  21.4 us
  transfers between devices with their start and end apart: 7, of which 0 were waited for; matrix products, arithmetic and copies ran while one was open for 88% of the time, Pallas kernels for 0%

commit v1 on v0

v1 whole, which is shorter than its diff:
```python
import functools

import jax
import jax.numpy as jnp
from jax import lax
from jax.experimental import pallas as pl
from jax.experimental.pallas import tpu as pltpu
from jax.sharding import PartitionSpec as P

smoothness = 4.0
LANES = 128
f32 = jnp.float32
bf16 = jnp.bfloat16
i32 = jnp.int32
VMEM = pl.BlockSpec(memory_space=pltpu.VMEM)
SMEM = pl.BlockSpec(memory_space=pltpu.SMEM)
ANY = pl.BlockSpec(memory_space=pl.ANY)
CHUNK = 16


def iota(shape, dim):
    return lax.broadcasted_iota(i32, shape, dim)


def as_bf16(mask):
    return jnp.where(mask, 1.0, 0.0).astype(bf16)


def split(x, pieces):
    out = []
    for _ in range(pieces - 1):
        head = x.astype(bf16)
        out.append(head)
        x = x - head.astype(f32)
    out.append(x.astype(bf16))
    return out


def mm(a, b):
    return jnp.dot(a, b, preferred_element_type=f32)


def mm_nt(a, b):
    return lax.dot_general(a, b, (((1,), (1,)), ((), ())), preferred_element_type=f32)


def params(mib=48):
    return pltpu.CompilerParams(vmem_limit_bytes=mib << 20)


def cost(flops, byte_count):
    return pl.CostEstimate(flops=flops, bytes_accessed=byte_count, transcendentals=0)


def read_wide(ref, count):
    per = ref.shape[0] // count
    return jnp.concatenate(
        [ref[pl.ds(i, count, stride=per), :] for i in range(per)], axis=1
    )


def write_wide(ref, value):
    count = value.shape[0]
    per = ref.shape[0] // count
    for i in range(per):
        ref[pl.ds(i, count, stride=per), :] = value[:, i * LANES : (i + 1) * LANES]


def slots_kernel(
    n, cap, tiles, group, group_count,
    shift_ref, owner_ref, offset_ref, taps_ref, pairs_ref, noise_ref, keep_ref,
    send_ref, rows_ref, cols_ref,
):
    rows = owner_ref.shape[1]
    taps = taps_ref.shape[0]
    width = send_ref.shape[0] // n * LANES
    owner = owner_ref[...]
    hit = iota((n, rows), 0) == owner
    onehot = as_bf16(hit)
    earlier = as_bf16(iota((rows, rows), 0) < iota((rows, rows), 1))
    before = mm(onehot, earlier)
    rank = jnp.sum(jnp.where(hit, before, 0.0), axis=0, keepdims=True)
    at_rank = iota((cap, rows), 0) == rank.astype(i32)
    offset = offset_ref[...]
    base = jnp.minimum(offset // LANES, tiles - 2)
    low = offset - base * LANES
    fields = [taps_ref[k : k + 1, :] for k in range(taps)]
    fields += [low.astype(f32), base.astype(f32)]
    parts = [jnp.where(at_rank, v, 0.0) for v in fields]
    spare = width - len(parts) * cap
    if spare:
        parts.append(jnp.zeros((spare, rows), f32))
    total = None
    for piece in split(jnp.concatenate(parts, axis=0), 3):
        term = mm_nt(onehot, piece)
        total = term if total is None else total + term
    write_wide(send_ref, total)
    station = pairs_ref[...]
    turn = shift_ref[0] - station // group + group_count
    turn = jnp.where(turn >= group_count, turn - group_count, turn)
    local = (turn * group + (station - station // group * group)).astype(f32)
    scale = noise_ref[...] * keep_ref[...].astype(f32)
    table = jnp.concatenate(
        [owner.astype(f32), rank, local, scale, jnp.zeros((3, rows), f32)], axis=0
    )
    rows_ref[...] = table
    cols_ref[...] = table.T


def degrid_kernel(
    n, cap, taps,
    base_ref, recv_ref, sky_ref, out_ref, w_ref, held, blocks, sem,
):
    pairs = sky_ref.shape[0]
    copies = []
    for i in range(pairs):
        copy = pltpu.make_async_copy(sky_ref.at[i], held.at[:, i], sem.at[i])
        copy.start()
        copies.append(copy)
    recv = read_wide(recv_ref, n)
    lane = iota((n, 2 * LANES), 1).astype(f32)
    for j in range(cap):
        place = lane - recv[:, taps * cap + j : taps * cap + j + 1]
        w = jnp.zeros((n, 2 * LANES), f32)
        for k in range(taps):
            w = jnp.where(place == float(k), recv[:, k * cap + j : k * cap + j + 1], w)
        w_ref[j * n : (j + 1) * n, :] = w
    for copy in copies:
        copy.wait()
    block_count = n * cap // LANES
    per_block = LANES // n
    unroll = min(n, 16)
    lane3 = iota((2, pairs, LANES), 2)

    def block(jb, carry):
        def step(g, acc):
            for u in range(unroll):
                at = g * unroll + u
                j = jb * per_block + at // n
                start = base_ref[at % n, j] * 2
                w = w_ref[pl.ds(jb * LANES + at, 1), :]
                window = held[pl.ds(start, 4)]
                prod = window[0:2] * w[:, :LANES] + window[2:4] * w[:, LANES:]
                acc = jnp.where(lane3 == at, jnp.sum(prod, axis=2, keepdims=True), acc)
            return acc

        acc = lax.fori_loop(
            0, LANES // unroll, step, jnp.zeros((2, pairs, LANES), f32)
        )
        blocks[jb] = acc.reshape(2 * pairs, LANES)
        return carry

    lax.fori_loop(0, block_count, block, 0)
    planes = 2 * pairs
    turned = [blocks[jb].T for jb in range(block_count)]
    pieces = []
    for j in range(cap):
        jb, lo = j * n // LANES, j * n % LANES
        pieces.append(turned[jb][lo : lo + n, :planes])
    per_line = LANES // planes
    per = cap // per_line
    for i in range(per):
        line = jnp.concatenate(pieces[i * per_line : (i + 1) * per_line], axis=1)
        out_ref[pl.ds(i, n, stride=per), :] = line


def rows_kernel(
    n, cap, group_count,
    rows_ref, cols_ref, vis_ref, back_ref, *rest,
):
    gain_refs = rest[:group_count]
    out_refs = rest[group_count : 2 * group_count]
    send_ref = rest[2 * group_count]
    gains, g3, spec, a_s, b_s, m_s, e_s, glr_hi, glr_lo, gm_hi, gm_lo = rest[
        2 * group_count + 1 :
    ]
    facets, _, group, channels = gain_refs[0].shape
    rows = cols_ref.shape[0]
    stations = group * group_count
    planes = 4 * facets
    pairs = 2 * facets
    half = m_s.shape[2] // 2
    wide = 2 * half
    cols = cols_ref[...]
    owner_col, rank_col = cols[:, 0:1].astype(i32), cols[:, 1:2].astype(i32)
    first_col, second_col = cols[:, 2:3].astype(i32), cols[:, 3:4].astype(i32)

    gains[...] = jnp.zeros(gains.shape, f32)
    for k in range(group_count):
        for f in range(facets):
            for x in range(2):
                gains[f, k * group : (k + 1) * group, x * half : x * half + channels] = (
                    gain_refs[k][f, x]
                )

    back = jnp.concatenate(split(read_wide(back_ref, n), 3), axis=0)
    lane_n = iota((rows, 3 * n), 1)
    owner3 = as_bf16(
        (lane_n == owner_col) | (lane_n == owner_col + n) | (lane_n == owner_col + 2 * n)
    )
    picked = mm(owner3, back)
    slot_width = cap * planes
    lane_s = iota((rows, slot_width), 1)
    in_slot = lane_s // planes == rank_col
    picked = jnp.where(in_slot, picked, 0.0)
    fold = as_bf16(iota((slot_width, planes), 0) % planes == iota((slot_width, planes), 1))
    degrid = None
    for piece in split(picked, 3):
        term = mm(piece, fold)
        degrid = term if degrid is None else degrid + term
    term_scale = jnp.where(
        iota((1, planes), 1) >= pairs, 1.0 / (channels - 1), 1.0
    )
    d3 = jnp.concatenate(split(degrid * term_scale, 3), axis=1)

    lane_st = iota((rows, 3 * stations), 1)
    first3 = as_bf16(
        (lane_st == first_col)
        | (lane_st == first_col + stations)
        | (lane_st == first_col + 2 * stations)
    )
    second3 = as_bf16(
        (lane_st == second_col)
        | (lane_st == second_col + stations)
        | (lane_st == second_col + 2 * stations)
    )
    plane = iota((3 * planes, wide), 0) % planes
    lane_w = iota((3 * planes, wide), 1)
    chan = jnp.where(lane_w >= half, lane_w - half, lane_w)
    side = jnp.where(lane_w >= half, 1, 0)
    value = jnp.where(plane >= pairs, 2 * chan - (channels - 1), 1).astype(f32)
    live = (chan < channels) & ((plane % pairs) // facets == side)
    value = jnp.where(live, value, 0.0)
    facet_of = plane % facets

    def gather(f, carry):
        for q, piece in enumerate(split(gains[f], 3)):
            g3[q * stations : (q + 1) * stations, :] = piece
        spec[f] = jnp.where(facet_of == f, value, 0.0).astype(bf16)
        table = g3[...]
        a_s[f] = mm(first3, table)
        b_s[f] = mm(second3, table)
        m_s[f] = mm(d3, spec[f])
        return carry

    lax.fori_loop(0, facets, gather, 0)

    def predict(rc, carry):
        at = pl.ds(rc * CHUNK, CHUNK)
        re = jnp.zeros((CHUNK, half), f32)
        im = jnp.zeros((CHUNK, half), f32)
        for f in range(facets):
            a_re, a_im = a_s[f, at, :half], a_s[f, at, half:]
            b_re, b_im = b_s[f, at, :half], b_s[f, at, half:]
            m_re, m_im = m_s[f, at, :half], m_s[f, at, half:]
            p_re = a_re * b_re + a_im * b_im
            p_im = a_im * b_re - a_re * b_im
            re = re + (p_re * m_re - p_im * m_im)
            im = im + (p_re * m_im + p_im * m_re)
        scale = cols_ref[at, 4:5]
        e_s[at, :half] = scale * (re - vis_ref[at, :half].astype(f32))
        e_s[at, half:] = scale * (im - vis_ref[at, half:].astype(f32))
        return carry

    lax.fori_loop(0, rows // CHUNK, predict, 0)

    station_row = iota((stations, rows), 0)
    to_station = jnp.concatenate(
        [
            as_bf16(station_row == rows_ref[2:3, :].astype(i32)),
            as_bf16(station_row == rows_ref[3:4, :].astype(i32)),
        ],
        axis=1,
    )

    def put(hi_ref, lo_ref, at, lanes, value):
        hi = value.astype(bf16)
        hi_ref[at, lanes] = hi
        lo_ref[at, lanes] = (value - hi.astype(f32)).astype(bf16)

    re_lanes, im_lanes = slice(0, half), slice(half, wide)

    def grads(f, grad_degrid):
        def chunk(rc, carry):
            at = pl.ds(rc * CHUNK, CHUNK)
            later = pl.ds(rows + rc * CHUNK, CHUNK)
            e_re, e_im = e_s[at, :half], e_s[at, half:]
            a_re, a_im = a_s[f, at, :half], a_s[f, at, half:]
            b_re, b_im = b_s[f, at, :half], b_s[f, at, half:]
            m_re, m_im = m_s[f, at, :half], m_s[f, at, half:]
            t_re = e_re * m_re + e_im * m_im
            t_im = e_im * m_re - e_re * m_im
            p_re = a_re * b_re + a_im * b_im
            p_im = a_im * b_re - a_re * b_im
            put(glr_hi, glr_lo, at, re_lanes, t_re * b_re - t_im * b_im)
            put(glr_hi, glr_lo, at, im_lanes, t_re * b_im + t_im * b_re)
            put(glr_hi, glr_lo, later, re_lanes, t_re * a_re + t_im * a_im)
            put(glr_hi, glr_lo, later, im_lanes, t_re * a_im - t_im * a_re)
            put(gm_hi, gm_lo, at, re_lanes, e_re * p_re + e_im * p_im)
            put(gm_hi, gm_lo, at, im_lanes, e_im * p_re - e_re * p_im)
            return carry

        lax.fori_loop(0, rows // CHUNK, chunk, 0)
        summed = mm(to_station, glr_hi[...]) + mm(to_station, glr_lo[...])
        for k in range(group_count):
            for x in range(2):
                out_refs[k][f, x] = summed[
                    k * group : (k + 1) * group, x * half : x * half + channels
                ]
        table = spec[f, :planes, :]
        return grad_degrid + (mm_nt(gm_hi[...], table) + mm_nt(gm_lo[...], table))

    grad_degrid = lax.fori_loop(0, facets, grads, jnp.zeros((rows, planes), f32))
    grad3 = jnp.concatenate(split(grad_degrid * term_scale, 3), axis=1)
    spread = as_bf16(
        iota((3 * planes, slot_width), 0) % planes
        == iota((3 * planes, slot_width), 1) % planes
    )
    placed = jnp.where(in_slot, mm(grad3, spread), 0.0)
    owner_rows = as_bf16(iota((n, rows), 0) == rows_ref[0:1, :].astype(i32))
    total = None
    for piece in split(placed, 3):
        term = mm(owner_rows, piece)
        total = term if total is None else total + term
    write_wide(send_ref, total)


def scatter_kernel(n, cap, base_ref, grad_ref, w_ref, out_ref, held, blocks, sem):
    pairs = out_ref.shape[0]
    planes = 2 * pairs
    lines = held.shape[0]
    fill = 32

    def clear(i, carry):
        held[pl.ds(i * fill, fill)] = jnp.zeros((fill, pairs, LANES), f32)
        return carry

    lax.fori_loop(0, lines // fill, clear, 0)
    per_line = LANES // planes
    per = cap // per_line
    pieces = []
    for i in range(per):
        line = grad_ref[pl.ds(i, n, stride=per), :]
        for q in range(per_line):
            pieces.append(line[:, q * planes : (q + 1) * planes])
    per_block = LANES // n
    block_count = cap // per_block
    for jb in range(block_count):
        mine = pieces[jb * per_block : (jb + 1) * per_block]
        joined = mine[0] if per_block == 1 else jnp.concatenate(mine, axis=0)
        blocks[jb] = joined.T
    unroll = min(n, 16)
    lane3 = iota((2, pairs, LANES), 2)

    def block(jb, carry):
        values = blocks[jb].reshape(2, pairs, LANES)

        def step(g, inner):
            for u in range(unroll):
                at = g * unroll + u
                start = base_ref[at % n, jb * per_block + at // n] * 2
                w = w_ref[pl.ds(jb * LANES + at, 1), :]
                value = jnp.sum(
                    jnp.where(lane3 == at, values, 0.0), axis=2, keepdims=True
                )
                held[pl.ds(start, 2)] += value * w[:, :LANES]
                held[pl.ds(start + 2, 2)] += value * w[:, LANES:]
            return inner

        return lax.fori_loop(0, LANES // unroll, step, carry)

    lax.fori_loop(0, block_count, block, 0)
    copies = []
    for i in range(pairs):
        copy = pltpu.make_async_copy(held.at[:, i], out_ref.at[i], sem.at[i])
        copy.start()
        copies.append(copy)
    for copy in copies:
        copy.wait()


def body(
    visibilities,
    noise_weight,
    keep_flag,
    station_pairs,
    tile_owner,
    tile_offset,
    kernel_taps,
    gain_field,
    sky_grid,
):
    rows, _, channels = visibilities.shape
    taps = kernel_taps.shape[0]
    time_count = lax.axis_size("tm")
    group_count = lax.axis_size("bl")
    n = time_count * group_count
    cap = max(2, 2 * rows // n)
    _, facets, terms, cells = sky_grid.shape
    pairs = 2 * facets
    planes = pairs * terms
    tiles = cells // LANES
    group = gain_field.shape[1]
    stations = group * group_count
    both = ("tm", "bl")
    half = -(-channels // LANES) * LANES
    wide = 2 * half

    gain_turned = gain_field[0].transpose(1, 2, 0, 3)
    gathered = [gain_turned]
    for k in range(1, group_count):
        gathered.append(
            lax.ppermute(
                gain_turned, "bl", [(i, (i + k) % group_count) for i in range(group_count)]
            )
        )
    below = lax.ppermute(gain_field, "tm", [(i, i + 1) for i in range(time_count - 1)])
    above = lax.ppermute(gain_field, "tm", [(i + 1, i) for i in range(time_count - 1)])

    fields = taps + 2
    lines = -(-fields * cap // LANES)
    shift = jnp.full((1,), lax.axis_index("bl"), i32)
    send, row_table, col_table = pl.pallas_call(
        functools.partial(slots_kernel, n, cap, tiles, group, group_count),
        out_shape=(
            jax.ShapeDtypeStruct((n * lines, LANES), f32),
            jax.ShapeDtypeStruct((8, rows), f32),
            jax.ShapeDtypeStruct((rows, 8), f32),
        ),
        in_specs=[SMEM] + [VMEM] * 6,
        out_specs=(VMEM,) * 3,
        compiler_params=params(),
        cost_estimate=cost(10**9, 10**6),
        name="slots",
    )(
        shift,
        tile_owner.reshape(1, rows),
        tile_offset.reshape(1, rows),
        kernel_taps,
        station_pairs,
        noise_weight.reshape(1, rows),
        keep_flag.reshape(1, rows),
    )

    def exchange(x):
        x = x.reshape(n, -1, LANES)
        x = lax.all_to_all(x, both, split_axis=0, concat_axis=0, tiled=True)
        return x.reshape(-1, LANES)

    received = exchange(send)
    base = received.reshape(n, lines * LANES)[:, (taps + 1) * cap : (taps + 2) * cap]
    base = jnp.clip(base.astype(i32), 0, tiles - 2)
    sky = (
        sky_grid.reshape(pairs, terms, tiles, LANES)
        .transpose(0, 2, 1, 3)
        .reshape(pairs, terms * tiles, LANES)
    )
    slot_lines = n * cap * planes // LANES
    block_count = n * cap // LANES
    values, weights = pl.pallas_call(
        functools.partial(degrid_kernel, n, cap, taps),
        out_shape=(
            jax.ShapeDtypeStruct((slot_lines, LANES), f32),
            jax.ShapeDtypeStruct((n * cap, 2 * LANES), f32),
        ),
        in_specs=[SMEM, VMEM, ANY],
        out_specs=(VMEM, VMEM),
        scratch_shapes=[
            pltpu.VMEM((terms * tiles, pairs, LANES), f32),
            pltpu.VMEM((block_count, planes, LANES), f32),
            pltpu.SemaphoreType.DMA((pairs,)),
        ],
        compiler_params=params(),
        cost_estimate=cost(10**8, 7 * 10**7),
        name="degrid",
    )(base, received, sky)
    back = exchange(values)

    vis_wide = jnp.pad(visibilities, ((0, 0), (0, 0), (0, half - channels))).reshape(
        rows, wide
    )
    partial_shape = jax.ShapeDtypeStruct((facets, 2, group, channels), f32)
    outs = pl.pallas_call(
        functools.partial(rows_kernel, n, cap, group_count),
        out_shape=(partial_shape,) * group_count
        + (jax.ShapeDtypeStruct((slot_lines, LANES), f32),),
        in_specs=[VMEM] * (4 + group_count),
        out_specs=(VMEM,) * (group_count + 1),
        scratch_shapes=[
            pltpu.VMEM((facets, stations, wide), f32),
            pltpu.VMEM((3 * stations, wide), bf16),
            pltpu.VMEM((facets, 3 * planes, wide), bf16),
            pltpu.VMEM((facets, rows, wide), f32),
            pltpu.VMEM((facets, rows, wide), f32),
            pltpu.VMEM((facets, rows, wide), f32),
            pltpu.VMEM((rows, wide), f32),
            pltpu.VMEM((2 * rows, wide), bf16),
            pltpu.VMEM((2 * rows, wide), bf16),
            pltpu.VMEM((rows, wide), bf16),
            pltpu.VMEM((rows, wide), bf16),
        ],
        compiler_params=params(),
        cost_estimate=cost(2 * 10**10, 10**7),
        name="rowgrads",
    )(row_table, col_table, vis_wide, back, *gathered)

    got = exchange(outs[group_count])
    total = outs[0]
    for k in range(1, group_count):
        total = total + lax.ppermute(
            outs[k], "bl", [(i, (i - k) % group_count) for i in range(group_count)]
        )
    grid = pl.pallas_call(
        functools.partial(scatter_kernel, n, cap),
        out_shape=jax.ShapeDtypeStruct((pairs, terms * tiles, LANES), f32),
        in_specs=[SMEM, VMEM, VMEM],
        out_specs=ANY,
        scratch_shapes=[
            pltpu.VMEM((terms * tiles, pairs, LANES), f32),
            pltpu.VMEM((block_count, planes, LANES), f32),
            pltpu.SemaphoreType.DMA((pairs,)),
        ],
        compiler_params=params(),
        cost_estimate=cost(10**8, 10**8),
        name="scatter",
    )(base, got, weights)
    grid_gradient = (
        grid.reshape(pairs, tiles, terms, LANES)
        .transpose(0, 2, 1, 3)
        .reshape(sky_grid.shape)
    )
    when = lax.axis_index("tm")
    prior = jnp.where(when > 0, gain_field - below, 0.0)
    prior = prior - jnp.where(when < time_count - 1, above - gain_field, 0.0)
    gain_gradient = total.transpose(2, 0, 1, 3)[None] + smoothness * prior
    return (gain_gradient, grid_gradient)


def solution(mesh):
    return jax.shard_map(
        body,
        mesh=mesh,
        in_specs=(
            P(("tm", "bl"), None, None),
            P(("tm", "bl")),
            P(("tm", "bl")),
            P(None, ("tm", "bl")),
            P(("tm", "bl"), None),
            P(("tm", "bl")),
            P(None, ("tm", "bl")),
            P("tm", "bl", None, None, None),
            P(None, None, None, ("tm", "bl")),
        ),
        out_specs=(P("tm", "bl", None, None, None), P(None, None, None, ("tm", "bl"))),
        check_vma=False,
    )
```

time: 756 us -> 154 us (0.20)
  the two profiles are of different devices: /device:TPU:9 before, /device:TPU:0 now
where the time goes in v1:
time: 154 us; the launch traced here: 153 us
  Pallas kernels  69.8 us (45%)
  waiting for transfers between devices  38.5 us (25%)
  starting transfers between devices  17.7 us (11%)
  blocking collectives  14.6 us (9%)
  local copies, waits for them, and re-layouts  10.1 us (7%)
    pallas_call x1, Pallas kernels, body(): pl.pallas_call(functools.partial(rows_kernel, n, cap, group_count), out_s...  25.7 us
    pallas_call x1, Pallas kernels, body(): pl.pallas_call(functools.partial(degrid_kernel, n, cap, taps), out_shape=...  23 us
    ppermute x3, waiting for transfers between devices, body(): lax.ppermute(gain_turned, 'bl', [(i, (i + k) % group_count) for i in rang...  20.6 us
    pallas_call x1, Pallas kernels, body(): pl.pallas_call(functools.partial(scatter_kernel, n, cap), out_shape=jax.S...  20.4 us
    ppermute x3, waiting for transfers between devices, body(): lax.ppermute(outs[k], 'bl', [(i, (i - k) % group_count) for i in range(gr...  17.9 us
    all_to_all x1, blocking collectives, exchange(): x = lax.all_to_all(x, both, split_axis=0, concat_axis=0, tiled=True)  14.6 us
    unnamed x31, local copies, waits for them, and re-layouts  9.82 us
    all_to_all x2, starting transfers between devices, exchange(): x = lax.all_to_all(x, both, split_axis=0, concat_axis=0, tiled=True)  7.4 us
  transfers between devices with their start and end apart: 10, of which 4 were waited for; matrix products, arithmetic and copies ran while one was open for 2% of the time, Pallas kernels for 17%

profile of v1, /device:TPU:0, one launch (start us, length us, event | category | flops | bytes accessed | tf_op | source)
XLA Modules:
  0.0 153.0 jit_solution(1080042599709829855)
XLA Ops:
  0.6 0.0 copy-start.2
  0.6 0.7 copy-done.2
  1.4 0.0 copy-start.3
  1.4 0.7 copy-done.3
  2.0 0.0 copy-start.4
  2.0 0.7 copy-done.4
  2.7 0.0 copy-start.5
  2.7 0.7 copy-done.5
  3.4 0.7 copy-done.6
  4.1 0.7 copy-done.7
  4.8 0.7 slots.1
  5.5 0.7 copy-done.8
  6.2 0.6 copy-done.10
  6.8 14.6 %all_to_all.15 = f32[32,3,128]{2,1,0:T(4,128)S(1)} all-to-all(f32[32,3,128]{2,1,0:T(4,128)S(1)} %reshape.54), channel_id=1, replica_groups=mesh['tm'=8,'bl'=4] {'tm','bl'}, dimensions={0} | all-to-all | bytes 98304 | tf_op jit(solution)/shard_map/all_to_all | solution.py:447
  21.4 0.1 fusion.base_ref
  21.5 23.0 %degrid.1 = (f32[256,128]{1,0:T(8,128)}, f32[1024,256]{1,0:T(8,128)S(1)}) custom-call(s32[32,32]{1,0:T(8,128)S(1)} %fusion.base_ref, f32[96,128]{1,0:T(8,128)S(1)} %reshape.55.recv_ref, f32[16,2048,128]{2,1,0:T(8,128)} %bitcast.44), custom_call_target="tpu_custom_call" | custom-call | flops 100000000 | bytes 70000000 | tf_op jit(solution)/shard_map/degrid/pallas_call | solution.py:460
  44.5 2.6 %all-to-all-start.1 = ((f32[32,8,128]{2,1,0:T(8,128)}), f32[32,8,128]{2,1,0:T(8,128)S(1)}, u32[]{:S(2)}, u32[]{:S(2)}) async-start(f32[32,8,128]{2,1,0:T(8,128)} %bitcast.9), calls=%async_computation.1 | async-start | bytes 262144 | tf_op jit(solution)/shard_map/all_to_all | solution.py:447
  47.1 0.0 copy-done.12
  47.1 0.2 copy.36
  47.3 3.7 %collective-permute-start.2 = (f32[8,2,16,240]{3,2,1,0:T(8,128)S(1)}, f32[8,2,16,240]{3,2,1,0:T(8,128)S(1)}, u32[]{:S(2)}, u32[]{:S(2)}) collective-permute-start(f32[8,2,16,240]{3,2,1,0:T(8,128)S(1)} %bitcast.34), channel_id=1, source_target_pairs={{0,3},{1,0},{2,1},{3,2},{4,7},{5,4},{6,5},{7,6},{8,11},{9,8},{10,9... | collective-permute-start | bytes 737288 | tf_op jit(solution)/shard_map/ppermute | solution.py:413
  51.0 0.0 collective-permute-start.1
  51.0 1.1 collective-permute-start
  52.0 2.0 %collective-permute-start.6 = (f32[1,16,8,2,240]{4,1,3,2,0:T(8,128)S(1)}, f32[1,16,8,2,240]{4,1,3,2,0:T(8,128)}, u32[]{:S(2)}, u32[]{:S(2)}) collective-permute-start(f32[1,16,8,2,240]{4,1,3,2,0:T(8,128)S(1)} %copy.36), channel_id=1, source_target_pairs={{0,4},{4,8},{8,12},{12,16},{16,20},{20,24},{24,28},{1,5},{5,9},{9,... | collective-permute-start | bytes 737288 | tf_op jit(solution)/shard_map/ppermute | solution.py:417
  54.0 1.3 collective-permute-start.7
  55.3 0.0 copy-done.13
  55.3 0.2 copy.29.vis_ref
  55.6 2.1 %collective-permute-done.2.rest_3_ = f32[8,2,16,240]{3,2,1,0:T(8,128)S(1)} collective-permute-done((f32[8,2,16,240]{3,2,1,0:T(8,128)S(1)}, f32[8,2,16,240]{3,2,1,0:T(8,128)S(1)}, u32[]{:S(2)}, u32[]{:S(2)}) %collective-permute-start.2) | collective-permute-done | bytes 245792 | tf_op jit(solution)/shard_map/ppermute | solution.py:413
  57.7 18.5 %collective-permute-done.1.rest_2_ = f32[8,2,16,240]{3,2,1,0:T(8,128)S(1)} collective-permute-done((f32[8,2,16,240]{3,2,1,0:T(8,128)S(1)}, f32[8,2,16,240]{3,2,1,0:T(8,128)S(1)}, u32[]{:S(2)}, u32[]{:S(2)}) %collective-permute-start.1) | collective-permute-done | bytes 245792 | tf_op jit(solution)/shard_map/ppermute | solution.py:413
  76.1 0.0 collective-permute-done.rest_1_
  76.2 0.7 copy-done
  76.9 0.0 all-to-all-done.1
  76.9 0.9 copy-done.1
  77.8 0.9 copy-done.9
  78.8 0.7 copy-done.11
  79.5 25.7 %rowgrads.1 = (f32[8,2,16,240]{3,2,1,0:T(8,128)S(1)}, f32[8,2,16,240]{3,2,1,0:T(8,128)S(1)}, f32[8,2,16,240]{3,2,1,0:T(8,128)S(1)}, f32[8,2,16,240]{3,2,1,0:T(8,128)S(1)}, f32[256,128]{1,0:T(8,128)}) custom-call(f32[8,512]{1,0:T(8,128)S(1)} %copy-done.11, f32[512,8]{1,0:T(8,128)S(1)} %copy-done.9, bf16[512,512]{1,0:T(8,128)(2,1)S(1)} %copy.29.vis_ref, ...), custom_call_target="tpu_custom_call" | custom-call | flops 20000000000 | bytes 10000000 | tf_op jit(solution)/shard_map/rowgrads/pallas_call | solution.py:483
  105.2 0.0 collective-permute-start.3
  105.2 0.3 collective-permute-start.4
  105.5 2.0 %collective-permute-start.5 = (f32[8,2,16,240]{3,2,1,0:T(8,128)S(1)}, f32[8,2,16,240]{3,2,1,0:T(8,128)S(1)}, u32[]{:S(2)}, u32[]{:S(2)}) collective-permute-start(f32[8,2,16,240]{3,2,1,0:T(8,128)S(1)} %get-tuple-element.19), channel_id=1, source_target_pairs={{0,1},{1,2},{2,3},{3,0},{4,5},{5,6},{6,7},{7,4},{8,9},{9,10},{10,1... | collective-permute-start | bytes 737288 | tf_op jit(solution)/shard_map/ppermute | solution.py:510
  107.5 4.8 %all-to-all-start.2 = ((f32[32,8,128]{2,1,0:T(8,128)}), f32[32,8,128]{2,1,0:T(8,128)S(1)}, u32[]{:S(2)}, u32[]{:S(2)}) async-start(f32[32,8,128]{2,1,0:T(8,128)} %bitcast.16), calls=%async_computation.2 | async-start | bytes 262144 | tf_op jit(solution)/shard_map/all_to_all | solution.py:447
  112.4 0.0 collective-permute-done.6
  112.4 0.0 collective-permute-done.7
  112.4 2.0 %collective-permute-done.3 = f32[8,2,16,240]{3,2,1,0:T(8,128)S(1)} collective-permute-done((f32[8,2,16,240]{3,2,1,0:T(8,128)S(1)}, f32[8,2,16,240]{3,2,1,0:T(8,128)S(1)}, u32[]{:S(2)}, u32[]{:S(2)}) %collective-permute-start.3) | collective-permute-done | bytes 245792 | tf_op jit(solution)/shard_map/ppermute | solution.py:510
  114.3 16.0 %collective-permute-done.4 = f32[8,2,16,240]{3,2,1,0:T(8,128)S(1)} collective-permute-done((f32[8,2,16,240]{3,2,1,0:T(8,128)S(1)}, f32[8,2,16,240]{3,2,1,0:T(8,128)S(1)}, u32[]{:S(2)}, u32[]{:S(2)}) %collective-permute-start.4) | collective-permute-done | bytes 245792 | tf_op jit(solution)/shard_map/ppermute | solution.py:510
  130.3 0.0 collective-permute-done.5
  130.3 1.4 bitcast_add_fusion
  131.7 0.9 copy.28
  132.6 0.0 all-to-all-done.2
  132.6 20.4 %scatter.1 = f32[16,2048,128]{2,1,0:T(8,128)} custom-call(s32[32,32]{1,0:T(8,128)S(1)} %fusion.base_ref, f32[256,128]{1,0:T(8,128)S(1)} %bitcast.33, f32[1024,256]{1,0:T(8,128)S(1)} %get-tuple-element.21.w_ref), custom_call_target="tpu_custom_call" | custom-call | flops 100000000 | bytes 100000000 | tf_op jit(solution)/shard_map/scatter/pallas_call | solution.py:513
  (14 shorter events, 0.1 us)
Async XLA Ops:
  0.6 0.7 copy-start.2
  1.4 0.7 copy-start.3
  2.0 0.7 copy-start.4
  2.7 0.7 copy-start.5
  3.4 0.7 copy-start.6
  4.1 0.7 copy-start.7
  4.8 42.4 %copy-start.12 = (f32[1,16,8,2,240]{4,3,2,1,0:T(2,128)S(1)}, f32[1,16,8,2,240]{4,3,2,1,0:T(2,128)}, u32[]{:S(2)}) copy-start(f32[1,16,8,2,240]{4,3,2,1,0:T(2,128)} %param.16) | copy-start | bytes 737284
  4.8 50.5 %copy-start.13 = (bf16[512,2,240]{0,2,1:T(8,128)(2,1)S(1)}, bf16[512,2,240]{0,2,1:T(8,128)(2,1)}, u32[]{:S(2)}) copy-start(bf16[512,2,240]{0,2,1:T(8,128)(2,1)} %param.9) | copy-start | bytes 1474564
  5.5 0.7 copy-start.8
  6.2 0.6 copy-start.10
  44.5 32.3 %all-to-all-start.1 = ((f32[32,8,128]{2,1,0:T(8,128)}), f32[32,8,128]{2,1,0:T(8,128)S(1)}, u32[]{:S(2)}, u32[]{:S(2)}) async-start(f32[32,8,128]{2,1,0:T(8,128)} %bitcast.9), calls=%async_computation.1 | async-start | bytes 262144 | tf_op jit(solution)/shard_map/all_to_all | solution.py:447
  47.3 10.4 %collective-permute-start.2 = (f32[8,2,16,240]{3,2,1,0:T(8,128)S(1)}, f32[8,2,16,240]{3,2,1,0:T(8,128)S(1)}, u32[]{:S(2)}, u32[]{:S(2)}) collective-permute-start(f32[8,2,16,240]{3,2,1,0:T(8,128)S(1)} %bitcast.34), channel_id=1, source_target_pairs={{0,3},{1,0},{2,1},{3,2},{4,7},{5,4},{6,5},{7,6},{8,11},{9,8},{10,9... | collective-permute-start | bytes 737288 | tf_op jit(solution)/shard_map/ppermute | solution.py:413
  51.0 25.2 %collective-permute-start.1 = (f32[8,2,16,240]{3,2,1,0:T(8,128)S(1)}, f32[8,2,16,240]{3,2,1,0:T(8,128)S(1)}, u32[]{:S(2)}, u32[]{:S(2)}) collective-permute-start(f32[8,2,16,240]{3,2,1,0:T(8,128)S(1)} %bitcast.35), channel_id=1, source_target_pairs={{0,2},{1,3},{2,0},{3,1},{4,6},{5,7},{6,4},{7,5},{8,10},{9,11},{10,... | collective-permute-start | bytes 737288 | tf_op jit(solution)/shard_map/ppermute | solution.py:413
  51.0 25.2 %collective-permute-start = (f32[8,2,16,240]{3,2,1,0:T(8,128)S(1)}, f32[8,2,16,240]{3,2,1,0:T(8,128)S(1)}, u32[]{:S(2)}, u32[]{:S(2)}) collective-permute-start(f32[8,2,16,240]{3,2,1,0:T(8,128)S(1)} %bitcast.36), channel_id=1, source_target_pairs={{0,1},{1,2},{2,3},{3,0},{4,5},{5,6},{6,7},{7,4},{8,9},{9,10},{10,1... | collective-permute-start | bytes 737288 | tf_op jit(solution)/shard_map/ppermute | solution.py:413
  52.0 60.3 %collective-permute-start.6 = (f32[1,16,8,2,240]{4,1,3,2,0:T(8,128)S(1)}, f32[1,16,8,2,240]{4,1,3,2,0:T(8,128)}, u32[]{:S(2)}, u32[]{:S(2)}) collective-permute-start(f32[1,16,8,2,240]{4,1,3,2,0:T(8,128)S(1)} %copy.36), channel_id=1, source_target_pairs={{0,4},{4,8},{8,12},{12,16},{16,20},{20,24},{24,28},{1,5},{5,9},{9,... | collective-permute-start | bytes 737288 | tf_op jit(solution)/shard_map/ppermute | solution.py:417
  54.0 58.4 %collective-permute-start.7 = (f32[1,16,8,2,240]{4,1,3,2,0:T(8,128)S(1)}, f32[1,16,8,2,240]{4,1,3,2,0:T(8,128)}, u32[]{:S(2)}, u32[]{:S(2)}) collective-permute-start(f32[1,16,8,2,240]{4,1,3,2,0:T(8,128)S(1)} %copy.36), channel_id=1, source_target_pairs={{4,0},{8,4},{12,8},{16,12},{20,16},{24,20},{28,24},{5,1},{9,5},{13... | collective-permute-start | bytes 737288 | tf_op jit(solution)/shard_map/ppermute | solution.py:418
  76.1 0.7 copy-start
  76.9 1.0 copy-start.1
  77.8 0.9 copy-start.9
  78.8 0.7 copy-start.11
  105.2 9.2 %collective-permute-start.3 = (f32[8,2,16,240]{3,2,1,0:T(8,128)S(1)}, f32[8,2,16,240]{3,2,1,0:T(8,128)S(1)}, u32[]{:S(2)}, u32[]{:S(2)}) collective-permute-start(f32[8,2,16,240]{3,2,1,0:T(8,128)S(1)} %get-tuple-element.17), channel_id=1, source_target_pairs={{0,3},{1,0},{2,1},{3,2},{4,7},{5,4},{6,5},{7,6},{8,11},{9,8},{10,9... | collective-permute-start | bytes 737288 | tf_op jit(solution)/shard_map/ppermute | solution.py:510
  105.2 25.1 %collective-permute-start.4 = (f32[8,2,16,240]{3,2,1,0:T(8,128)S(1)}, f32[8,2,16,240]{3,2,1,0:T(8,128)S(1)}, u32[]{:S(2)}, u32[]{:S(2)}) collective-permute-start(f32[8,2,16,240]{3,2,1,0:T(8,128)S(1)} %get-tuple-element.18), channel_id=1, source_target_pairs={{0,2},{1,3},{2,0},{3,1},{4,6},{5,7},{6,4},{7,5},{8,10},{9,11},{10,... | collective-permute-start | bytes 737288 | tf_op jit(solution)/shard_map/ppermute | solution.py:510
  105.5 24.8 %collective-permute-start.5 = (f32[8,2,16,240]{3,2,1,0:T(8,128)S(1)}, f32[8,2,16,240]{3,2,1,0:T(8,128)S(1)}, u32[]{:S(2)}, u32[]{:S(2)}) collective-permute-start(f32[8,2,16,240]{3,2,1,0:T(8,128)S(1)} %get-tuple-element.19), channel_id=1, source_target_pairs={{0,1},{1,2},{2,3},{3,0},{4,5},{5,6},{6,7},{7,4},{8,9},{9,10},{10,1... | collective-permute-start | bytes 737288 | tf_op jit(solution)/shard_map/ppermute | solution.py:510
  107.5 25.1 %all-to-all-start.2 = ((f32[32,8,128]{2,1,0:T(8,128)}), f32[32,8,128]{2,1,0:T(8,128)S(1)}, u32[]{:S(2)}, u32[]{:S(2)}) async-start(f32[32,8,128]{2,1,0:T(8,128)} %bitcast.16), calls=%async_computation.2 | async-start | bytes 262144 | tf_op jit(solution)/shard_map/all_to_all | solution.py:447

commit v2 on v1

--- a/solution.py
+++ b/solution.py
@@ -44,7 +44,7 @@
     return lax.dot_general(a, b, (((1,), (1,)), ((), ())), preferred_element_type=f32)
 
 
-def params(mib=48):
+def params(mib=60):
     return pltpu.CompilerParams(vmem_limit_bytes=mib << 20)
 
 
@@ -407,16 +407,6 @@
     wide = 2 * half
 
     gain_turned = gain_field[0].transpose(1, 2, 0, 3)
-    gathered = [gain_turned]
-    for k in range(1, group_count):
-        gathered.append(
-            lax.ppermute(
-                gain_turned, "bl", [(i, (i + k) % group_count) for i in range(group_count)]
-            )
-        )
-    below = lax.ppermute(gain_field, "tm", [(i, i + 1) for i in range(time_count - 1)])
-    above = lax.ppermute(gain_field, "tm", [(i + 1, i) for i in range(time_count - 1)])
-
     fields = taps + 2
     lines = -(-fields * cap // LANES)
     shift = jnp.full((1,), lax.axis_index("bl"), i32)
@@ -447,7 +437,14 @@
         x = lax.all_to_all(x, both, split_axis=0, concat_axis=0, tiled=True)
         return x.reshape(-1, LANES)
 
-    received = exchange(send)
+    received, gain_turned = lax.optimization_barrier((exchange(send), gain_turned))
+    gathered = [gain_turned]
+    for k in range(1, group_count):
+        gathered.append(
+            lax.ppermute(
+                gain_turned, "bl", [(i, (i + k) % group_count) for i in range(group_count)]
+            )
+        )
     base = received.reshape(n, lines * LANES)[:, (taps + 1) * cap : (taps + 2) * cap]
     base = jnp.clip(base.astype(i32), 0, tiles - 2)
     sky = (
@@ -474,7 +471,10 @@
         cost_estimate=cost(10**8, 7 * 10**7),
         name="degrid",
     )(base, received, sky)
-    back = exchange(values)
+    values, *gathered = lax.optimization_barrier((values, *gathered))
+    back, gain_here = lax.optimization_barrier((exchange(values), gain_field))
+    below = lax.ppermute(gain_here, "tm", [(i, i + 1) for i in range(time_count - 1)])
+    above = lax.ppermute(gain_here, "tm", [(i + 1, i) for i in range(time_count - 1)])
 
     vis_wide = jnp.pad(visibilities, ((0, 0), (0, 0), (0, half - channels))).reshape(
         rows, wide
@@ -504,11 +504,12 @@
         name="rowgrads",
     )(row_table, col_table, vis_wide, back, *gathered)
 
-    got = exchange(outs[group_count])
-    total = outs[0]
+    *parts, send_grad = outs
+    send_grad, below, above = lax.optimization_barrier((send_grad, below, above))
+    got, *parts = lax.optimization_barrier((exchange(send_grad), *parts))
     for k in range(1, group_count):
-        total = total + lax.ppermute(
-            outs[k], "bl", [(i, (i - k) % group_count) for i in range(group_count)]
+        parts[k] = lax.ppermute(
+            parts[k], "bl", [(i, (i - k) % group_count) for i in range(group_count)]
         )
     grid = pl.pallas_call(
         functools.partial(scatter_kernel, n, cap),
@@ -524,6 +525,10 @@
         cost_estimate=cost(10**8, 10**8),
         name="scatter",
     )(base, got, weights)
+    grid, *parts = lax.optimization_barrier((grid, *parts))
+    total = parts[0]
+    for part in parts[1:]:
+        total = total + part
     grid_gradient = (
         grid.reshape(pairs, tiles, terms, LANES)
         .transpose(0, 2, 1, 3)

time: 154 us -> 127 us (0.82)
  waiting for transfers between devices: 38.5 us -> 16.2 us
  local copies, waits for them, and re-layouts: 10.1 us -> 4.74 us
    ppermute x3, waiting for transfers between devices: 20.6 us -> 0.01 us  [body(): lax.ppermute(gain_turned, 'bl', [(i, (i + k) % group_count) for i in rang...]
    ppermute x5, waiting for transfers between devices: 17.9 us -> 2.5 us  [the longest x3 2.5 us: body(): lax.ppermute(parts[k], 'bl', [(i, (i - k) % group_count) for i in range(g...]
    all_to_all x2, waiting for transfers between devices: 0.01 us -> 13.7 us  [exchange(): x = lax.all_to_all(x, both, split_axis=0, concat_axis=0, tiled=True)]
    unnamed x31 -> x20, local copies, waits for them, and re-layouts: 9.82 us -> 2.06 us
    all_to_all x2, starting transfers between devices: 7.4 us -> 9.88 us  [exchange(): x = lax.all_to_all(x, both, split_axis=0, concat_axis=0, tiled=True)]
    pallas_call x1, Pallas kernels: 25.7 us -> 27.2 us  [body(): pl.pallas_call(functools.partial(rows_kernel, n, cap, group_count), out_s...]
  transfers between devices with their start and end apart: 10 -> 10, of which waited for: 4 -> 3; matrix products, arithmetic and copies ran while one was open for 2% -> 2% of each run, Pallas kernels for 17% -> 54%
where the time goes in v2:
time: 127 us
  Pallas kernels  71.2 us (56%)
  starting transfers between devices  18.8 us (15%)
  waiting for transfers between devices  16.2 us (13%)
  blocking collectives  14.1 us (11%)
  local copies, waits for them, and re-layouts  4.74 us (4%)
    pallas_call x1, Pallas kernels, body(): pl.pallas_call(functools.partial(rows_kernel, n, cap, group_count), out_s...  27.2 us
    pallas_call x1, Pallas kernels, body(): pl.pallas_call(functools.partial(degrid_kernel, n, cap, taps), out_shape=...  21.6 us
    pallas_call x1, Pallas kernels, body(): pl.pallas_call(functools.partial(scatter_kernel, n, cap), out_shape=jax.S...  20.1 us
    all_to_all x1, blocking collectives, exchange(): x = lax.all_to_all(x, both, split_axis=0, concat_axis=0, tiled=True)  14.1 us
    all_to_all x2, waiting for transfers between devices, exchange(): x = lax.all_to_all(x, both, split_axis=0, concat_axis=0, tiled=True)  13.7 us
    all_to_all x2, starting transfers between devices, exchange(): x = lax.all_to_all(x, both, split_axis=0, concat_axis=0, tiled=True)  9.88 us
    ppermute x3, starting transfers between devices, body(): lax.ppermute(gain_turned, 'bl', [(i, (i + k) % group_count) for i in rang...  3.88 us
  transfers between devices with their start and end apart: 10, of which 3 were waited for; matrix products, arithmetic and copies ran while one was open for 2% of the time, Pallas kernels for 54%

profile of v2, /device:TPU:0, one launch (start us, length us, event | category | flops | bytes accessed | tf_op | source)
XLA Modules:
  0.0 126.8 jit_solution(2797046512689666854)
XLA Ops:
  0.6 0.0 copy-start
  0.6 0.0 copy-start.1
  0.7 2.2 %slots.1 = (f32[96,128]{1,0:T(8,128)}, f32[8,512]{1,0:T(8,128)}, f32[512,8]{1,0:T(8,128)}) custom-call(s32[1]{0:T(128)} %bitcast.shift_ref, s32[1,512]{1,0:T(1,128)} %bitcast.40, s32[1,512]{1,0:T(1,128)} %bitcast.41, f32[8,512]{1,0:T(8,128)} %taps_ref.1, s32[2,512]{1,0:T(2,128)} %pairs_ref.1, f32[1,512]{1,0:T(1,128)} %bitcast.42, s32[1,512]{1,0:T(1,128)} %bitcast.43), custom_call_target="tpu_custom_call" | custom-call | flops 1000000000 | bytes 1000000 | tf_op jit(solution)/shard_map/slots/pallas_call | solution.py:413
  2.8 1.4 %reshape.56 = f32[32,3,128]{2,1,0:T(4,128)} reshape(f32[96,128]{1,0:T(8,128)} %get-tuple-element.34) | data formatting | bytes 98304 | tf_op jit(solution)/shard_map/reshape | solution.py:436
  4.3 7.3 %all-to-all-start = ((f32[32,3,128]{2,1,0:T(4,128)}), f32[32,3,128]{2,1,0:T(4,128)S(1)}, u32[]{:S(2)}, u32[]{:S(2)}) async-start(f32[32,3,128]{2,1,0:T(4,128)} %reshape.56), calls=%async_computation | async-start | bytes 131072 | tf_op jit(solution)/shard_map/all_to_all | solution.py:437
  11.6 1.1 copy.32
  12.7 0.0 copy-start.3
  12.7 6.4 %all-to-all-done = f32[32,3,128]{2,1,0:T(4,128)S(1)} async-done(((f32[32,3,128]{2,1,0:T(4,128)}), f32[32,3,128]{2,1,0:T(4,128)S(1)}, u32[]{:S(2)}, u32[]{:S(2)}) %all-to-all-start) | async-done | bytes 49184 | tf_op jit(solution)/shard_map/all_to_all | solution.py:437
  19.1 0.0 copy-start.2
  19.1 0.3 collective-permute-start
  19.4 1.2 collective-permute-start.1
  20.6 2.4 %collective-permute-start.2 = (f32[8,2,16,240]{3,2,1,0:T(8,128)S(1)}, f32[8,2,16,240]{3,2,1,0:T(8,128)S(1)}, u32[]{:S(2)}, u32[]{:S(2)}) collective-permute-start(f32[8,2,16,240]{3,2,1,0:T(8,128)S(1)} %bitcast.35), channel_id=1, source_target_pairs={{0,3},{1,0},{2,1},{3,2},{4,7},{5,4},{6,5},{7,6},{8,11},{9,8},{10,9... | collective-permute-start | bytes 737288 | tf_op jit(solution)/shard_map/ppermute | solution.py:444
  23.0 0.7 fusion.base_ref
  23.7 0.0 copy-done.2
  23.7 21.6 %degrid.1 = (f32[256,128]{1,0:T(8,128)}, f32[1024,256]{1,0:T(8,128)}) custom-call(s32[32,32]{1,0:T(8,128)} %fusion.base_ref, f32[96,128]{1,0:T(8,128)} %copy-done.2, f32[16,2048,128]{2,1,0:T(8,128)} %bitcast.30), custom_call_target="tpu_custom_call" | custom-call | flops 100000000 | bytes 70000000 | tf_op jit(solution)/shard_map/degrid/pallas_call | solution.py:457
  45.3 0.0 collective-permute-done.rest_1_
  45.3 0.0 copy-start.6
  45.4 0.0 collective-permute-done.1.rest_2_
  45.4 0.0 copy-start.7
  45.4 0.0 collective-permute-done.2.rest_3_
  45.4 0.0 copy-start.8
  45.4 2.6 %all-to-all-start.1 = ((f32[32,8,128]{2,1,0:T(8,128)}), f32[32,8,128]{2,1,0:T(8,128)S(1)}, u32[]{:S(2)}, u32[]{:S(2)}) async-start(f32[32,8,128]{2,1,0:T(8,128)} %bitcast.38), calls=%async_computation.1 | async-start | bytes 262144 | tf_op jit(solution)/shard_map/all_to_all | solution.py:437
  48.0 0.0 copy-done.1
  48.0 1.0 copy.29.vis_ref
  49.0 7.3 %all-to-all-done.1 = f32[32,8,128]{2,1,0:T(8,128)S(1)} async-done(((f32[32,8,128]{2,1,0:T(8,128)}), f32[32,8,128]{2,1,0:T(8,128)S(1)}, u32[]{:S(2)}, u32[]{:S(2)}) %all-to-all-start.1) | async-done | bytes 131104 | tf_op jit(solution)/shard_map/all_to_all | solution.py:437
  56.4 0.0 copy-done
  56.4 0.2 copy.23
  56.6 1.3 %collective-permute-start.3 = (f32[1,16,8,2,240]{4,1,3,2,0:T(8,128)S(1)}, f32[1,16,8,2,240]{4,1,3,2,0:T(8,128)S(1)}, u32[]{:S(2)}, u32[]{:S(2)}) collective-permute-start(f32[1,16,8,2,240]{4,1,3,2,0:T(8,128)S(1)} %copy.23), channel_id=1, source_target_pairs={{0,4},{4,8},{8,12},{12,16},{16,20},{20,24},{24,28},{1,5},{5,9},{9,... | collective-permute-start | bytes 737288 | tf_op jit(solution)/shard_map/ppermute | solution.py:476
  57.9 1.3 %collective-permute-start.4 = (f32[1,16,8,2,240]{4,1,3,2,0:T(8,128)S(1)}, f32[1,16,8,2,240]{4,1,3,2,0:T(8,128)S(1)}, u32[]{:S(2)}, u32[]{:S(2)}) collective-permute-start(f32[1,16,8,2,240]{4,1,3,2,0:T(8,128)S(1)} %copy.23), channel_id=1, source_target_pairs={{4,0},{8,4},{12,8},{16,12},{20,16},{24,20},{28,24},{5,1},{9,5},{13... | collective-permute-start | bytes 737288 | tf_op jit(solution)/shard_map/ppermute | solution.py:477
  59.2 0.0 copy-done.3
  59.2 0.0 copy-done.6
  59.2 0.0 copy-done.7
  59.2 0.0 copy-done.8
  59.2 0.0 copy-done.5
  59.2 27.2 %rowgrads.1 = (f32[8,2,16,240]{3,2,1,0:T(8,128)}, f32[8,2,16,240]{3,2,1,0:T(8,128)}, f32[8,2,16,240]{3,2,1,0:T(8,128)}, f32[8,2,16,240]{3,2,1,0:T(8,128)}, f32[256,128]{1,0:T(8,128)}) custom-call(f32[8,512]{1,0:T(8,128)} %get-tuple-element.36.rows_ref, f32[512,8]{1,0:T(8,128)} %get-tuple-element.37.cols_ref, bf16[512,512]{1,0:T(8,128)(2,1)} %copy.29.vis_ref, ...), custom_call_target="tpu_custom_call" | custom-call | flops 20000000000 | bytes 10000000 | tf_op jit(solution)/shard_map/rowgrads/pallas_call | solution.py:483
  86.5 0.0 collective-permute-done.3
  86.5 0.0 collective-permute-done.4
  86.5 14.1 %all_to_all.15 = f32[32,8,128]{2,1,0:T(8,128)} all-to-all(f32[32,8,128]{2,1,0:T(8,128)} %bitcast.39), channel_id=1, replica_groups=mesh['tm'=8,'bl'=4] {'tm','bl'}, dimensions={0} | all-to-all | bytes 262144 | tf_op jit(solution)/shard_map/all_to_all | solution.py:437
  100.6 1.2 collective-permute-start.5
  101.8 0.0 collective-permute-start.6
  101.8 1.2 collective-permute-start.7
  103.0 20.1 %scatter.1 = f32[16,2048,128]{2,1,0:T(8,128)} custom-call(s32[32,32]{1,0:T(8,128)} %fusion.base_ref, f32[256,128]{1,0:T(8,128)} %bitcast.32, f32[1024,256]{1,0:T(8,128)} %get-tuple-element.54.w_ref), custom_call_target="tpu_custom_call" | custom-call | flops 100000000 | bytes 100000000 | tf_op jit(solution)/shard_map/scatter/pallas_call | solution.py:514
  123.1 0.0 collective-permute-done.5
  123.1 2.5 %collective-permute-done.6 = f32[8,2,16,240]{3,2,1,0:T(8,128)S(1)} collective-permute-done((f32[8,2,16,240]{3,2,1,0:T(8,128)}, f32[8,2,16,240]{3,2,1,0:T(8,128)S(1)}, u32[]{:S(2)}, u32[]{:S(2)}) %collective-permute-start.6) | collective-permute-done | bytes 245792 | tf_op jit(solution)/shard_map/ppermute | solution.py:511
  125.6 0.0 collective-permute-done.7
  125.6 0.0 copy-done.4
  125.6 0.2 bitcast_add_fusion
  125.8 0.9 copy.28
  (5 shorter events, 0.1 us)
Async XLA Ops:
  0.6 55.8 %copy-start = (f32[1,16,8,2,240]{4,3,2,1,0:T(2,128)S(1)}, f32[1,16,8,2,240]{4,3,2,1,0:T(2,128)}, u32[]{:S(2)}) copy-start(f32[1,16,8,2,240]{4,3,2,1,0:T(2,128)} %param.16) | copy-start | bytes 737284
  0.6 47.3 %copy-start.1 = (bf16[512,2,240]{0,2,1:T(8,128)(2,1)S(1)}, bf16[512,2,240]{0,2,1:T(8,128)(2,1)}, u32[]{:S(2)}) copy-start(bf16[512,2,240]{0,2,1:T(8,128)(2,1)} %param.9) | copy-start | bytes 1474564
  4.3 14.8 %all-to-all-start = ((f32[32,3,128]{2,1,0:T(4,128)}), f32[32,3,128]{2,1,0:T(4,128)S(1)}, u32[]{:S(2)}, u32[]{:S(2)}) async-start(f32[32,3,128]{2,1,0:T(4,128)} %reshape.56), calls=%async_computation | async-start | bytes 131072 | tf_op jit(solution)/shard_map/all_to_all | solution.py:437
  12.7 46.5 %copy-start.3 = (f32[1,16,8,2,240]{4,1,3,2,0:T(8,128)}, f32[1,16,8,2,240]{4,1,3,2,0:T(8,128)S(1)}, u32[]{:S(2)}) copy-start(f32[1,16,8,2,240]{4,1,3,2,0:T(8,128)S(1)} %copy.32) | copy-start | bytes 737284
  19.1 4.6 %copy-start.2 = (f32[96,128]{1,0:T(8,128)}, f32[96,128]{1,0:T(8,128)S(1)}, u32[]{:S(2)}) copy-start(f32[96,128]{1,0:T(8,128)S(1)} %reshape.57.recv_ref) | copy-start | bytes 147460
  19.1 26.2 %collective-permute-start = (f32[8,2,16,240]{3,2,1,0:T(8,128)S(1)}, f32[8,2,16,240]{3,2,1,0:T(8,128)S(1)}, u32[]{:S(2)}, u32[]{:S(2)}) collective-permute-start(f32[8,2,16,240]{3,2,1,0:T(8,128)S(1)} %bitcast.33), channel_id=1, source_target_pairs={{0,1},{1,2},{2,3},{3,0},{4,5},{5,6},{6,7},{7,4},{8,9},{9,10},{10,1... | collective-permute-start | bytes 737288 | tf_op jit(solution)/shard_map/ppermute | solution.py:444
  19.4 25.9 %collective-permute-start.1 = (f32[8,2,16,240]{3,2,1,0:T(8,128)S(1)}, f32[8,2,16,240]{3,2,1,0:T(8,128)S(1)}, u32[]{:S(2)}, u32[]{:S(2)}) collective-permute-start(f32[8,2,16,240]{3,2,1,0:T(8,128)S(1)} %bitcast.34), channel_id=1, source_target_pairs={{0,2},{1,3},{2,0},{3,1},{4,6},{5,7},{6,4},{7,5},{8,10},{9,11},{10,... | collective-permute-start | bytes 737288 | tf_op jit(solution)/shard_map/ppermute | solution.py:444
  20.6 24.8 %collective-permute-start.2 = (f32[8,2,16,240]{3,2,1,0:T(8,128)S(1)}, f32[8,2,16,240]{3,2,1,0:T(8,128)S(1)}, u32[]{:S(2)}, u32[]{:S(2)}) collective-permute-start(f32[8,2,16,240]{3,2,1,0:T(8,128)S(1)} %bitcast.35), channel_id=1, source_target_pairs={{0,3},{1,0},{2,1},{3,2},{4,7},{5,4},{6,5},{7,6},{8,11},{9,8},{10,9... | collective-permute-start | bytes 737288 | tf_op jit(solution)/shard_map/ppermute | solution.py:444
  45.3 13.8 %copy-start.6 = (f32[8,2,16,240]{3,2,1,0:T(8,128)}, f32[8,2,16,240]{3,2,1,0:T(8,128)S(1)}, u32[]{:S(2)}) copy-start(f32[8,2,16,240]{3,2,1,0:T(8,128)S(1)} %collective-permute-done.rest_1_) | copy-start | bytes 737284
  45.4 13.8 %copy-start.7 = (f32[8,2,16,240]{3,2,1,0:T(8,128)}, f32[8,2,16,240]{3,2,1,0:T(8,128)S(1)}, u32[]{:S(2)}) copy-start(f32[8,2,16,240]{3,2,1,0:T(8,128)S(1)} %collective-permute-done.1.rest_2_) | copy-start | bytes 737284
  45.4 13.8 %copy-start.8 = (f32[8,2,16,240]{3,2,1,0:T(8,128)}, f32[8,2,16,240]{3,2,1,0:T(8,128)S(1)}, u32[]{:S(2)}) copy-start(f32[8,2,16,240]{3,2,1,0:T(8,128)S(1)} %collective-permute-done.2.rest_3_) | copy-start | bytes 737284
  45.4 11.0 %all-to-all-start.1 = ((f32[32,8,128]{2,1,0:T(8,128)}), f32[32,8,128]{2,1,0:T(8,128)S(1)}, u32[]{:S(2)}, u32[]{:S(2)}) async-start(f32[32,8,128]{2,1,0:T(8,128)} %bitcast.38), calls=%async_computation.1 | async-start | bytes 262144 | tf_op jit(solution)/shard_map/all_to_all | solution.py:437
  56.4 2.8 %copy-start.5 = (f32[32,8,128]{2,1,0:T(8,128)}, f32[32,8,128]{2,1,0:T(8,128)S(1)}, u32[]{:S(2)}) copy-start(f32[32,8,128]{2,1,0:T(8,128)S(1)} %all-to-all-done.1) | copy-start | bytes 393220
  56.6 29.9 %collective-permute-start.3 = (f32[1,16,8,2,240]{4,1,3,2,0:T(8,128)S(1)}, f32[1,16,8,2,240]{4,1,3,2,0:T(8,128)S(1)}, u32[]{:S(2)}, u32[]{:S(2)}) collective-permute-start(f32[1,16,8,2,240]{4,1,3,2,0:T(8,128)S(1)} %copy.23), channel_id=1, source_target_pairs={{0,4},{4,8},{8,12},{12,16},{16,20},{20,24},{24,28},{1,5},{5,9},{9,... | collective-permute-start | bytes 737288 | tf_op jit(solution)/shard_map/ppermute | solution.py:476
  57.9 28.6 %collective-permute-start.4 = (f32[1,16,8,2,240]{4,1,3,2,0:T(8,128)S(1)}, f32[1,16,8,2,240]{4,1,3,2,0:T(8,128)S(1)}, u32[]{:S(2)}, u32[]{:S(2)}) collective-permute-start(f32[1,16,8,2,240]{4,1,3,2,0:T(8,128)S(1)} %copy.23), channel_id=1, source_target_pairs={{4,0},{8,4},{12,8},{16,12},{20,16},{24,20},{28,24},{5,1},{9,5},{13... | collective-permute-start | bytes 737288 | tf_op jit(solution)/shard_map/ppermute | solution.py:477
  86.5 39.1 %copy-start.4 = (f32[8,2,16,240]{3,2,1,0:T(8,128)S(1)}, f32[8,2,16,240]{3,2,1,0:T(8,128)}, u32[]{:S(2)}) copy-start(f32[8,2,16,240]{3,2,1,0:T(8,128)} %get-tuple-element.59) | copy-start | bytes 737284
  100.6 22.5 %collective-permute-start.5 = (f32[8,2,16,240]{3,2,1,0:T(8,128)}, f32[8,2,16,240]{3,2,1,0:T(8,128)S(1)}, u32[]{:S(2)}, u32[]{:S(2)}) collective-permute-start(f32[8,2,16,240]{3,2,1,0:T(8,128)} %get-tuple-element.56), channel_id=1, source_target_pairs={{0,3},{1,0},{2,1},{3,2},{4,7},{5,4},{6,5},{7,6},{8,11},{9,8},{10,9... | collective-permute-start | bytes 737288 | tf_op jit(solution)/shard_map/ppermute | solution.py:511
  101.8 23.8 %collective-permute-start.6 = (f32[8,2,16,240]{3,2,1,0:T(8,128)}, f32[8,2,16,240]{3,2,1,0:T(8,128)S(1)}, u32[]{:S(2)}, u32[]{:S(2)}) collective-permute-start(f32[8,2,16,240]{3,2,1,0:T(8,128)} %get-tuple-element.57), channel_id=1, source_target_pairs={{0,2},{1,3},{2,0},{3,1},{4,6},{5,7},{6,4},{7,5},{8,10},{9,11},{10,... | collective-permute-start | bytes 737288 | tf_op jit(solution)/shard_map/ppermute | solution.py:511
  101.8 23.8 %collective-permute-start.7 = (f32[8,2,16,240]{3,2,1,0:T(8,128)}, f32[8,2,16,240]{3,2,1,0:T(8,128)S(1)}, u32[]{:S(2)}, u32[]{:S(2)}) collective-permute-start(f32[8,2,16,240]{3,2,1,0:T(8,128)} %get-tuple-element.58), channel_id=1, source_target_pairs={{0,1},{1,2},{2,3},{3,0},{4,5},{5,6},{6,7},{7,4},{8,9},{9,10},{10,1... | collective-permute-start | bytes 737288 | tf_op jit(solution)/shard_map/ppermute | solution.py:511

commit v3 on v2

--- a/solution.py
+++ b/solution.py
@@ -42,6 +42,14 @@
 
 def mm_nt(a, b):
     return lax.dot_general(a, b, (((1,), (1,)), ((), ())), preferred_element_type=f32)
+
+
+def div(x, k):
+    return x >> (k.bit_length() - 1) if k & (k - 1) == 0 else x // k
+
+
+def mod(x, k):
+    return x & (k - 1) if k & (k - 1) == 0 else x - x // k * k
 
 
 def params(mib=60):
@@ -107,16 +115,22 @@
     cols_ref[...] = table.T
 
 
+def load_kernel(sky_ref, held_ref, sem):
+    copies = []
+    for i in range(sky_ref.shape[0]):
+        copy = pltpu.make_async_copy(sky_ref.at[i], held_ref.at[:, i], sem.at[i])
+        copy.start()
+        copies.append(copy)
+    for copy in copies:
+        copy.wait()
+
+
 def degrid_kernel(
     n, cap, taps,
-    base_ref, recv_ref, sky_ref, out_ref, w_ref, held, blocks, sem,
+    base_ref, recv_ref, held, out_ref, w_ref, blocks,
 ):
-    pairs = sky_ref.shape[0]
-    copies = []
-    for i in range(pairs):
-        copy = pltpu.make_async_copy(sky_ref.at[i], held.at[:, i], sem.at[i])
-        copy.start()
-        copies.append(copy)
+    pairs = held.shape[1]
+    planes = 2 * pairs
     recv = read_wide(recv_ref, n)
     lane = iota((n, 2 * LANES), 1).astype(f32)
     for j in range(cap):
@@ -125,33 +139,32 @@
         for k in range(taps):
             w = jnp.where(place == float(k), recv[:, k * cap + j : k * cap + j + 1], w)
         w_ref[j * n : (j + 1) * n, :] = w
-    for copy in copies:
-        copy.wait()
-    block_count = n * cap // LANES
     per_block = LANES // n
+    block_count = cap // per_block
     unroll = min(n, 16)
     lane3 = iota((2, pairs, LANES), 2)
 
     def block(jb, carry):
-        def step(g, acc):
-            for u in range(unroll):
-                at = g * unroll + u
-                j = jb * per_block + at // n
-                start = base_ref[at % n, j] * 2
-                w = w_ref[pl.ds(jb * LANES + at, 1), :]
-                window = held[pl.ds(start, 4)]
-                prod = window[0:2] * w[:, :LANES] + window[2:4] * w[:, LANES:]
-                acc = jnp.where(lane3 == at, jnp.sum(prod, axis=2, keepdims=True), acc)
-            return acc
-
-        acc = lax.fori_loop(
-            0, LANES // unroll, step, jnp.zeros((2, pairs, LANES), f32)
-        )
-        blocks[jb] = acc.reshape(2 * pairs, LANES)
+        acc = jnp.zeros((2, pairs, LANES), f32)
+        for q in range(per_block):
+            j = jb * per_block + q
+
+            def step(g, acc):
+                first = g * unroll
+                rel = lane3 - (q * n + first)
+                for u in range(unroll):
+                    start = base_ref[j, first + u]
+                    w = w_ref[pl.ds(j * n + first + u, 1), :]
+                    window = held[pl.ds(start, 4)]
+                    prod = window[0:2] * w[:, :LANES] + window[2:4] * w[:, LANES:]
+                    acc = jnp.where(rel == u, jnp.sum(prod, axis=2, keepdims=True), acc)
+                return acc
+
+            acc = lax.fori_loop(0, n // unroll, step, acc)
+        blocks[jb] = acc.reshape(planes, LANES)
         return carry
 
     lax.fori_loop(0, block_count, block, 0)
-    planes = 2 * pairs
     turned = [blocks[jb].T for jb in range(block_count)]
     pieces = []
     for j in range(cap):
@@ -171,7 +184,7 @@
     gain_refs = rest[:group_count]
     out_refs = rest[group_count : 2 * group_count]
     send_ref = rest[2 * group_count]
-    gains, g3, spec, a_s, b_s, m_s, e_s, glr_hi, glr_lo, gm_hi, gm_lo = rest[
+    gains, spec, a_s, b_s, m_s, e_s, glr_hi, glr_lo, gm_hi, gm_lo = rest[
         2 * group_count + 1 :
     ]
     facets, _, group, channels = gain_refs[0].shape
@@ -193,85 +206,75 @@
                     gain_refs[k][f, x]
                 )
 
-    back = jnp.concatenate(split(read_wide(back_ref, n), 3), axis=0)
-    lane_n = iota((rows, 3 * n), 1)
-    owner3 = as_bf16(
-        (lane_n == owner_col) | (lane_n == owner_col + n) | (lane_n == owner_col + 2 * n)
-    )
-    picked = mm(owner3, back)
-    slot_width = cap * planes
-    lane_s = iota((rows, slot_width), 1)
-    in_slot = lane_s // planes == rank_col
-    picked = jnp.where(in_slot, picked, 0.0)
-    fold = as_bf16(iota((slot_width, planes), 0) % planes == iota((slot_width, planes), 1))
-    degrid = None
-    for piece in split(picked, 3):
-        term = mm(piece, fold)
-        degrid = term if degrid is None else degrid + term
-    term_scale = jnp.where(
-        iota((1, planes), 1) >= pairs, 1.0 / (channels - 1), 1.0
-    )
+    owner3 = as_bf16(mod(iota((1, 3 * n), 1), n) == owner_col)
+    per_line = LANES // planes
+    line_count = cap // per_line
+    slot_of = div(iota((1, LANES), 1), planes) - rank_col
+    degrid = jnp.zeros((rows, LANES), f32)
+    for i in range(line_count):
+        line = jnp.concatenate(split(back_ref[pl.ds(i, n, stride=line_count), :], 3), axis=0)
+        degrid = degrid + jnp.where(slot_of == -i * per_line, mm(owner3, line), 0.0)
+    fold = as_bf16(mod(iota((3 * LANES, planes), 0), planes) == iota((3 * LANES, planes), 1))
+    degrid = mm(jnp.concatenate(split(degrid, 3), axis=1), fold)
+    term_scale = jnp.where(iota((1, planes), 1) >= pairs, 1.0 / (channels - 1), 1.0)
     d3 = jnp.concatenate(split(degrid * term_scale, 3), axis=1)
 
-    lane_st = iota((rows, 3 * stations), 1)
-    first3 = as_bf16(
-        (lane_st == first_col)
-        | (lane_st == first_col + stations)
-        | (lane_st == first_col + 2 * stations)
-    )
-    second3 = as_bf16(
-        (lane_st == second_col)
-        | (lane_st == second_col + stations)
-        | (lane_st == second_col + 2 * stations)
-    )
-    plane = iota((3 * planes, wide), 0) % planes
+    lane_st = mod(iota((1, 3 * stations), 1), stations)
+    first3 = as_bf16(lane_st == first_col)
+    second3 = as_bf16(lane_st == second_col)
+    plane = mod(iota((3 * planes, wide), 0), planes)
     lane_w = iota((3 * planes, wide), 1)
     chan = jnp.where(lane_w >= half, lane_w - half, lane_w)
     side = jnp.where(lane_w >= half, 1, 0)
     value = jnp.where(plane >= pairs, 2 * chan - (channels - 1), 1).astype(f32)
-    live = (chan < channels) & ((plane % pairs) // facets == side)
+    live = (chan < channels) & (div(mod(plane, pairs), facets) == side)
     value = jnp.where(live, value, 0.0)
-    facet_of = plane % facets
-
-    def gather(f, carry):
-        for q, piece in enumerate(split(gains[f], 3)):
-            g3[q * stations : (q + 1) * stations, :] = piece
+    facet_of = mod(plane, facets)
+    chunks = [pl.ds(i * CHUNK, CHUNK) for i in range(rows // CHUNK)]
+
+    def gather(f):
+        table = jnp.concatenate(split(gains[f], 3), axis=0)
         spec[f] = jnp.where(facet_of == f, value, 0.0).astype(bf16)
-        table = g3[...]
         a_s[f] = mm(first3, table)
         b_s[f] = mm(second3, table)
         m_s[f] = mm(d3, spec[f])
-        return carry
-
-    lax.fori_loop(0, facets, gather, 0)
-
-    def predict(rc, carry):
-        at = pl.ds(rc * CHUNK, CHUNK)
-        re = jnp.zeros((CHUNK, half), f32)
-        im = jnp.zeros((CHUNK, half), f32)
-        for f in range(facets):
-            a_re, a_im = a_s[f, at, :half], a_s[f, at, half:]
-            b_re, b_im = b_s[f, at, :half], b_s[f, at, half:]
-            m_re, m_im = m_s[f, at, :half], m_s[f, at, half:]
+
+    def load(f, at):
+        return (
+            a_s[f, at, :half], a_s[f, at, half:],
+            b_s[f, at, :half], b_s[f, at, half:],
+            m_s[f, at, :half], m_s[f, at, half:],
+        )
+
+    def predict(f):
+        for at in chunks:
+            a_re, a_im, b_re, b_im, m_re, m_im = load(f, at)
             p_re = a_re * b_re + a_im * b_im
             p_im = a_im * b_re - a_re * b_im
-            re = re + (p_re * m_re - p_im * m_im)
-            im = im + (p_re * m_im + p_im * m_re)
-        scale = cols_ref[at, 4:5]
-        e_s[at, :half] = scale * (re - vis_ref[at, :half].astype(f32))
-        e_s[at, half:] = scale * (im - vis_ref[at, half:].astype(f32))
+            e_s[at, :half] += p_re * m_re - p_im * m_im
+            e_s[at, half:] += p_re * m_im + p_im * m_re
+
+    e_s[...] = -vis_ref[...].astype(f32)
+    gather(0)
+
+    def forward(f, carry):
+        gather(f + 1)
+        predict(f)
         return carry
 
-    lax.fori_loop(0, rows // CHUNK, predict, 0)
-
+    lax.fori_loop(0, facets - 1, forward, 0)
+    predict(facets - 1)
+    e_s[...] = e_s[...] * cols[:, 4:5]
+
+    block = min(rows, 128)
+    block_count = rows // block
     station_row = iota((stations, rows), 0)
-    to_station = jnp.concatenate(
-        [
-            as_bf16(station_row == rows_ref[2:3, :].astype(i32)),
-            as_bf16(station_row == rows_ref[3:4, :].astype(i32)),
-        ],
-        axis=1,
-    )
+    to_first = as_bf16(station_row == rows_ref[2:3, :].astype(i32))
+    to_second = as_bf16(station_row == rows_ref[3:4, :].astype(i32))
+    to_station = []
+    for c in range(block_count):
+        part = slice(c * block, (c + 1) * block)
+        to_station.append(jnp.concatenate([to_first[:, part], to_second[:, part]], axis=1))
 
     def put(hi_ref, lo_ref, at, lanes, value):
         hi = value.astype(bf16)
@@ -281,48 +284,53 @@
     re_lanes, im_lanes = slice(0, half), slice(half, wide)
 
     def grads(f, grad_degrid):
-        def chunk(rc, carry):
-            at = pl.ds(rc * CHUNK, CHUNK)
-            later = pl.ds(rows + rc * CHUNK, CHUNK)
-            e_re, e_im = e_s[at, :half], e_s[at, half:]
-            a_re, a_im = a_s[f, at, :half], a_s[f, at, half:]
-            b_re, b_im = b_s[f, at, :half], b_s[f, at, half:]
-            m_re, m_im = m_s[f, at, :half], m_s[f, at, half:]
-            t_re = e_re * m_re + e_im * m_im
-            t_im = e_im * m_re - e_re * m_im
-            p_re = a_re * b_re + a_im * b_im
-            p_im = a_im * b_re - a_re * b_im
-            put(glr_hi, glr_lo, at, re_lanes, t_re * b_re - t_im * b_im)
-            put(glr_hi, glr_lo, at, im_lanes, t_re * b_im + t_im * b_re)
-            put(glr_hi, glr_lo, later, re_lanes, t_re * a_re + t_im * a_im)
-            put(glr_hi, glr_lo, later, im_lanes, t_re * a_im - t_im * a_re)
-            put(gm_hi, gm_lo, at, re_lanes, e_re * p_re + e_im * p_im)
-            put(gm_hi, gm_lo, at, im_lanes, e_im * p_re - e_re * p_im)
-            return carry
-
-        lax.fori_loop(0, rows // CHUNK, chunk, 0)
-        summed = mm(to_station, glr_hi[...]) + mm(to_station, glr_lo[...])
+        summed = jnp.zeros((stations, wide), f32)
+        table = spec[f, :planes, :]
+        parts = []
+        for c in range(block_count):
+            for i in range(block // CHUNK):
+                at = pl.ds(c * block + i * CHUNK, CHUNK)
+                left = pl.ds(2 * c * block + i * CHUNK, CHUNK)
+                right = pl.ds((2 * c + 1) * block + i * CHUNK, CHUNK)
+                e_re, e_im = e_s[at, :half], e_s[at, half:]
+                a_re, a_im, b_re, b_im, m_re, m_im = load(f, at)
+                t_re = e_re * m_re + e_im * m_im
+                t_im = e_im * m_re - e_re * m_im
+                p_re = a_re * b_re + a_im * b_im
+                p_im = a_im * b_re - a_re * b_im
+                put(glr_hi, glr_lo, left, re_lanes, t_re * b_re - t_im * b_im)
+                put(glr_hi, glr_lo, left, im_lanes, t_re * b_im + t_im * b_re)
+                put(glr_hi, glr_lo, right, re_lanes, t_re * a_re + t_im * a_im)
+                put(glr_hi, glr_lo, right, im_lanes, t_re * a_im - t_im * a_re)
+                put(gm_hi, gm_lo, at, re_lanes, e_re * p_re + e_im * p_im)
+                put(gm_hi, gm_lo, at, im_lanes, e_im * p_re - e_re * p_im)
+            both = pl.ds(2 * c * block, 2 * block)
+            here = pl.ds(c * block, block)
+            summed = summed + (
+                mm(to_station[c], glr_hi[both, :]) + mm(to_station[c], glr_lo[both, :])
+            )
+            parts.append(mm_nt(gm_hi[here, :], table) + mm_nt(gm_lo[here, :], table))
         for k in range(group_count):
             for x in range(2):
                 out_refs[k][f, x] = summed[
                     k * group : (k + 1) * group, x * half : x * half + channels
                 ]
-        table = spec[f, :planes, :]
-        return grad_degrid + (mm_nt(gm_hi[...], table) + mm_nt(gm_lo[...], table))
+        return grad_degrid + jnp.concatenate(parts, axis=0)
 
     grad_degrid = lax.fori_loop(0, facets, grads, jnp.zeros((rows, planes), f32))
     grad3 = jnp.concatenate(split(grad_degrid * term_scale, 3), axis=1)
     spread = as_bf16(
-        iota((3 * planes, slot_width), 0) % planes
-        == iota((3 * planes, slot_width), 1) % planes
-    )
-    placed = jnp.where(in_slot, mm(grad3, spread), 0.0)
+        mod(iota((3 * planes, LANES), 0), planes) == mod(iota((3 * planes, LANES), 1), planes)
+    )
+    heads = [h.astype(f32) for h in split(mm(grad3, spread), 2)]
     owner_rows = as_bf16(iota((n, rows), 0) == rows_ref[0:1, :].astype(i32))
-    total = None
-    for piece in split(placed, 3):
-        term = mm(owner_rows, piece)
-        total = term if total is None else total + term
-    write_wide(send_ref, total)
+    for i in range(line_count):
+        here = slot_of == -i * per_line
+        placed = jnp.concatenate(
+            [jnp.where(here, h, 0.0).astype(bf16) for h in heads], axis=1
+        )
+        total = mm(owner_rows, placed)
+        send_ref[pl.ds(i, n, stride=line_count), :] = total[:, :LANES] + total[:, LANES:]
 
 
 def scatter_kernel(n, cap, base_ref, grad_ref, w_ref, out_ref, held, blocks, sem):
@@ -354,20 +362,25 @@
 
     def block(jb, carry):
         values = blocks[jb].reshape(2, pairs, LANES)
-
-        def step(g, inner):
-            for u in range(unroll):
-                at = g * unroll + u
-                start = base_ref[at % n, jb * per_block + at // n] * 2
-                w = w_ref[pl.ds(jb * LANES + at, 1), :]
-                value = jnp.sum(
-                    jnp.where(lane3 == at, values, 0.0), axis=2, keepdims=True
-                )
-                held[pl.ds(start, 2)] += value * w[:, :LANES]
-                held[pl.ds(start + 2, 2)] += value * w[:, LANES:]
-            return inner
-
-        return lax.fori_loop(0, LANES // unroll, step, carry)
+        for q in range(per_block):
+            j = jb * per_block + q
+
+            def step(g, inner):
+                first = g * unroll
+                rel = lane3 - (q * n + first)
+                for u in range(unroll):
+                    at = pl.ds(base_ref[j, first + u], 4)
+                    w = w_ref[pl.ds(j * n + first + u, 1), :]
+                    value = jnp.sum(
+                        jnp.where(rel == u, values, 0.0), axis=2, keepdims=True
+                    )
+                    held[at] = held[at] + jnp.concatenate(
+                        [value * w[:, :LANES], value * w[:, LANES:]], axis=0
+                    )
+                return inner
+
+            carry = lax.fori_loop(0, n // unroll, step, carry)
+        return carry
 
     lax.fori_loop(0, block_count, block, 0)
     copies = []
@@ -408,7 +421,7 @@
 
     gain_turned = gain_field[0].transpose(1, 2, 0, 3)
     fields = taps + 2
-    lines = -(-fields * cap // LANES)
+    lines = 1 << (-(-fields * cap // LANES) - 1).bit_length()
     shift = jnp.full((1,), lax.axis_index("bl"), i32)
     send, row_table, col_table = pl.pallas_call(
         functools.partial(slots_kernel, n, cap, tiles, group, group_count),
@@ -437,7 +450,24 @@
         x = lax.all_to_all(x, both, split_axis=0, concat_axis=0, tiled=True)
         return x.reshape(-1, LANES)
 
-    received, gain_turned = lax.optimization_barrier((exchange(send), gain_turned))
+    sky = (
+        sky_grid.reshape(pairs, terms, tiles, LANES)
+        .transpose(0, 2, 1, 3)
+        .reshape(pairs, terms * tiles, LANES)
+    )
+    held = pl.pallas_call(
+        load_kernel,
+        out_shape=pltpu.VMEM((terms * tiles, pairs, LANES), f32),
+        in_specs=[ANY],
+        out_specs=VMEM,
+        scratch_shapes=[pltpu.SemaphoreType.DMA((pairs,))],
+        compiler_params=params(44),
+        cost_estimate=cost(0, 2 * 10**7),
+        name="load",
+    )(sky)
+    received, gain_turned, held = lax.optimization_barrier(
+        (exchange(send), gain_turned, held)
+    )
     gathered = [gain_turned]
     for k in range(1, group_count):
         gathered.append(
@@ -446,12 +476,7 @@
             )
         )
     base = received.reshape(n, lines * LANES)[:, (taps + 1) * cap : (taps + 2) * cap]
-    base = jnp.clip(base.astype(i32), 0, tiles - 2)
-    sky = (
-        sky_grid.reshape(pairs, terms, tiles, LANES)
-        .transpose(0, 2, 1, 3)
-        .reshape(pairs, terms * tiles, LANES)
-    )
+    base = jnp.clip(base.T.astype(i32), 0, tiles - 2) * terms
     slot_lines = n * cap * planes // LANES
     block_count = n * cap // LANES
     values, weights = pl.pallas_call(
@@ -460,17 +485,13 @@
             jax.ShapeDtypeStruct((slot_lines, LANES), f32),
             jax.ShapeDtypeStruct((n * cap, 2 * LANES), f32),
         ),
-        in_specs=[SMEM, VMEM, ANY],
+        in_specs=[SMEM, VMEM, VMEM],
         out_specs=(VMEM, VMEM),
-        scratch_shapes=[
-            pltpu.VMEM((terms * tiles, pairs, LANES), f32),
-            pltpu.VMEM((block_count, planes, LANES), f32),
-            pltpu.SemaphoreType.DMA((pairs,)),
-        ],
-        compiler_params=params(),
-        cost_estimate=cost(10**8, 7 * 10**7),
+        scratch_shapes=[pltpu.VMEM((block_count, planes, LANES), f32)],
+        compiler_params=params(24),
+        cost_estimate=cost(10**8, 5 * 10**7),
         name="degrid",
-    )(base, received, sky)
+    )(base, received, held)
     values, *gathered = lax.optimization_barrier((values, *gathered))
     back, gain_here = lax.optimization_barrier((exchange(values), gain_field))
     below = lax.ppermute(gain_here, "tm", [(i, i + 1) for i in range(time_count - 1)])
@@ -488,7 +509,6 @@
         out_specs=(VMEM,) * (group_count + 1),
         scratch_shapes=[
             pltpu.VMEM((facets, stations, wide), f32),
-            pltpu.VMEM((3 * stations, wide), bf16),
             pltpu.VMEM((facets, 3 * planes, wide), bf16),
             pltpu.VMEM((facets, rows, wide), f32),
             pltpu.VMEM((facets, rows, wide), f32),

time: 127 us -> 126 us (level)
  local copies, waits for them, and re-layouts: 4.74 us -> 16.3 us
  Pallas kernels: 71.2 us -> 61.5 us
  waiting for transfers between devices: 16.2 us -> 8.78 us
  starting transfers between devices: 18.8 us -> 23.4 us
    unnamed x20 -> x27, local copies, waits for them, and re-layouts: 2.06 us -> 15.1 us
    pallas_call x1, Pallas kernels: 21.6 us -> 12.9 us  [body(): pl.pallas_call(functools.partial(degrid_kernel, n, cap, taps), out_shape=...]
    pallas_call x1, Pallas kernels: 27.2 us -> 19.3 us  [body(): pl.pallas_call(functools.partial(rows_kernel, n, cap, group_count), out_s...]
    all_to_all x2, waiting for transfers between devices: 13.7 us -> 7.35 us  [exchange(): x = lax.all_to_all(x, both, split_axis=0, concat_axis=0, tiled=True)]
    pallas_call x0 -> x1, Pallas kernels: none -> 6.03 us  [body(): pl.pallas_call(load_kernel, out_shape=pltpu.VMEM((terms * tiles, pairs, L...]
    all_to_all x2, starting transfers between devices: 9.88 us -> 12.8 us  [exchange(): x = lax.all_to_all(x, both, split_axis=0, concat_axis=0, tiled=True)]
    ppermute x3, starting transfers between devices: 3.88 us -> 5.6 us  [body(): lax.ppermute(gain_turned, 'bl', [(i, (i + k) % group_count) for i in rang...]
    reshape x2 -> x0, local copies, waits for them, and re-layouts: 1.47 us -> none  [the longest x1 1.45 us: exchange(): x = x.reshape(n, -1, LANES)]
  transfers between devices with their start and end apart: 10 -> 10, of which waited for: 3 -> 2; matrix products, arithmetic and copies ran while one was open for 2% -> 2% of each run, Pallas kernels for 54% -> 47%
where the time goes in v3:
time: 126 us; the launch traced here: 125 us
  Pallas kernels  61.5 us (49%)
  starting transfers between devices  23.4 us (19%)
  local copies, waits for them, and re-layouts  16.3 us (13%)
  blocking collectives  14.1 us (11%)
  waiting for transfers between devices  8.78 us (7%)
    pallas_call x1, Pallas kernels, body(): pl.pallas_call(functools.partial(scatter_kernel, n, cap), out_shape=jax.S...  21.2 us
    pallas_call x1, Pallas kernels, body(): pl.pallas_call(functools.partial(rows_kernel, n, cap, group_count), out_s...  19.3 us
    unnamed x27, local copies, waits for them, and re-layouts  15.1 us
    all_to_all x1, blocking collectives, exchange(): x = lax.all_to_all(x, both, split_axis=0, concat_axis=0, tiled=True)  14.1 us
    pallas_call x1, Pallas kernels, body(): pl.pallas_call(functools.partial(degrid_kernel, n, cap, taps), out_shape=...  12.9 us
    all_to_all x2, starting transfers between devices, exchange(): x = lax.all_to_all(x, both, split_axis=0, concat_axis=0, tiled=True)  12.8 us
    all_to_all x2, waiting for transfers between devices, exchange(): x = lax.all_to_all(x, both, split_axis=0, concat_axis=0, tiled=True)  7.35 us
    pallas_call x1, Pallas kernels, body(): pl.pallas_call(load_kernel, out_shape=pltpu.VMEM((terms * tiles, pairs, L...  6.03 us
  transfers between devices with their start and end apart: 10, of which 2 were waited for; matrix products, arithmetic and copies ran while one was open for 2% of the time, Pallas kernels for 47%

profile of v3, /device:TPU:0, one launch (start us, length us, event | category | flops | bytes accessed | tf_op | source)
XLA Modules:
  0.0 125.3 jit_solution(590773807838157048)
XLA Ops:
  0.6 2.1 %slots.1 = (f32[128,128]{1,0:T(8,128)}, f32[8,512]{1,0:T(8,128)}, f32[512,8]{1,0:T(8,128)}) custom-call(s32[1]{0:T(128)} %bitcast.shift_ref, s32[1,512]{1,0:T(1,128)} %bitcast.46, s32[1,512]{1,0:T(1,128)} %bitcast.47, f32[8,512]{1,0:T(8,128)} %taps_ref.1, s32[2,512]{1,0:T(2,128)} %pairs_ref.1, f32[1,512]{1,0:T(1,128)} %bitcast.48, s32[1,512]{1,0:T(1,128)} %bitcast.49), custom_call_target="tpu_custom_call" | custom-call | flops 1000000000 | bytes 1000000 | tf_op jit(solution)/shard_map/slots/pallas_call | solution.py:426
  2.8 7.3 %all-to-all-start = ((f32[32,4,128]{2,1,0:T(4,128)}), f32[32,4,128]{2,1,0:T(4,128)S(1)}, u32[]{:S(2)}, u32[]{:S(2)}) async-start(f32[32,4,128]{2,1,0:T(4,128)} %bitcast.45), calls=%async_computation | async-start | bytes 131072 | tf_op jit(solution)/shard_map/all_to_all | solution.py:450
  10.1 1.1 copy.34
  11.2 0.0 copy-start.6
  11.2 0.0 copy-start.5
  11.2 0.0 copy-start.4
  11.2 6.0 %load.1.held = f32[2048,16,128]{2,1,0:T(8,128)S(1)} custom-call(f32[16,2048,128]{2,1,0:T(8,128)} %bitcast.36), custom_call_target="tpu_custom_call" | custom-call | bytes 20000000 | tf_op jit(solution)/shard_map/load/pallas_call | solution.py:458
  17.2 0.0 copy-start
  17.3 6.2 %copy-done = f32[2048,16,128]{2,1,0:T(8,128)} copy-done((f32[2048,16,128]{2,1,0:T(8,128)}, f32[2048,16,128]{2,1,0:T(8,128)S(1)}, u32[]{:S(2)}) %copy-start) | copy-done | bytes 16777240
  23.4 0.0 all-to-all-done
  23.4 1.8 %collective-permute-start = (f32[8,2,16,240]{3,2,1,0:T(8,128)S(1)}, f32[8,2,16,240]{3,2,1,0:T(8,128)S(1)}, u32[]{:S(2)}, u32[]{:S(2)}) collective-permute-start(f32[8,2,16,240]{3,2,1,0:T(8,128)S(1)} %bitcast.39), channel_id=1, source_target_pairs={{0,1},{1,2},{2,3},{3,0},{4,5},{5,6},{6,7},{7,4},{8,9},{9,10},{10,1... | collective-permute-start | bytes 737288 | tf_op jit(solution)/shard_map/ppermute | solution.py:474
  25.2 2.4 %collective-permute-start.1 = (f32[8,2,16,240]{3,2,1,0:T(8,128)S(1)}, f32[8,2,16,240]{3,2,1,0:T(8,128)S(1)}, u32[]{:S(2)}, u32[]{:S(2)}) collective-permute-start(f32[8,2,16,240]{3,2,1,0:T(8,128)S(1)} %bitcast.40), channel_id=1, source_target_pairs={{0,2},{1,3},{2,0},{3,1},{4,6},{5,7},{6,4},{7,5},{8,10},{9,11},{10,... | collective-permute-start | bytes 737288 | tf_op jit(solution)/shard_map/ppermute | solution.py:474
  27.6 0.0 copy-done.6
  27.6 1.4 %collective-permute-start.2 = (f32[8,2,16,240]{3,2,1,0:T(8,128)S(1)}, f32[8,2,16,240]{3,2,1,0:T(8,128)S(1)}, u32[]{:S(2)}, u32[]{:S(2)}) collective-permute-start(f32[8,2,16,240]{3,2,1,0:T(8,128)S(1)} %bitcast.41), channel_id=1, source_target_pairs={{0,3},{1,0},{2,1},{3,2},{4,7},{5,4},{6,5},{7,6},{8,11},{9,8},{10,9... | collective-permute-start | bytes 737288 | tf_op jit(solution)/shard_map/ppermute | solution.py:474
  29.0 0.1 slice.4
  29.1 0.1 copy.31
  29.2 0.0 copy-start.1
  29.2 5.8 %copy-done.1 = f32[2048,16,128]{2,1,0:T(8,128)S(1)} copy-done((f32[2048,16,128]{2,1,0:T(8,128)S(1)}, f32[2048,16,128]{2,1,0:T(8,128)}, u32[]{:S(2)}) %copy-start.1) | copy-done | bytes 16777240
  35.0 12.9 %degrid.1 = (f32[256,128]{1,0:T(8,128)}, f32[1024,256]{1,0:T(8,128)S(1)}) custom-call(s32[32,32]{1,0:T(8,128)S(1)} %multiply_bitcast_fusion.base_ref, f32[128,128]{1,0:T(8,128)S(1)} %bitcast.34, f32[2048,16,128]{2,1,0:T(8,128)S(1)} %copy-done.1), custom_call_target="tpu_custom_call" | custom-call | flops 100000000 | bytes 50000000 | tf_op jit(solution)/shard_map/degrid/pallas_call | solution.py:482
  47.8 1.0 copy-done.2
  48.8 0.0 collective-permute-done.rest_1_
  48.9 0.0 collective-permute-done.1.rest_2_
  48.9 0.0 copy-start.10
  48.9 0.0 collective-permute-done.2.rest_3_
  48.9 0.0 copy-start.11
  48.9 5.5 %all-to-all-start.1 = ((f32[32,8,128]{2,1,0:T(8,128)}), f32[32,8,128]{2,1,0:T(8,128)S(1)}, u32[]{:S(2)}, u32[]{:S(2)}) async-start(f32[32,8,128]{2,1,0:T(8,128)} %bitcast.14), calls=%async_computation.1 | async-start | bytes 262144 | tf_op jit(solution)/shard_map/all_to_all | solution.py:450
  54.4 0.0 copy-done.5
  54.5 1.0 copy.30.vis_ref
  55.5 7.3 %all-to-all-done.1 = f32[32,8,128]{2,1,0:T(8,128)S(1)} async-done(((f32[32,8,128]{2,1,0:T(8,128)}), f32[32,8,128]{2,1,0:T(8,128)S(1)}, u32[]{:S(2)}, u32[]{:S(2)}) %all-to-all-start.1) | async-done | bytes 131104 | tf_op jit(solution)/shard_map/all_to_all | solution.py:450
  62.8 0.0 copy-done.4
  62.8 0.2 copy.24
  63.0 1.3 %collective-permute-start.3 = (f32[1,16,8,2,240]{4,1,3,2,0:T(8,128)S(1)}, f32[1,16,8,2,240]{4,1,3,2,0:T(8,128)S(1)}, u32[]{:S(2)}, u32[]{:S(2)}) collective-permute-start(f32[1,16,8,2,240]{4,1,3,2,0:T(8,128)S(1)} %copy.24), channel_id=1, source_target_pairs={{0,4},{4,8},{8,12},{12,16},{16,20},{20,24},{24,28},{1,5},{5,9},{9,... | collective-permute-start | bytes 737288 | tf_op jit(solution)/shard_map/ppermute | solution.py:497
  64.3 1.3 %collective-permute-start.4 = (f32[1,16,8,2,240]{4,1,3,2,0:T(8,128)S(1)}, f32[1,16,8,2,240]{4,1,3,2,0:T(8,128)S(1)}, u32[]{:S(2)}, u32[]{:S(2)}) collective-permute-start(f32[1,16,8,2,240]{4,1,3,2,0:T(8,128)S(1)} %copy.24), channel_id=1, source_target_pairs={{4,0},{8,4},{12,8},{16,12},{20,16},{24,20},{28,24},{5,1},{9,5},{13... | collective-permute-start | bytes 737288 | tf_op jit(solution)/shard_map/ppermute | solution.py:498
  65.6 0.0 copy-done.9
  65.6 19.3 %rowgrads.1 = (f32[8,2,16,240]{3,2,1,0:T(8,128)}, f32[8,2,16,240]{3,2,1,0:T(8,128)}, f32[8,2,16,240]{3,2,1,0:T(8,128)}, f32[8,2,16,240]{3,2,1,0:T(8,128)}, f32[256,128]{1,0:T(8,128)}) custom-call(f32[8,512]{1,0:T(8,128)} %get-tuple-element.37.rows_ref, f32[512,8]{1,0:T(8,128)} %get-tuple-element.38.cols_ref, bf16[512,512]{1,0:T(8,128)(2,1)} %copy.30.vis_ref, ...), custom_call_target="tpu_custom_call" | custom-call | flops 20000000000 | bytes 10000000 | tf_op jit(solution)/shard_map/rowgrads/pallas_call | solution.py:504
  84.9 0.0 collective-permute-done.3
  85.0 0.0 collective-permute-done.4
  85.0 14.1 %all_to_all.15 = f32[32,8,128]{2,1,0:T(8,128)} all-to-all(f32[32,8,128]{2,1,0:T(8,128)} %bitcast.44), channel_id=1, replica_groups=mesh['tm'=8,'bl'=4] {'tm','bl'}, dimensions={0} | all-to-all | bytes 262144 | tf_op jit(solution)/shard_map/all_to_all | solution.py:450
  99.1 1.2 collective-permute-start.5
  100.3 0.0 collective-permute-start.6
  100.3 1.2 collective-permute-start.7
  101.5 21.2 %scatter.1 = f32[16,2048,128]{2,1,0:T(8,128)} custom-call(s32[32,32]{1,0:T(8,128)} %copy-done.3, f32[256,128]{1,0:T(8,128)} %bitcast.38, f32[1024,256]{1,0:T(8,128)} %copy-done.2), custom_call_target="tpu_custom_call" | custom-call | flops 100000000 | bytes 100000000 | tf_op jit(solution)/shard_map/scatter/pallas_call | solution.py:534
  122.7 0.0 collective-permute-done.5
  122.7 1.4 %collective-permute-done.6 = f32[8,2,16,240]{3,2,1,0:T(8,128)S(1)} collective-permute-done((f32[8,2,16,240]{3,2,1,0:T(8,128)}, f32[8,2,16,240]{3,2,1,0:T(8,128)S(1)}, u32[]{:S(2)}, u32[]{:S(2)}) %collective-permute-start.6) | collective-permute-done | bytes 245792 | tf_op jit(solution)/shard_map/ppermute | solution.py:531
  124.1 0.0 collective-permute-done.7
  124.1 0.0 copy-done.7
  124.1 0.2 bitcast_add_fusion
  124.4 0.9 copy.29
  (12 shorter events, 0.1 us)
Async XLA Ops:
  2.8 20.7 %all-to-all-start = ((f32[32,4,128]{2,1,0:T(4,128)}), f32[32,4,128]{2,1,0:T(4,128)S(1)}, u32[]{:S(2)}, u32[]{:S(2)}) async-start(f32[32,4,128]{2,1,0:T(4,128)} %bitcast.45), calls=%async_computation | async-start | bytes 131072 | tf_op jit(solution)/shard_map/all_to_all | solution.py:450
  11.2 16.4 %copy-start.6 = (f32[1,16,8,2,240]{4,1,3,2,0:T(8,128)}, f32[1,16,8,2,240]{4,1,3,2,0:T(8,128)S(1)}, u32[]{:S(2)}) copy-start(f32[1,16,8,2,240]{4,1,3,2,0:T(8,128)S(1)} %copy.34) | copy-start | bytes 737284
  11.2 43.2 %copy-start.5 = (bf16[512,2,240]{0,2,1:T(8,128)(2,1)S(1)}, bf16[512,2,240]{0,2,1:T(8,128)(2,1)}, u32[]{:S(2)}) copy-start(bf16[512,2,240]{0,2,1:T(8,128)(2,1)} %param.9) | copy-start | bytes 1474564
  11.2 51.6 %copy-start.4 = (f32[1,16,8,2,240]{4,3,2,1,0:T(2,128)S(1)}, f32[1,16,8,2,240]{4,3,2,1,0:T(2,128)}, u32[]{:S(2)}) copy-start(f32[1,16,8,2,240]{4,3,2,1,0:T(2,128)} %param.16) | copy-start | bytes 737284
  17.2 6.2 %copy-start = (f32[2048,16,128]{2,1,0:T(8,128)}, f32[2048,16,128]{2,1,0:T(8,128)S(1)}, u32[]{:S(2)}) copy-start(f32[2048,16,128]{2,1,0:T(8,128)S(1)} %load.1.held) | copy-start | bytes 50331652
  23.4 25.4 %collective-permute-start = (f32[8,2,16,240]{3,2,1,0:T(8,128)S(1)}, f32[8,2,16,240]{3,2,1,0:T(8,128)S(1)}, u32[]{:S(2)}, u32[]{:S(2)}) collective-permute-start(f32[8,2,16,240]{3,2,1,0:T(8,128)S(1)} %bitcast.39), channel_id=1, source_target_pairs={{0,1},{1,2},{2,3},{3,0},{4,5},{5,6},{6,7},{7,4},{8,9},{9,10},{10,1... | collective-permute-start | bytes 737288 | tf_op jit(solution)/shard_map/ppermute | solution.py:474
  25.2 23.7 %collective-permute-start.1 = (f32[8,2,16,240]{3,2,1,0:T(8,128)S(1)}, f32[8,2,16,240]{3,2,1,0:T(8,128)S(1)}, u32[]{:S(2)}, u32[]{:S(2)}) collective-permute-start(f32[8,2,16,240]{3,2,1,0:T(8,128)S(1)} %bitcast.40), channel_id=1, source_target_pairs={{0,2},{1,3},{2,0},{3,1},{4,6},{5,7},{6,4},{7,5},{8,10},{9,11},{10,... | collective-permute-start | bytes 737288 | tf_op jit(solution)/shard_map/ppermute | solution.py:474
  27.6 21.3 %collective-permute-start.2 = (f32[8,2,16,240]{3,2,1,0:T(8,128)S(1)}, f32[8,2,16,240]{3,2,1,0:T(8,128)S(1)}, u32[]{:S(2)}, u32[]{:S(2)}) collective-permute-start(f32[8,2,16,240]{3,2,1,0:T(8,128)S(1)} %bitcast.41), channel_id=1, source_target_pairs={{0,3},{1,0},{2,1},{3,2},{4,7},{5,4},{6,5},{7,6},{8,11},{9,8},{10,9... | collective-permute-start | bytes 737288 | tf_op jit(solution)/shard_map/ppermute | solution.py:474
  29.2 5.8 %copy-start.1 = (f32[2048,16,128]{2,1,0:T(8,128)S(1)}, f32[2048,16,128]{2,1,0:T(8,128)}, u32[]{:S(2)}) copy-start(f32[2048,16,128]{2,1,0:T(8,128)} %copy-done) | copy-start | bytes 50331652
  35.0 50.0 %copy-start.3 = (s32[32,32]{1,0:T(8,128)}, s32[32,32]{1,0:T(8,128)S(1)}, u32[]{:S(2)}) copy-start(s32[32,32]{1,0:T(8,128)S(1)} %multiply_bitcast_fusion.base_ref) | copy-start | bytes 12292
  47.8 1.0 copy-start.2
  48.9 16.7 %copy-start.9 = (f32[8,2,16,240]{3,2,1,0:T(8,128)}, f32[8,2,16,240]{3,2,1,0:T(8,128)S(1)}, u32[]{:S(2)}) copy-start(f32[8,2,16,240]{3,2,1,0:T(8,128)S(1)} %collective-permute-done.rest_1_) | copy-start | bytes 737284
  48.9 16.7 %copy-start.10 = (f32[8,2,16,240]{3,2,1,0:T(8,128)}, f32[8,2,16,240]{3,2,1,0:T(8,128)S(1)}, u32[]{:S(2)}) copy-start(f32[8,2,16,240]{3,2,1,0:T(8,128)S(1)} %collective-permute-done.1.rest_2_) | copy-start | bytes 737284
  48.9 16.7 %copy-start.11 = (f32[8,2,16,240]{3,2,1,0:T(8,128)}, f32[8,2,16,240]{3,2,1,0:T(8,128)S(1)}, u32[]{:S(2)}) copy-start(f32[8,2,16,240]{3,2,1,0:T(8,128)S(1)} %collective-permute-done.2.rest_3_) | copy-start | bytes 737284
  48.9 13.9 %all-to-all-start.1 = ((f32[32,8,128]{2,1,0:T(8,128)}), f32[32,8,128]{2,1,0:T(8,128)S(1)}, u32[]{:S(2)}, u32[]{:S(2)}) async-start(f32[32,8,128]{2,1,0:T(8,128)} %bitcast.14), calls=%async_computation.1 | async-start | bytes 262144 | tf_op jit(solution)/shard_map/all_to_all | solution.py:450
  62.8 2.8 %copy-start.8 = (f32[32,8,128]{2,1,0:T(8,128)}, f32[32,8,128]{2,1,0:T(8,128)S(1)}, u32[]{:S(2)}) copy-start(f32[32,8,128]{2,1,0:T(8,128)S(1)} %all-to-all-done.1) | copy-start | bytes 393220
  63.0 22.0 %collective-permute-start.3 = (f32[1,16,8,2,240]{4,1,3,2,0:T(8,128)S(1)}, f32[1,16,8,2,240]{4,1,3,2,0:T(8,128)S(1)}, u32[]{:S(2)}, u32[]{:S(2)}) collective-permute-start(f32[1,16,8,2,240]{4,1,3,2,0:T(8,128)S(1)} %copy.24), channel_id=1, source_target_pairs={{0,4},{4,8},{8,12},{12,16},{16,20},{20,24},{24,28},{1,5},{5,9},{9,... | collective-permute-start | bytes 737288 | tf_op jit(solution)/shard_map/ppermute | solution.py:497
  64.3 20.7 %collective-permute-start.4 = (f32[1,16,8,2,240]{4,1,3,2,0:T(8,128)S(1)}, f32[1,16,8,2,240]{4,1,3,2,0:T(8,128)S(1)}, u32[]{:S(2)}, u32[]{:S(2)}) collective-permute-start(f32[1,16,8,2,240]{4,1,3,2,0:T(8,128)S(1)} %copy.24), channel_id=1, source_target_pairs={{4,0},{8,4},{12,8},{16,12},{20,16},{24,20},{28,24},{5,1},{9,5},{13... | collective-permute-start | bytes 737288 | tf_op jit(solution)/shard_map/ppermute | solution.py:498
  84.9 39.2 %copy-start.7 = (f32[8,2,16,240]{3,2,1,0:T(8,128)S(1)}, f32[8,2,16,240]{3,2,1,0:T(8,128)}, u32[]{:S(2)}) copy-start(f32[8,2,16,240]{3,2,1,0:T(8,128)} %get-tuple-element.61) | copy-start | bytes 737284
  99.1 23.6 %collective-permute-start.5 = (f32[8,2,16,240]{3,2,1,0:T(8,128)}, f32[8,2,16,240]{3,2,1,0:T(8,128)S(1)}, u32[]{:S(2)}, u32[]{:S(2)}) collective-permute-start(f32[8,2,16,240]{3,2,1,0:T(8,128)} %get-tuple-element.58), channel_id=1, source_target_pairs={{0,3},{1,0},{2,1},{3,2},{4,7},{5,4},{6,5},{7,6},{8,11},{9,8},{10,9... | collective-permute-start | bytes 737288 | tf_op jit(solution)/shard_map/ppermute | solution.py:531
  100.3 23.8 %collective-permute-start.6 = (f32[8,2,16,240]{3,2,1,0:T(8,128)}, f32[8,2,16,240]{3,2,1,0:T(8,128)S(1)}, u32[]{:S(2)}, u32[]{:S(2)}) collective-permute-start(f32[8,2,16,240]{3,2,1,0:T(8,128)} %get-tuple-element.59), channel_id=1, source_target_pairs={{0,2},{1,3},{2,0},{3,1},{4,6},{5,7},{6,4},{7,5},{8,10},{9,11},{10,... | collective-permute-start | bytes 737288 | tf_op jit(solution)/shard_map/ppermute | solution.py:531
  100.3 23.8 %collective-permute-start.7 = (f32[8,2,16,240]{3,2,1,0:T(8,128)}, f32[8,2,16,240]{3,2,1,0:T(8,128)S(1)}, u32[]{:S(2)}, u32[]{:S(2)}) collective-permute-start(f32[8,2,16,240]{3,2,1,0:T(8,128)} %get-tuple-element.60), channel_id=1, source_target_pairs={{0,1},{1,2},{2,3},{3,0},{4,5},{5,6},{6,7},{7,4},{8,9},{9,10},{10,1... | collective-permute-start | bytes 737288 | tf_op jit(solution)/shard_map/ppermute | solution.py:531

commit v4 on v3

--- a/solution.py
+++ b/solution.py
@@ -115,7 +115,8 @@
     cols_ref[...] = table.T
 
 
-def load_kernel(sky_ref, held_ref, sem):
+def load_kernel(sky_ref, held_ref, token_ref, sem):
+    token_ref[...] = jnp.zeros(token_ref.shape, f32)
     copies = []
     for i in range(sky_ref.shape[0]):
         copy = pltpu.make_async_copy(sky_ref.at[i], held_ref.at[:, i], sem.at[i])
@@ -127,22 +128,36 @@
 
 def degrid_kernel(
     n, cap, taps,
-    base_ref, recv_ref, held, out_ref, w_ref, blocks,
+    base_ref, recv_ref, held, out_ref, w_ref, w_s, turn_s, blocks, sem,
 ):
     pairs = held.shape[1]
     planes = 2 * pairs
-    recv = read_wide(recv_ref, n)
-    lane = iota((n, 2 * LANES), 1).astype(f32)
-    for j in range(cap):
-        place = lane - recv[:, taps * cap + j : taps * cap + j + 1]
-        w = jnp.zeros((n, 2 * LANES), f32)
-        for k in range(taps):
-            w = jnp.where(place == float(k), recv[:, k * cap + j : k * cap + j + 1], w)
-        w_ref[j * n : (j + 1) * n, :] = w
     per_block = LANES // n
     block_count = cap // per_block
+    turn_s[...] = read_wide(recv_ref, n).T
+    fields = []
+    for k in range(taps + 1):
+        fields.append(
+            jnp.concatenate(
+                [
+                    turn_s[pl.ds(k * cap + q, block_count, stride=per_block), :]
+                    for q in range(per_block)
+                ],
+                axis=1,
+            )
+        )
+    line = iota((2 * LANES, LANES), 0).astype(f32)
+    for jb in range(block_count):
+        place = line - fields[taps][jb : jb + 1, :]
+        w = jnp.zeros((2 * LANES, LANES), f32)
+        for k in range(taps):
+            w = jnp.where(place == float(k), fields[k][jb : jb + 1, :], w)
+        w_s[jb * LANES : (jb + 1) * LANES, :] = w.T
+    save = pltpu.make_async_copy(w_s, w_ref, sem.at[0])
+    save.start()
     unroll = min(n, 16)
     lane3 = iota((2, pairs, LANES), 2)
+    ones = jnp.ones((2 * LANES, LANES), bf16)
 
     def block(jb, carry):
         acc = jnp.zeros((2, pairs, LANES), f32)
@@ -152,12 +167,18 @@
             def step(g, acc):
                 first = g * unroll
                 rel = lane3 - (q * n + first)
+                prods = []
                 for u in range(unroll):
                     start = base_ref[j, first + u]
-                    w = w_ref[pl.ds(j * n + first + u, 1), :]
+                    w = w_s[pl.ds(j * n + first + u, 1), :]
                     window = held[pl.ds(start, 4)]
                     prod = window[0:2] * w[:, :LANES] + window[2:4] * w[:, LANES:]
-                    acc = jnp.where(rel == u, jnp.sum(prod, axis=2, keepdims=True), acc)
+                    prods.append(prod.reshape(planes, LANES))
+                halves = split(jnp.concatenate(prods, axis=0), 2)
+                sums = mm(jnp.concatenate(halves, axis=1), ones)
+                for u in range(unroll):
+                    one = sums[u * planes : (u + 1) * planes, :].reshape(2, pairs, LANES)
+                    acc = jnp.where(rel == u, one, acc)
                 return acc
 
             acc = lax.fori_loop(0, n // unroll, step, acc)
@@ -175,6 +196,7 @@
     for i in range(per):
         line = jnp.concatenate(pieces[i * per_line : (i + 1) * per_line], axis=1)
         out_ref[pl.ds(i, n, stride=per), :] = line
+    save.wait()
 
 
 def rows_kernel(
@@ -333,56 +355,57 @@
         send_ref[pl.ds(i, n, stride=line_count), :] = total[:, :LANES] + total[:, LANES:]
 
 
-def scatter_kernel(n, cap, base_ref, grad_ref, w_ref, out_ref, held, blocks, sem):
+def clear_kernel(after_ref, held):
+    fill = 32
+
+    def clear(i, carry):
+        held[pl.ds(i * fill, fill)] = jnp.zeros((fill,) + held.shape[1:], f32)
+        return carry
+
+    lax.fori_loop(0, held.shape[0] // fill, clear, 0)
+
+
+def scatter_kernel(n, cap, base_ref, grad_ref, w_ref, zero_ref, out_ref, held, sem):
     pairs = out_ref.shape[0]
     planes = 2 * pairs
-    lines = held.shape[0]
-    fill = 32
-
-    def clear(i, carry):
-        held[pl.ds(i * fill, fill)] = jnp.zeros((fill, pairs, LANES), f32)
-        return carry
-
-    lax.fori_loop(0, lines // fill, clear, 0)
     per_line = LANES // planes
-    per = cap // per_line
-    pieces = []
-    for i in range(per):
-        line = grad_ref[pl.ds(i, n, stride=per), :]
-        for q in range(per_line):
-            pieces.append(line[:, q * planes : (q + 1) * planes])
-    per_block = LANES // n
-    block_count = cap // per_block
-    for jb in range(block_count):
-        mine = pieces[jb * per_block : (jb + 1) * per_block]
-        joined = mine[0] if per_block == 1 else jnp.concatenate(mine, axis=0)
-        blocks[jb] = joined.T
-    unroll = min(n, 16)
-    lane3 = iota((2, pairs, LANES), 2)
-
-    def block(jb, carry):
-        values = blocks[jb].reshape(2, pairs, LANES)
-        for q in range(per_block):
-            j = jb * per_block + q
-
-            def step(g, inner):
-                first = g * unroll
-                rel = lane3 - (q * n + first)
-                for u in range(unroll):
-                    at = pl.ds(base_ref[j, first + u], 4)
-                    w = w_ref[pl.ds(j * n + first + u, 1), :]
-                    value = jnp.sum(
-                        jnp.where(rel == u, values, 0.0), axis=2, keepdims=True
+    line_count = cap // per_line
+    tall = 16
+    eye = as_bf16(iota((LANES, LANES), 0) == iota((LANES, LANES), 1))
+    ones = jnp.ones((2 * LANES, LANES), bf16)
+    unroll = 4
+
+    def line(i, carry):
+        def step(g, inner):
+            for u in range(unroll):
+                src = g * unroll + u
+                row = grad_ref[pl.ds(src * line_count + i, 1), :]
+                spread = []
+                for piece in split(jnp.broadcast_to(row, (tall, LANES)), 2):
+                    spread.append(
+                        jnp.concatenate(
+                            [
+                                eye[m * tall : (m + 1) * tall, :] * piece
+                                for m in range(LANES // tall)
+                            ],
+                            axis=0,
+                        )
                     )
+                values = mm(jnp.concatenate(spread, axis=1), ones)
+                for q in range(per_line):
+                    j = i * per_line + q
+                    at = pl.ds(base_ref[j, src], 4)
+                    w = w_ref[pl.ds(j * n + src, 1), :]
+                    value = values[q * planes : (q + 1) * planes, :]
+                    value = value.reshape(2, pairs, LANES)
                     held[at] = held[at] + jnp.concatenate(
                         [value * w[:, :LANES], value * w[:, LANES:]], axis=0
                     )
-                return inner
-
-            carry = lax.fori_loop(0, n // unroll, step, carry)
-        return carry
-
-    lax.fori_loop(0, block_count, block, 0)
+            return inner
+
+        return lax.fori_loop(0, n // unroll, step, carry)
+
+    lax.fori_loop(0, line_count, line, 0)
     copies = []
     for i in range(pairs):
         copy = pltpu.make_async_copy(held.at[:, i], out_ref.at[i], sem.at[i])
@@ -455,18 +478,22 @@
         .transpose(0, 2, 1, 3)
         .reshape(pairs, terms * tiles, LANES)
     )
-    held = pl.pallas_call(
+    grid_shape = (terms * tiles, pairs, LANES)
+    held, token = pl.pallas_call(
         load_kernel,
-        out_shape=pltpu.VMEM((terms * tiles, pairs, LANES), f32),
+        out_shape=(
+            pltpu.VMEM(grid_shape, f32),
+            jax.ShapeDtypeStruct((8, LANES), f32),
+        ),
         in_specs=[ANY],
-        out_specs=VMEM,
+        out_specs=(VMEM, VMEM),
         scratch_shapes=[pltpu.SemaphoreType.DMA((pairs,))],
-        compiler_params=params(44),
+        compiler_params=params(40),
         cost_estimate=cost(0, 2 * 10**7),
         name="load",
     )(sky)
-    received, gain_turned, held = lax.optimization_barrier(
-        (exchange(send), gain_turned, held)
+    received, gain_turned, token = lax.optimization_barrier(
+        (exchange(send), gain_turned, token)
     )
     gathered = [gain_turned]
     for k in range(1, group_count):
@@ -486,14 +513,20 @@
             jax.ShapeDtypeStruct((n * cap, 2 * LANES), f32),
         ),
         in_specs=[SMEM, VMEM, VMEM],
-        out_specs=(VMEM, VMEM),
-        scratch_shapes=[pltpu.VMEM((block_count, planes, LANES), f32)],
-        compiler_params=params(24),
+        out_specs=(VMEM, pl.BlockSpec(memory_space=pltpu.HBM)),
+        scratch_shapes=[
+            pltpu.VMEM((n * cap, 2 * LANES), f32),
+            pltpu.VMEM((lines * LANES, n), f32),
+            pltpu.VMEM((block_count, planes, LANES), f32),
+            pltpu.SemaphoreType.DMA((1,)),
+        ],
+        compiler_params=params(30),
         cost_estimate=cost(10**8, 5 * 10**7),
         name="degrid",
     )(base, received, held)
     values, *gathered = lax.optimization_barrier((values, *gathered))
-    back, gain_here = lax.optimization_barrier((exchange(values), gain_field))
+    values, gain_here = lax.optimization_barrier((values, gain_field))
+    back = exchange(values)
     below = lax.ppermute(gain_here, "tm", [(i, i + 1) for i in range(time_count - 1)])
     above = lax.ppermute(gain_here, "tm", [(i + 1, i) for i in range(time_count - 1)])
 
@@ -526,25 +559,34 @@
 
     *parts, send_grad = outs
     send_grad, below, above = lax.optimization_barrier((send_grad, below, above))
-    got, *parts = lax.optimization_barrier((exchange(send_grad), *parts))
+    zero = pl.pallas_call(
+        clear_kernel,
+        out_shape=pltpu.VMEM(grid_shape, f32),
+        in_specs=[ANY],
+        out_specs=VMEM,
+        compiler_params=params(24),
+        cost_estimate=cost(0, 2 * 10**7),
+        name="clear",
+    )(send_grad)
+    got = exchange(send_grad)
     for k in range(1, group_count):
         parts[k] = lax.ppermute(
             parts[k], "bl", [(i, (i - k) % group_count) for i in range(group_count)]
         )
-    grid = pl.pallas_call(
+    grid, _ = pl.pallas_call(
         functools.partial(scatter_kernel, n, cap),
-        out_shape=jax.ShapeDtypeStruct((pairs, terms * tiles, LANES), f32),
-        in_specs=[SMEM, VMEM, VMEM],
-        out_specs=ANY,
-        scratch_shapes=[
-            pltpu.VMEM((terms * tiles, pairs, LANES), f32),
-            pltpu.VMEM((block_count, planes, LANES), f32),
-            pltpu.SemaphoreType.DMA((pairs,)),
-        ],
-        compiler_params=params(),
+        out_shape=(
+            jax.ShapeDtypeStruct((pairs, terms * tiles, LANES), f32),
+            pltpu.VMEM(grid_shape, f32),
+        ),
+        in_specs=[SMEM, VMEM, VMEM, VMEM],
+        out_specs=(ANY, VMEM),
+        scratch_shapes=[pltpu.SemaphoreType.DMA((pairs,))],
+        input_output_aliases={3: 1},
+        compiler_params=params(24),
         cost_estimate=cost(10**8, 10**8),
         name="scatter",
-    )(base, got, weights)
+    )(base, got, weights, zero)
     grid, *parts = lax.optimization_barrier((grid, *parts))
     total = parts[0]
     for part in parts[1:]:

time: 126 us -> 138 us (1.095)
  blocking collectives: 14.1 us -> 0 us
  local copies, waits for them, and re-layouts: 16.3 us -> 28.8 us
  Pallas kernels: 61.5 us -> 71.6 us
  starting transfers between devices: 23.4 us -> 26.1 us
  waiting for transfers between devices: 8.78 us -> 10.2 us
    all_to_all x1 -> x0, blocking collectives: 14.1 us -> none  [exchange(): x = lax.all_to_all(x, both, split_axis=0, concat_axis=0, tiled=True)]
    unnamed x27 -> x29, local copies, waits for them, and re-layouts: 15.1 us -> 27.5 us
    pallas_call x1, Pallas kernels: 12.9 us -> 18.3 us  [body(): pl.pallas_call(functools.partial(degrid_kernel, n, cap, taps), out_shape=...]
    pallas_call x2 -> x3, Pallas kernels: 27.2 us -> 31.9 us  [the longest x1 24.1 us: body(): pl.pallas_call(functools.partial(scatter_kernel, n, cap), out_shape=(jax....]
    all_to_all x2 -> x3, waiting for transfers between devices: 7.35 us -> 10.2 us  [exchange(): x = lax.all_to_all(x, both, split_axis=0, concat_axis=0, tiled=True)]
    ppermute x3, starting transfers between devices: 2.4 us -> 4.75 us  [body(): lax.ppermute(parts[k], 'bl', [(i, (i - k) % group_count) for i in range(g...]
    ppermute x3, starting transfers between devices: 5.6 us -> 3.83 us  [body(): lax.ppermute(gain_turned, 'bl', [(i, (i + k) % group_count) for i in rang...]
    ppermute x3, waiting for transfers between devices: 1.42 us -> 0.01 us  [body(): lax.ppermute(parts[k], 'bl', [(i, (i - k) % group_count) for i in range(g...]
  transfers between devices with their start and end apart: 10 -> 11, of which waited for: 2 -> 2; matrix products, arithmetic and copies ran while one was open for 2% -> 2% of each run, Pallas kernels for 47% -> 50%
where the time goes in v4:
time: 138 us
  Pallas kernels  71.6 us (52%)
  local copies, waits for them, and re-layouts  28.8 us (21%)
  starting transfers between devices  26.1 us (19%)
  waiting for transfers between devices  10.2 us (7%)
    unnamed x29, local copies, waits for them, and re-layouts  27.5 us
    pallas_call x1, Pallas kernels, body(): pl.pallas_call(functools.partial(scatter_kernel, n, cap), out_shape=(jax....  24.1 us
    pallas_call x1, Pallas kernels, body(): pl.pallas_call(functools.partial(rows_kernel, n, cap, group_count), out_s...  19.3 us
    pallas_call x1, Pallas kernels, body(): pl.pallas_call(functools.partial(degrid_kernel, n, cap, taps), out_shape=...  18.3 us
    all_to_all x3, starting transfers between devices, exchange(): x = lax.all_to_all(x, both, split_axis=0, concat_axis=0, tiled=True)  14.1 us
    all_to_all x3, waiting for transfers between devices, exchange(): x = lax.all_to_all(x, both, split_axis=0, concat_axis=0, tiled=True)  10.2 us
    pallas_call x1, Pallas kernels, body(): pl.pallas_call(load_kernel, out_shape=(pltpu.VMEM(grid_shape, f32), jax.S...  6.58 us
    ppermute x3, starting transfers between devices, body(): lax.ppermute(parts[k], 'bl', [(i, (i - k) % group_count) for i in range(g...  4.75 us
  transfers between devices with their start and end apart: 11, of which 2 were waited for; matrix products, arithmetic and copies ran while one was open for 2% of the time, Pallas kernels for 50%

profile of v4, /device:TPU:0, one launch (start us, length us, event | category | flops | bytes accessed | tf_op | source)
XLA Modules:
  0.0 137.8 jit_solution(8041604237462321399)
XLA Ops:
  0.6 2.1 %slots.1 = (f32[128,128]{1,0:T(8,128)}, f32[8,512]{1,0:T(8,128)}, f32[512,8]{1,0:T(8,128)}) custom-call(s32[1]{0:T(128)} %bitcast.shift_ref, s32[1,512]{1,0:T(1,128)} %bitcast.46, s32[1,512]{1,0:T(1,128)} %bitcast.47, f32[8,512]{1,0:T(8,128)} %taps_ref.1, s32[2,512]{1,0:T(2,128)} %pairs_ref.1, f32[1,512]{1,0:T(1,128)} %bitcast.48, s32[1,512]{1,0:T(1,128)} %bitcast.49), custom_call_target="tpu_custom_call" | custom-call | flops 1000000000 | bytes 1000000 | tf_op jit(solution)/shard_map/slots/pallas_call | solution.py:449
  2.8 7.3 %all-to-all-start = ((f32[32,4,128]{2,1,0:T(4,128)}), f32[32,4,128]{2,1,0:T(4,128)S(1)}, u32[]{:S(2)}, u32[]{:S(2)}) async-start(f32[32,4,128]{2,1,0:T(4,128)} %bitcast.44), calls=%async_computation | async-start | bytes 131072 | tf_op jit(solution)/shard_map/all_to_all | solution.py:473
  10.1 1.1 copy.35
  11.2 6.4 %all-to-all-done = f32[32,4,128]{2,1,0:T(4,128)S(1)} async-done(((f32[32,4,128]{2,1,0:T(4,128)}), f32[32,4,128]{2,1,0:T(4,128)S(1)}, u32[]{:S(2)}, u32[]{:S(2)}) %all-to-all-start) | async-done | bytes 65568 | tf_op jit(solution)/shard_map/all_to_all | solution.py:473
  17.6 0.2 collective-permute-start
  17.8 1.2 collective-permute-start.1
  18.9 2.4 %collective-permute-start.2 = (f32[8,2,16,240]{3,2,1,0:T(8,128)S(1)}, f32[8,2,16,240]{3,2,1,0:T(8,128)S(1)}, u32[]{:S(2)}, u32[]{:S(2)}) collective-permute-start(f32[8,2,16,240]{3,2,1,0:T(8,128)S(1)} %bitcast.41), channel_id=1, source_target_pairs={{0,3},{1,0},{2,1},{3,2},{4,7},{5,4},{6,5},{7,6},{8,11},{9,8},{10,9... | collective-permute-start | bytes 737288 | tf_op jit(solution)/shard_map/ppermute | solution.py:501
  21.4 6.6 %load.1 = (f32[2048,16,128]{2,1,0:T(8,128)S(1)}, f32[8,128]{1,0:T(8,128)}) custom-call(f32[16,2048,128]{2,1,0:T(8,128)} %bitcast.37), custom_call_target="tpu_custom_call" | custom-call | bytes 20000000 | tf_op jit(solution)/shard_map/load/pallas_call | solution.py:482
  28.0 0.0 copy-start.2
  28.0 6.2 %copy-done.2 = f32[2048,16,128]{2,1,0:T(8,128)} copy-done((f32[2048,16,128]{2,1,0:T(8,128)}, f32[2048,16,128]{2,1,0:T(8,128)S(1)}, u32[]{:S(2)}) %copy-start.2) | copy-done | bytes 16777240
  34.2 0.1 slice.4
  34.2 0.1 copy.32
  34.3 0.0 copy-start.3
  34.3 5.8 %copy-done.3 = f32[2048,16,128]{2,1,0:T(8,128)S(1)} copy-done((f32[2048,16,128]{2,1,0:T(8,128)S(1)}, f32[2048,16,128]{2,1,0:T(8,128)}, u32[]{:S(2)}) %copy-start.3) | copy-done | bytes 16777240
  40.1 18.3 %degrid.1 = (f32[256,128]{1,0:T(8,128)}, f32[1024,256]{1,0:T(8,128)S(1)}) custom-call(s32[32,32]{1,0:T(8,128)S(1)} %multiply_bitcast_fusion.base_ref, f32[128,128]{1,0:T(8,128)S(1)} %bitcast.34, f32[2048,16,128]{2,1,0:T(8,128)S(1)} %copy-done.3), custom_call_target="tpu_custom_call" | custom-call | flops 100000000 | bytes 50000000 | tf_op jit(solution)/shard_map/degrid/pallas_call | solution.py:509
  58.4 0.0 copy-done.7
  58.4 0.0 collective-permute-done.rest_1_
  58.5 0.0 collective-permute-done.1.rest_2_
  58.5 0.0 collective-permute-done.2.rest_3_
  58.5 0.0 copy-start.12
  58.5 2.6 %all-to-all-start.1 = ((f32[32,8,128]{2,1,0:T(8,128)}), f32[32,8,128]{2,1,0:T(8,128)S(1)}, u32[]{:S(2)}, u32[]{:S(2)}) async-start(f32[32,8,128]{2,1,0:T(8,128)} %bitcast.14), calls=%async_computation.1 | async-start | bytes 262144 | tf_op jit(solution)/shard_map/all_to_all | solution.py:473
  61.1 0.0 copy-done.6
  61.1 1.0 copy.31.vis_ref
  62.1 0.2 copy.25
  62.3 2.1 %collective-permute-start.3 = (f32[1,16,8,2,240]{4,1,3,2,0:T(8,128)S(1)}, f32[1,16,8,2,240]{4,1,3,2,0:T(8,128)S(1)}, u32[]{:S(2)}, u32[]{:S(2)}) collective-permute-start(f32[1,16,8,2,240]{4,1,3,2,0:T(8,128)S(1)} %copy.25), channel_id=1, source_target_pairs={{0,4},{4,8},{8,12},{12,16},{16,20},{20,24},{24,28},{1,5},{5,9},{9,... | collective-permute-start | bytes 737288 | tf_op jit(solution)/shard_map/ppermute | solution.py:530
  64.4 1.3 collective-permute-start.4
  65.7 3.8 %all-to-all-done.1 = f32[32,8,128]{2,1,0:T(8,128)S(1)} async-done(((f32[32,8,128]{2,1,0:T(8,128)}), f32[32,8,128]{2,1,0:T(8,128)S(1)}, u32[]{:S(2)}, u32[]{:S(2)}) %all-to-all-start.1) | async-done | bytes 131104 | tf_op jit(solution)/shard_map/all_to_all | solution.py:473
  69.5 0.0 copy-done.10
  69.5 0.6 copy-done.9
  70.1 19.3 %rowgrads.1 = (f32[8,2,16,240]{3,2,1,0:T(8,128)}, f32[8,2,16,240]{3,2,1,0:T(8,128)}, f32[8,2,16,240]{3,2,1,0:T(8,128)}, f32[8,2,16,240]{3,2,1,0:T(8,128)}, f32[256,128]{1,0:T(8,128)}) custom-call(f32[8,512]{1,0:T(8,128)} %get-tuple-element.33.rows_ref, f32[512,8]{1,0:T(8,128)} %get-tuple-element.34.cols_ref, bf16[512,512]{1,0:T(8,128)(2,1)} %copy.31.vis_ref, ...), custom_call_target="tpu_custom_call" | custom-call | flops 20000000000 | bytes 10000000 | tf_op jit(solution)/shard_map/rowgrads/pallas_call | solution.py:537
  89.4 0.0 collective-permute-done.3
  89.4 0.0 collective-permute-done.4
  89.4 4.2 %all-to-all-start.2 = ((f32[32,8,128]{2,1,0:T(8,128)}), f32[32,8,128]{2,1,0:T(8,128)S(1)}, u32[]{:S(2)}, u32[]{:S(2)}) async-start(f32[32,8,128]{2,1,0:T(8,128)} %bitcast.35), calls=%async_computation.2 | async-start | bytes 262144 | tf_op jit(solution)/shard_map/all_to_all | solution.py:473
  93.7 3.7 %collective-permute-start.5 = (f32[8,2,16,240]{3,2,1,0:T(8,128)}, f32[8,2,16,240]{3,2,1,0:T(8,128)S(1)}, u32[]{:S(2)}, u32[]{:S(2)}) collective-permute-start(f32[8,2,16,240]{3,2,1,0:T(8,128)} %get-tuple-element.50), channel_id=1, source_target_pairs={{0,3},{1,0},{2,1},{3,2},{4,7},{5,4},{6,5},{7,6},{8,11},{9,8},{10,9... | collective-permute-start | bytes 737288 | tf_op jit(solution)/shard_map/ppermute | solution.py:573
  97.4 0.0 collective-permute-start.6
  97.4 1.1 collective-permute-start.7
  98.4 0.9 copy-done.4
  99.4 1.1 clear.1.zero_ref
  100.5 0.0 copy-start
  100.5 6.2 %copy-done = f32[2048,16,128]{2,1,0:T(8,128)} copy-done((f32[2048,16,128]{2,1,0:T(8,128)}, f32[2048,16,128]{2,1,0:T(8,128)S(1)}, u32[]{:S(2)}) %copy-start) | copy-done | bytes 16777240
  106.7 0.0 all-to-all-done.2
  106.7 5.8 %copy-done.1 = f32[2048,16,128]{2,1,0:T(8,128)S(1)} copy-done((f32[2048,16,128]{2,1,0:T(8,128)S(1)}, f32[2048,16,128]{2,1,0:T(8,128)}, u32[]{:S(2)}) %copy-start.1) | copy-done | bytes 16777240
  112.4 24.1 %scatter.1 = (f32[16,2048,128]{2,1,0:T(8,128)}, f32[2048,16,128]{2,1,0:T(8,128)S(1)}) custom-call(s32[32,32]{1,0:T(8,128)S(1)} %multiply_bitcast_fusion.base_ref, f32[256,128]{1,0:T(8,128)S(1)} %bitcast.36, f32[1024,256]{1,0:T(8,128)S(1)} %get-tuple-element.47.w_ref, f32[2048,16,128]{2,1,0:T(8,128)S(1)} %copy-done.1), custom_call_target="tpu_custom_call", output_to_operand_aliasing={{1}: (3, {})} | custom-call | flops 100000000 | bytes 100000000 | tf_op jit(solution)/shard_map/scatter/pallas_call | solution.py:576
  136.6 0.0 collective-permute-done.5
  136.6 0.0 collective-permute-done.6
  136.6 0.0 collective-permute-done.7
  136.6 0.2 bitcast_add_fusion
  136.9 0.9 copy.30
  (16 shorter events, 0.1 us)
Async XLA Ops:
  2.8 14.8 %all-to-all-start = ((f32[32,4,128]{2,1,0:T(4,128)}), f32[32,4,128]{2,1,0:T(4,128)S(1)}, u32[]{:S(2)}, u32[]{:S(2)}) async-start(f32[32,4,128]{2,1,0:T(4,128)} %bitcast.44), calls=%async_computation | async-start | bytes 131072 | tf_op jit(solution)/shard_map/all_to_all | solution.py:473
  11.2 47.3 %copy-start.7 = (f32[1,16,8,2,240]{4,1,3,2,0:T(8,128)}, f32[1,16,8,2,240]{4,1,3,2,0:T(8,128)S(1)}, u32[]{:S(2)}) copy-start(f32[1,16,8,2,240]{4,1,3,2,0:T(8,128)S(1)} %copy.35) | copy-start | bytes 737284
  17.6 40.9 %collective-permute-start = (f32[8,2,16,240]{3,2,1,0:T(8,128)S(1)}, f32[8,2,16,240]{3,2,1,0:T(8,128)S(1)}, u32[]{:S(2)}, u32[]{:S(2)}) collective-permute-start(f32[8,2,16,240]{3,2,1,0:T(8,128)S(1)} %bitcast.39), channel_id=1, source_target_pairs={{0,1},{1,2},{2,3},{3,0},{4,5},{5,6},{6,7},{7,4},{8,9},{9,10},{10,1... | collective-permute-start | bytes 737288 | tf_op jit(solution)/shard_map/ppermute | solution.py:501
  17.8 40.7 %collective-permute-start.1 = (f32[8,2,16,240]{3,2,1,0:T(8,128)S(1)}, f32[8,2,16,240]{3,2,1,0:T(8,128)S(1)}, u32[]{:S(2)}, u32[]{:S(2)}) collective-permute-start(f32[8,2,16,240]{3,2,1,0:T(8,128)S(1)} %bitcast.40), channel_id=1, source_target_pairs={{0,2},{1,3},{2,0},{3,1},{4,6},{5,7},{6,4},{7,5},{8,10},{9,11},{10,... | collective-permute-start | bytes 737288 | tf_op jit(solution)/shard_map/ppermute | solution.py:501
  18.9 39.5 %collective-permute-start.2 = (f32[8,2,16,240]{3,2,1,0:T(8,128)S(1)}, f32[8,2,16,240]{3,2,1,0:T(8,128)S(1)}, u32[]{:S(2)}, u32[]{:S(2)}) collective-permute-start(f32[8,2,16,240]{3,2,1,0:T(8,128)S(1)} %bitcast.41), channel_id=1, source_target_pairs={{0,3},{1,0},{2,1},{3,2},{4,7},{5,4},{6,5},{7,6},{8,11},{9,8},{10,9... | collective-permute-start | bytes 737288 | tf_op jit(solution)/shard_map/ppermute | solution.py:501
  21.4 39.7 %copy-start.6 = (bf16[512,2,240]{0,2,1:T(8,128)(2,1)S(1)}, bf16[512,2,240]{0,2,1:T(8,128)(2,1)}, u32[]{:S(2)}) copy-start(bf16[512,2,240]{0,2,1:T(8,128)(2,1)} %param.9) | copy-start | bytes 1474564
  21.4 40.8 %copy-start.5 = (f32[1,16,8,2,240]{4,3,2,1,0:T(2,128)S(1)}, f32[1,16,8,2,240]{4,3,2,1,0:T(2,128)}, u32[]{:S(2)}) copy-start(f32[1,16,8,2,240]{4,3,2,1,0:T(2,128)} %param.16) | copy-start | bytes 737284
  28.0 6.2 %copy-start.2 = (f32[2048,16,128]{2,1,0:T(8,128)}, f32[2048,16,128]{2,1,0:T(8,128)S(1)}, u32[]{:S(2)}) copy-start(f32[2048,16,128]{2,1,0:T(8,128)S(1)} %get-tuple-element.35.held) | copy-start | bytes 50331652
  34.3 5.8 %copy-start.3 = (f32[2048,16,128]{2,1,0:T(8,128)S(1)}, f32[2048,16,128]{2,1,0:T(8,128)}, u32[]{:S(2)}) copy-start(f32[2048,16,128]{2,1,0:T(8,128)} %copy-done.2) | copy-start | bytes 50331652
  58.5 11.0 %copy-start.10 = (f32[8,2,16,240]{3,2,1,0:T(8,128)}, f32[8,2,16,240]{3,2,1,0:T(8,128)S(1)}, u32[]{:S(2)}) copy-start(f32[8,2,16,240]{3,2,1,0:T(8,128)S(1)} %collective-permute-done.rest_1_) | copy-start | bytes 737284
  58.5 11.0 %copy-start.11 = (f32[8,2,16,240]{3,2,1,0:T(8,128)}, f32[8,2,16,240]{3,2,1,0:T(8,128)S(1)}, u32[]{:S(2)}) copy-start(f32[8,2,16,240]{3,2,1,0:T(8,128)S(1)} %collective-permute-done.1.rest_2_) | copy-start | bytes 737284
  58.5 11.0 %copy-start.12 = (f32[8,2,16,240]{3,2,1,0:T(8,128)}, f32[8,2,16,240]{3,2,1,0:T(8,128)S(1)}, u32[]{:S(2)}) copy-start(f32[8,2,16,240]{3,2,1,0:T(8,128)S(1)} %collective-permute-done.2.rest_3_) | copy-start | bytes 737284
  58.5 11.0 %all-to-all-start.1 = ((f32[32,8,128]{2,1,0:T(8,128)}), f32[32,8,128]{2,1,0:T(8,128)S(1)}, u32[]{:S(2)}, u32[]{:S(2)}) async-start(f32[32,8,128]{2,1,0:T(8,128)} %bitcast.14), calls=%async_computation.1 | async-start | bytes 262144 | tf_op jit(solution)/shard_map/all_to_all | solution.py:473
  62.3 27.1 %collective-permute-start.3 = (f32[1,16,8,2,240]{4,1,3,2,0:T(8,128)S(1)}, f32[1,16,8,2,240]{4,1,3,2,0:T(8,128)S(1)}, u32[]{:S(2)}, u32[]{:S(2)}) collective-permute-start(f32[1,16,8,2,240]{4,1,3,2,0:T(8,128)S(1)} %copy.25), channel_id=1, source_target_pairs={{0,4},{4,8},{8,12},{12,16},{16,20},{20,24},{24,28},{1,5},{5,9},{9,... | collective-permute-start | bytes 737288 | tf_op jit(solution)/shard_map/ppermute | solution.py:530
  64.4 25.0 %collective-permute-start.4 = (f32[1,16,8,2,240]{4,1,3,2,0:T(8,128)S(1)}, f32[1,16,8,2,240]{4,1,3,2,0:T(8,128)S(1)}, u32[]{:S(2)}, u32[]{:S(2)}) collective-permute-start(f32[1,16,8,2,240]{4,1,3,2,0:T(8,128)S(1)} %copy.25), channel_id=1, source_target_pairs={{4,0},{8,4},{12,8},{16,12},{20,16},{24,20},{28,24},{5,1},{9,5},{13... | collective-permute-start | bytes 737288 | tf_op jit(solution)/shard_map/ppermute | solution.py:531
  69.5 0.6 copy-start.9
  89.4 17.2 %all-to-all-start.2 = ((f32[32,8,128]{2,1,0:T(8,128)}), f32[32,8,128]{2,1,0:T(8,128)S(1)}, u32[]{:S(2)}, u32[]{:S(2)}) async-start(f32[32,8,128]{2,1,0:T(8,128)} %bitcast.35), calls=%async_computation.2 | async-start | bytes 262144 | tf_op jit(solution)/shard_map/all_to_all | solution.py:473
  93.7 42.9 %collective-permute-start.5 = (f32[8,2,16,240]{3,2,1,0:T(8,128)}, f32[8,2,16,240]{3,2,1,0:T(8,128)S(1)}, u32[]{:S(2)}, u32[]{:S(2)}) collective-permute-start(f32[8,2,16,240]{3,2,1,0:T(8,128)} %get-tuple-element.50), channel_id=1, source_target_pairs={{0,3},{1,0},{2,1},{3,2},{4,7},{5,4},{6,5},{7,6},{8,11},{9,8},{10,9... | collective-permute-start | bytes 737288 | tf_op jit(solution)/shard_map/ppermute | solution.py:573
  97.4 39.2 %collective-permute-start.6 = (f32[8,2,16,240]{3,2,1,0:T(8,128)}, f32[8,2,16,240]{3,2,1,0:T(8,128)S(1)}, u32[]{:S(2)}, u32[]{:S(2)}) collective-permute-start(f32[8,2,16,240]{3,2,1,0:T(8,128)} %get-tuple-element.51), channel_id=1, source_target_pairs={{0,2},{1,3},{2,0},{3,1},{4,6},{5,7},{6,4},{7,5},{8,10},{9,11},{10,... | collective-permute-start | bytes 737288 | tf_op jit(solution)/shard_map/ppermute | solution.py:573
  97.4 39.3 %collective-permute-start.7 = (f32[8,2,16,240]{3,2,1,0:T(8,128)}, f32[8,2,16,240]{3,2,1,0:T(8,128)S(1)}, u32[]{:S(2)}, u32[]{:S(2)}) collective-permute-start(f32[8,2,16,240]{3,2,1,0:T(8,128)} %get-tuple-element.52), channel_id=1, source_target_pairs={{0,1},{1,2},{2,3},{3,0},{4,5},{5,6},{6,7},{7,4},{8,9},{9,10},{10,1... | collective-permute-start | bytes 737288 | tf_op jit(solution)/shard_map/ppermute | solution.py:573
  98.4 0.9 copy-start.4
  99.4 37.3 %copy-start.8 = (f32[8,2,16,240]{3,2,1,0:T(8,128)S(1)}, f32[8,2,16,240]{3,2,1,0:T(8,128)}, u32[]{:S(2)}) copy-start(f32[8,2,16,240]{3,2,1,0:T(8,128)} %get-tuple-element.53) | copy-start | bytes 737284
  100.5 6.2 %copy-start = (f32[2048,16,128]{2,1,0:T(8,128)}, f32[2048,16,128]{2,1,0:T(8,128)S(1)}, u32[]{:S(2)}) copy-start(f32[2048,16,128]{2,1,0:T(8,128)S(1)} %clear.1.zero_ref) | copy-start | bytes 50331652
  106.7 5.8 %copy-start.1 = (f32[2048,16,128]{2,1,0:T(8,128)S(1)}, f32[2048,16,128]{2,1,0:T(8,128)}, u32[]{:S(2)}) copy-start(f32[2048,16,128]{2,1,0:T(8,128)} %copy-done) | copy-start | bytes 50331652

commit v5 on v3

--- a/solution.py
+++ b/solution.py
@@ -115,56 +115,89 @@
     cols_ref[...] = table.T
 
 
-def load_kernel(sky_ref, held_ref, sem):
-    copies = []
-    for i in range(sky_ref.shape[0]):
-        copy = pltpu.make_async_copy(sky_ref.at[i], held_ref.at[:, i], sem.at[i])
-        copy.start()
-        copies.append(copy)
-    for copy in copies:
-        copy.wait()
+def turn_fields(n, cap, count, recv_ref, turn_s):
+    per_block = LANES // n
+    turn_s[...] = read_wide(recv_ref, n).T
+    return [
+        jnp.concatenate(
+            [
+                turn_s[pl.ds(k * cap + q, cap // per_block, stride=per_block), :]
+                for q in range(per_block)
+            ],
+            axis=1,
+        )
+        for k in range(count)
+    ]
+
+
+def each_slot(n, visit, carry, jb):
+    per_block = LANES // n
+    unroll = min(n, 32)
+    for q in range(per_block):
+        j = jb * per_block + q
+
+        def step(g, inner):
+            first = g * unroll
+            for u in range(unroll):
+                inner = visit(inner, j, first + u, u, q * n + first)
+            return inner
+
+        if n == unroll:
+            carry = step(0, carry)
+        else:
+            carry = lax.fori_loop(0, n // unroll, step, carry)
+    return carry
 
 
 def degrid_kernel(
     n, cap, taps,
-    base_ref, recv_ref, held, out_ref, w_ref, blocks,
+    base_ref, recv_ref, sky_ref, out_ref, w_ref,
+    held_re, held_im, w_s, turn_s, blocks, sem,
 ):
-    pairs = held.shape[1]
-    planes = 2 * pairs
-    recv = read_wide(recv_ref, n)
-    lane = iota((n, 2 * LANES), 1).astype(f32)
-    for j in range(cap):
-        place = lane - recv[:, taps * cap + j : taps * cap + j + 1]
-        w = jnp.zeros((n, 2 * LANES), f32)
-        for k in range(taps):
-            w = jnp.where(place == float(k), recv[:, k * cap + j : k * cap + j + 1], w)
-        w_ref[j * n : (j + 1) * n, :] = w
+    halves = (held_re, held_im)
+    facets = held_re.shape[1]
+    planes = 4 * facets
+    copies = []
+    for x, held in enumerate(halves):
+        mine = []
+        for f in range(facets):
+            i = x * facets + f
+            copy = pltpu.make_async_copy(sky_ref.at[i], held.at[:, f], sem.at[i])
+            copy.start()
+            mine.append(copy)
+        copies.append(mine)
     per_block = LANES // n
     block_count = cap // per_block
-    unroll = min(n, 16)
-    lane3 = iota((2, pairs, LANES), 2)
-
-    def block(jb, carry):
-        acc = jnp.zeros((2, pairs, LANES), f32)
-        for q in range(per_block):
-            j = jb * per_block + q
-
-            def step(g, acc):
-                first = g * unroll
-                rel = lane3 - (q * n + first)
-                for u in range(unroll):
-                    start = base_ref[j, first + u]
-                    w = w_ref[pl.ds(j * n + first + u, 1), :]
-                    window = held[pl.ds(start, 4)]
-                    prod = window[0:2] * w[:, :LANES] + window[2:4] * w[:, LANES:]
-                    acc = jnp.where(rel == u, jnp.sum(prod, axis=2, keepdims=True), acc)
-                return acc
-
-            acc = lax.fori_loop(0, n // unroll, step, acc)
-        blocks[jb] = acc.reshape(planes, LANES)
-        return carry
-
-    lax.fori_loop(0, block_count, block, 0)
+    fields = turn_fields(n, cap, taps + 1, recv_ref, turn_s)
+    line = iota((2 * LANES, LANES), 0).astype(f32)
+    for jb in range(block_count):
+        place = line - fields[taps][jb : jb + 1, :]
+        w = jnp.zeros((2 * LANES, LANES), f32)
+        for k in range(taps):
+            w = jnp.where(place == float(k), fields[k][jb : jb + 1, :], w)
+        w_s[jb * LANES : (jb + 1) * LANES, :] = w.T
+    save = pltpu.make_async_copy(w_s, w_ref, sem.at[2 * facets])
+    save.start()
+    lane3 = iota((2, facets, LANES), 2)
+    for x, held in enumerate(halves):
+        for copy in copies[x]:
+            copy.wait()
+
+        def visit(acc, j, src, u, first):
+            w = w_s[pl.ds(j * n + src, 1), :]
+            window = held[pl.ds(base_ref[j, src], 4)]
+            prod = window[0:2] * w[:, :LANES] + window[2:4] * w[:, LANES:]
+            return jnp.where(
+                lane3 == first + u, jnp.sum(prod, axis=2, keepdims=True), acc
+            )
+
+        def block(jb, carry):
+            acc = each_slot(n, visit, jnp.zeros((2, facets, LANES), f32), jb)
+            for t in range(2):
+                blocks[jb, pl.ds((2 * t + x) * facets, facets), :] = acc[t]
+            return carry
+
+        lax.fori_loop(0, block_count, block, 0)
     turned = [blocks[jb].T for jb in range(block_count)]
     pieces = []
     for j in range(cap):
@@ -173,8 +206,9 @@
     per_line = LANES // planes
     per = cap // per_line
     for i in range(per):
-        line = jnp.concatenate(pieces[i * per_line : (i + 1) * per_line], axis=1)
-        out_ref[pl.ds(i, n, stride=per), :] = line
+        wide_line = jnp.concatenate(pieces[i * per_line : (i + 1) * per_line], axis=1)
+        out_ref[pl.ds(i, n, stride=per), :] = wide_line
+    save.wait()
 
 
 def rows_kernel(
@@ -333,17 +367,20 @@
         send_ref[pl.ds(i, n, stride=line_count), :] = total[:, :LANES] + total[:, LANES:]
 
 
-def scatter_kernel(n, cap, base_ref, grad_ref, w_ref, out_ref, held, blocks, sem):
-    pairs = out_ref.shape[0]
-    planes = 2 * pairs
-    lines = held.shape[0]
-    fill = 32
+def scatter_kernel(
+    n, cap, base_ref, grad_ref, w_ref, out_ref, held_re, held_im, blocks, sem
+):
+    halves = (held_re, held_im)
+    facets = held_re.shape[1]
+    planes = 4 * facets
+    fill = 64
 
     def clear(i, carry):
-        held[pl.ds(i * fill, fill)] = jnp.zeros((fill, pairs, LANES), f32)
+        for held in halves:
+            held[pl.ds(i * fill, fill)] = jnp.zeros((fill, facets, LANES), f32)
         return carry
 
-    lax.fori_loop(0, lines // fill, clear, 0)
+    lax.fori_loop(0, held_re.shape[0] // fill, clear, 0)
     per_line = LANES // planes
     per = cap // per_line
     pieces = []
@@ -357,37 +394,34 @@
         mine = pieces[jb * per_block : (jb + 1) * per_block]
         joined = mine[0] if per_block == 1 else jnp.concatenate(mine, axis=0)
         blocks[jb] = joined.T
-    unroll = min(n, 16)
-    lane3 = iota((2, pairs, LANES), 2)
-
-    def block(jb, carry):
-        values = blocks[jb].reshape(2, pairs, LANES)
-        for q in range(per_block):
-            j = jb * per_block + q
-
-            def step(g, inner):
-                first = g * unroll
-                rel = lane3 - (q * n + first)
-                for u in range(unroll):
-                    at = pl.ds(base_ref[j, first + u], 4)
-                    w = w_ref[pl.ds(j * n + first + u, 1), :]
-                    value = jnp.sum(
-                        jnp.where(rel == u, values, 0.0), axis=2, keepdims=True
-                    )
-                    held[at] = held[at] + jnp.concatenate(
-                        [value * w[:, :LANES], value * w[:, LANES:]], axis=0
-                    )
+    lane3 = iota((2, facets, LANES), 2)
+    copies = []
+    for x, held in enumerate(halves):
+
+        def block(jb, carry):
+            values = jnp.stack(
+                [blocks[jb, pl.ds((2 * t + x) * facets, facets), :] for t in range(2)]
+            )
+
+            def visit(inner, j, src, u, first):
+                at = pl.ds(base_ref[j, src], 4)
+                w = w_ref[pl.ds(j * n + src, 1), :]
+                value = jnp.sum(
+                    jnp.where(lane3 == first + u, values, 0.0), axis=2, keepdims=True
+                )
+                held[at] = held[at] + jnp.concatenate(
+                    [value * w[:, :LANES], value * w[:, LANES:]], axis=0
+                )
                 return inner
 
-            carry = lax.fori_loop(0, n // unroll, step, carry)
-        return carry
-
-    lax.fori_loop(0, block_count, block, 0)
-    copies = []
-    for i in range(pairs):
-        copy = pltpu.make_async_copy(held.at[:, i], out_ref.at[i], sem.at[i])
-        copy.start()
-        copies.append(copy)
+            return each_slot(n, visit, carry, jb)
+
+        lax.fori_loop(0, block_count, block, 0)
+        for f in range(facets):
+            i = x * facets + f
+            copy = pltpu.make_async_copy(held.at[:, f], out_ref.at[i], sem.at[i])
+            copy.start()
+            copies.append(copy)
     for copy in copies:
         copy.wait()
 
@@ -455,19 +489,8 @@
         .transpose(0, 2, 1, 3)
         .reshape(pairs, terms * tiles, LANES)
     )
-    held = pl.pallas_call(
-        load_kernel,
-        out_shape=pltpu.VMEM((terms * tiles, pairs, LANES), f32),
-        in_specs=[ANY],
-        out_specs=VMEM,
-        scratch_shapes=[pltpu.SemaphoreType.DMA((pairs,))],
-        compiler_params=params(44),
-        cost_estimate=cost(0, 2 * 10**7),
-        name="load",
-    )(sky)
-    received, gain_turned, held = lax.optimization_barrier(
-        (exchange(send), gain_turned, held)
-    )
+    send, gain_turned = lax.optimization_barrier((send, gain_turned))
+    received = exchange(send)
     gathered = [gain_turned]
     for k in range(1, group_count):
         gathered.append(
@@ -485,15 +508,23 @@
             jax.ShapeDtypeStruct((slot_lines, LANES), f32),
             jax.ShapeDtypeStruct((n * cap, 2 * LANES), f32),
         ),
-        in_specs=[SMEM, VMEM, VMEM],
-        out_specs=(VMEM, VMEM),
-        scratch_shapes=[pltpu.VMEM((block_count, planes, LANES), f32)],
-        compiler_params=params(24),
-        cost_estimate=cost(10**8, 5 * 10**7),
+        in_specs=[SMEM, VMEM, ANY],
+        out_specs=(VMEM, ANY),
+        scratch_shapes=[
+            pltpu.VMEM((terms * tiles, facets, LANES), f32),
+            pltpu.VMEM((terms * tiles, facets, LANES), f32),
+            pltpu.VMEM((n * cap, 2 * LANES), f32),
+            pltpu.VMEM((lines * LANES, n), f32),
+            pltpu.VMEM((block_count, planes, LANES), f32),
+            pltpu.SemaphoreType.DMA((pairs + 1,)),
+        ],
+        compiler_params=params(),
+        cost_estimate=cost(10**8, 7 * 10**7),
         name="degrid",
-    )(base, received, held)
+    )(base, received, sky)
     values, *gathered = lax.optimization_barrier((values, *gathered))
-    back, gain_here = lax.optimization_barrier((exchange(values), gain_field))
+    values, gain_here = lax.optimization_barrier((values, gain_field))
+    back = exchange(values)
     below = lax.ppermute(gain_here, "tm", [(i, i + 1) for i in range(time_count - 1)])
     above = lax.ppermute(gain_here, "tm", [(i + 1, i) for i in range(time_count - 1)])
 
@@ -526,7 +557,7 @@
 
     *parts, send_grad = outs
     send_grad, below, above = lax.optimization_barrier((send_grad, below, above))
-    got, *parts = lax.optimization_barrier((exchange(send_grad), *parts))
+    got = exchange(send_grad)
     for k in range(1, group_count):
         parts[k] = lax.ppermute(
             parts[k], "bl", [(i, (i - k) % group_count) for i in range(group_count)]
@@ -537,7 +568,8 @@
         in_specs=[SMEM, VMEM, VMEM],
         out_specs=ANY,
         scratch_shapes=[
-            pltpu.VMEM((terms * tiles, pairs, LANES), f32),
+            pltpu.VMEM((terms * tiles, facets, LANES), f32),
+            pltpu.VMEM((terms * tiles, facets, LANES), f32),
             pltpu.VMEM((block_count, planes, LANES), f32),
             pltpu.SemaphoreType.DMA((pairs,)),
         ],

time: 126 us -> 107 us (0.85)
  blocking collectives: 14.1 us -> 0 us
  local copies, waits for them, and re-layouts: 16.3 us -> 4.72 us
  starting transfers between devices: 23.4 us -> 34 us
  Pallas kernels: 61.5 us -> 53.4 us
  waiting for transfers between devices: 8.78 us -> 11.7 us
    all_to_all x1 -> x0, blocking collectives: 14.1 us -> none  [exchange(): x = lax.all_to_all(x, both, split_axis=0, concat_axis=0, tiled=True)]
    unnamed x27 -> x22, local copies, waits for them, and re-layouts: 15.1 us -> 3.4 us
    all_to_all x2 -> x3, starting transfers between devices: 12.8 us -> 20.2 us  [exchange(): x = lax.all_to_all(x, both, split_axis=0, concat_axis=0, tiled=True)]
    pallas_call x1 -> x0, Pallas kernels: 6.03 us -> none  [body(): pl.pallas_call(load_kernel, out_shape=pltpu.VMEM((terms * tiles, pairs, L...]
    all_to_all x2 -> x3, waiting for transfers between devices: 7.35 us -> 9.75 us  [exchange(): x = lax.all_to_all(x, both, split_axis=0, concat_axis=0, tiled=True)]
    ppermute x3, starting transfers between devices: 2.4 us -> 4.75 us  [body(): lax.ppermute(parts[k], 'bl', [(i, (i - k) % group_count) for i in range(g...]
    pallas_call x1, Pallas kernels: 21.2 us -> 19 us  [body(): pl.pallas_call(functools.partial(scatter_kernel, n, cap), out_shape=jax.S...]
  transfers between devices with their start and end apart: 10 -> 11, of which waited for: 2 -> 5; matrix products, arithmetic and copies ran while one was open for 2% -> 2% of each run, Pallas kernels for 47% -> 48%
where the time goes in v5:
time: 107 us; the launch traced here: 105 us
  Pallas kernels  53.4 us (50%)
  starting transfers between devices  34 us (32%)
  waiting for transfers between devices  11.7 us (11%)
  local copies, waits for them, and re-layouts  4.72 us (4%)
    all_to_all x3, starting transfers between devices, exchange(): x = lax.all_to_all(x, both, split_axis=0, concat_axis=0, tiled=True)  20.2 us
    pallas_call x1, Pallas kernels, body(): pl.pallas_call(functools.partial(rows_kernel, n, cap, group_count), out_s...  19.3 us
    pallas_call x1, Pallas kernels, body(): pl.pallas_call(functools.partial(scatter_kernel, n, cap), out_shape=jax.S...  19 us
    pallas_call x1, Pallas kernels, body(): pl.pallas_call(functools.partial(degrid_kernel, n, cap, taps), out_shape=...  12.8 us
    all_to_all x3, waiting for transfers between devices, exchange(): x = lax.all_to_all(x, both, split_axis=0, concat_axis=0, tiled=True)  9.75 us
    ppermute x3, starting transfers between devices, body(): lax.ppermute(gain_turned, 'bl', [(i, (i + k) % group_count) for i in rang...  5.65 us
    ppermute x3, starting transfers between devices, body(): lax.ppermute(parts[k], 'bl', [(i, (i - k) % group_count) for i in range(g...  4.75 us
    unnamed x22, local copies, waits for them, and re-layouts  3.4 us
  transfers between devices with their start and end apart: 11, of which 5 were waited for; matrix products, arithmetic and copies ran while one was open for 2% of the time, Pallas kernels for 48%

profile of v5, /device:TPU:0, one launch (start us, length us, event | category | flops | bytes accessed | tf_op | source)
XLA Modules:
  0.0 105.5 jit_solution(15843261891604211371)
XLA Ops:
  0.6 0.0 copy-start
  0.6 0.0 copy-start.3
  0.7 1.2 %copy.35 = f32[1,16,8,2,240]{4,1,3,2,0:T(8,128)S(1)} copy(f32[1,16,8,2,240]{4,3,2,1,0:T(2,128)} %param.16) | data formatting | bytes 491520 | tf_op args[7]
  1.8 0.0 copy-start.4
  1.8 2.2 %slots.1 = (f32[128,128]{1,0:T(8,128)}, f32[8,512]{1,0:T(8,128)}, f32[512,8]{1,0:T(8,128)}) custom-call(s32[1]{0:T(128)} %bitcast.shift_ref, s32[1,512]{1,0:T(1,128)} %bitcast.48, s32[1,512]{1,0:T(1,128)} %bitcast.49, f32[8,512]{1,0:T(8,128)} %taps_ref.1, s32[2,512]{1,0:T(2,128)} %pairs_ref.1, f32[1,512]{1,0:T(1,128)} %bitcast.50, s32[1,512]{1,0:T(1,128)} %bitcast.51), custom_call_target="tpu_custom_call" | custom-call | flops 1000000000 | bytes 1000000 | tf_op jit(solution)/shard_map/slots/pallas_call | solution.py:460
  4.1 7.3 %all-to-all-start = ((f32[32,4,128]{2,1,0:T(4,128)}), f32[32,4,128]{2,1,0:T(4,128)S(1)}, u32[]{:S(2)}, u32[]{:S(2)}) async-start(f32[32,4,128]{2,1,0:T(4,128)} %bitcast.47), calls=%async_computation | async-start | bytes 131072 | tf_op jit(solution)/shard_map/all_to_all | solution.py:484
  11.4 1.8 %collective-permute-start = (f32[8,2,16,240]{3,2,1,0:T(8,128)S(1)}, f32[8,2,16,240]{3,2,1,0:T(8,128)S(1)}, u32[]{:S(2)}, u32[]{:S(2)}) collective-permute-start(f32[8,2,16,240]{3,2,1,0:T(8,128)S(1)} %bitcast.40), channel_id=1, source_target_pairs={{0,1},{1,2},{2,3},{3,0},{4,5},{5,6},{6,7},{7,4},{8,9},{9,10},{10,1... | collective-permute-start | bytes 737288 | tf_op jit(solution)/shard_map/ppermute | solution.py:497
  13.2 2.4 %collective-permute-start.1 = (f32[8,2,16,240]{3,2,1,0:T(8,128)S(1)}, f32[8,2,16,240]{3,2,1,0:T(8,128)S(1)}, u32[]{:S(2)}, u32[]{:S(2)}) collective-permute-start(f32[8,2,16,240]{3,2,1,0:T(8,128)S(1)} %bitcast.41), channel_id=1, source_target_pairs={{0,2},{1,3},{2,0},{3,1},{4,6},{5,7},{6,4},{7,5},{8,10},{9,11},{10,... | collective-permute-start | bytes 737288 | tf_op jit(solution)/shard_map/ppermute | solution.py:497
  15.6 1.4 %collective-permute-start.2 = (f32[8,2,16,240]{3,2,1,0:T(8,128)S(1)}, f32[8,2,16,240]{3,2,1,0:T(8,128)S(1)}, u32[]{:S(2)}, u32[]{:S(2)}) collective-permute-start(f32[8,2,16,240]{3,2,1,0:T(8,128)S(1)} %bitcast.42), channel_id=1, source_target_pairs={{0,3},{1,0},{2,1},{3,2},{4,7},{5,4},{6,5},{7,6},{8,11},{9,8},{10,9... | collective-permute-start | bytes 737288 | tf_op jit(solution)/shard_map/ppermute | solution.py:497
  17.0 2.2 %all-to-all-done = f32[32,4,128]{2,1,0:T(4,128)S(1)} async-done(((f32[32,4,128]{2,1,0:T(4,128)}), f32[32,4,128]{2,1,0:T(4,128)S(1)}, u32[]{:S(2)}, u32[]{:S(2)}) %all-to-all-start) | async-done | bytes 65568 | tf_op jit(solution)/shard_map/all_to_all | solution.py:484
  19.2 0.0 copy-start.1
  19.2 0.1 copy.23
  19.3 0.6 fusion.2.base_ref
  19.9 0.0 copy-done.1
  19.9 12.8 %degrid.1 = (f32[256,128]{1,0:T(8,128)}, f32[1024,256]{1,0:T(8,128)}) custom-call(s32[32,32]{1,0:T(8,128)} %fusion.2.base_ref, f32[128,128]{1,0:T(8,128)} %bitcast.37, f32[16,2048,128]{2,1,0:T(8,128)} %bitcast.35), custom_call_target="tpu_custom_call" | custom-call | flops 100000000 | bytes 70000000 | tf_op jit(solution)/shard_map/degrid/pallas_call | solution.py:505
  32.8 0.0 collective-permute-done.rest_1_
  32.8 0.0 copy-start.7
  32.8 1.2 %collective-permute-done.1.rest_2_ = f32[8,2,16,240]{3,2,1,0:T(8,128)S(1)} collective-permute-done((f32[8,2,16,240]{3,2,1,0:T(8,128)S(1)}, f32[8,2,16,240]{3,2,1,0:T(8,128)S(1)}, u32[]{:S(2)}, u32[]{:S(2)}) %collective-permute-start.1) | collective-permute-done | bytes 245792 | tf_op jit(solution)/shard_map/ppermute | solution.py:497
  34.0 0.0 collective-permute-done.2.rest_3_
  34.0 8.6 %all-to-all-start.1 = ((f32[32,8,128]{2,1,0:T(8,128)}), f32[32,8,128]{2,1,0:T(8,128)S(1)}, u32[]{:S(2)}, u32[]{:S(2)}) async-start(f32[32,8,128]{2,1,0:T(8,128)} %bitcast.46), calls=%async_computation.1 | async-start | bytes 262144 | tf_op jit(solution)/shard_map/all_to_all | solution.py:484
  42.6 0.0 copy-done.3
  42.7 1.0 copy.32.vis_ref
  43.7 0.0 copy-done
  43.7 0.2 copy.26
  43.9 2.2 %collective-permute-start.3 = (f32[1,16,8,2,240]{4,1,3,2,0:T(8,128)S(1)}, f32[1,16,8,2,240]{4,1,3,2,0:T(8,128)S(1)}, u32[]{:S(2)}, u32[]{:S(2)}) collective-permute-start(f32[1,16,8,2,240]{4,1,3,2,0:T(8,128)S(1)} %copy.26), channel_id=1, source_target_pairs={{0,4},{4,8},{8,12},{12,16},{16,20},{20,24},{24,28},{1,5},{5,9},{9,... | collective-permute-start | bytes 737288 | tf_op jit(solution)/shard_map/ppermute | solution.py:528
  46.0 1.3 %collective-permute-start.4 = (f32[1,16,8,2,240]{4,1,3,2,0:T(8,128)S(1)}, f32[1,16,8,2,240]{4,1,3,2,0:T(8,128)S(1)}, u32[]{:S(2)}, u32[]{:S(2)}) collective-permute-start(f32[1,16,8,2,240]{4,1,3,2,0:T(8,128)S(1)} %copy.26), channel_id=1, source_target_pairs={{4,0},{8,4},{12,8},{16,12},{20,16},{24,20},{28,24},{5,1},{9,5},{13... | collective-permute-start | bytes 737288 | tf_op jit(solution)/shard_map/ppermute | solution.py:529
  47.3 3.7 %all-to-all-done.1 = f32[32,8,128]{2,1,0:T(8,128)S(1)} async-done(((f32[32,8,128]{2,1,0:T(8,128)}), f32[32,8,128]{2,1,0:T(8,128)S(1)}, u32[]{:S(2)}, u32[]{:S(2)}) %all-to-all-start.1) | async-done | bytes 131104 | tf_op jit(solution)/shard_map/all_to_all | solution.py:484
  51.1 0.0 copy-done.4
  51.1 0.0 copy-done.7
  51.1 0.0 copy-done.8
  51.1 0.0 copy-done.9
  51.1 0.6 copy-done.6
  51.7 19.3 %rowgrads.1 = (f32[8,2,16,240]{3,2,1,0:T(8,128)}, f32[8,2,16,240]{3,2,1,0:T(8,128)}, f32[8,2,16,240]{3,2,1,0:T(8,128)}, f32[8,2,16,240]{3,2,1,0:T(8,128)}, f32[256,128]{1,0:T(8,128)}) custom-call(f32[8,512]{1,0:T(8,128)} %get-tuple-element.31.rows_ref, f32[512,8]{1,0:T(8,128)} %get-tuple-element.32.cols_ref, bf16[512,512]{1,0:T(8,128)(2,1)} %copy.32.vis_ref, ...), custom_call_target="tpu_custom_call" | custom-call | flops 20000000000 | bytes 10000000 | tf_op jit(solution)/shard_map/rowgrads/pallas_call | solution.py:535
  71.0 0.0 collective-permute-done.3
  71.0 0.0 collective-permute-done.4
  71.0 4.2 %all-to-all-start.2 = ((f32[32,8,128]{2,1,0:T(8,128)}), f32[32,8,128]{2,1,0:T(8,128)S(1)}, u32[]{:S(2)}, u32[]{:S(2)}) async-start(f32[32,8,128]{2,1,0:T(8,128)} %bitcast.44), calls=%async_computation.2 | async-start | bytes 262144 | tf_op jit(solution)/shard_map/all_to_all | solution.py:484
  75.3 3.7 %collective-permute-start.5 = (f32[8,2,16,240]{3,2,1,0:T(8,128)}, f32[8,2,16,240]{3,2,1,0:T(8,128)S(1)}, u32[]{:S(2)}, u32[]{:S(2)}) collective-permute-start(f32[8,2,16,240]{3,2,1,0:T(8,128)} %get-tuple-element.46), channel_id=1, source_target_pairs={{0,3},{1,0},{2,1},{3,2},{4,7},{5,4},{6,5},{7,6},{8,11},{9,8},{10,9... | collective-permute-start | bytes 737288 | tf_op jit(solution)/shard_map/ppermute | solution.py:562
  79.0 0.0 collective-permute-start.6
  79.0 1.1 %collective-permute-start.7 = (f32[8,2,16,240]{3,2,1,0:T(8,128)}, f32[8,2,16,240]{3,2,1,0:T(8,128)S(1)}, u32[]{:S(2)}, u32[]{:S(2)}) collective-permute-start(f32[8,2,16,240]{3,2,1,0:T(8,128)} %get-tuple-element.48), channel_id=1, source_target_pairs={{0,1},{1,2},{2,3},{3,0},{4,5},{5,6},{6,7},{7,4},{8,9},{9,10},{10,1... | collective-permute-start | bytes 737288 | tf_op jit(solution)/shard_map/ppermute | solution.py:562
  80.0 3.9 %all-to-all-done.2 = f32[32,8,128]{2,1,0:T(8,128)S(1)} async-done(((f32[32,8,128]{2,1,0:T(8,128)}), f32[32,8,128]{2,1,0:T(8,128)S(1)}, u32[]{:S(2)}, u32[]{:S(2)}) %all-to-all-start.2) | async-done | bytes 131104 | tf_op jit(solution)/shard_map/all_to_all | solution.py:484
  83.9 0.7 copy-done.2
  84.6 19.0 %scatter.1 = f32[16,2048,128]{2,1,0:T(8,128)} custom-call(s32[32,32]{1,0:T(8,128)} %fusion.2.base_ref, f32[256,128]{1,0:T(8,128)} %bitcast.38, f32[1024,256]{1,0:T(8,128)} %get-tuple-element.44.w_ref), custom_call_target="tpu_custom_call" | custom-call | flops 100000000 | bytes 100000000 | tf_op jit(solution)/shard_map/scatter/pallas_call | solution.py:565
  103.6 0.0 collective-permute-done.5
  103.6 0.7 collective-permute-done.6
  104.3 0.0 collective-permute-done.7
  104.3 0.0 copy-done.5
  104.3 0.2 bitcast_add_fusion
  104.6 0.9 copy.31
  (6 shorter events, 0.0 us)
Async XLA Ops:
  0.6 43.1 %copy-start = (f32[1,16,8,2,240]{4,3,2,1,0:T(2,128)S(1)}, f32[1,16,8,2,240]{4,3,2,1,0:T(2,128)}, u32[]{:S(2)}) copy-start(f32[1,16,8,2,240]{4,3,2,1,0:T(2,128)} %param.16) | copy-start | bytes 737284
  0.6 42.0 %copy-start.3 = (bf16[512,2,240]{0,2,1:T(8,128)(2,1)S(1)}, bf16[512,2,240]{0,2,1:T(8,128)(2,1)}, u32[]{:S(2)}) copy-start(bf16[512,2,240]{0,2,1:T(8,128)(2,1)} %param.9) | copy-start | bytes 1474564
  1.8 49.2 %copy-start.4 = (f32[1,16,8,2,240]{4,1,3,2,0:T(8,128)}, f32[1,16,8,2,240]{4,1,3,2,0:T(8,128)S(1)}, u32[]{:S(2)}) copy-start(f32[1,16,8,2,240]{4,1,3,2,0:T(8,128)S(1)} %copy.35) | copy-start | bytes 737284
  4.1 15.1 %all-to-all-start = ((f32[32,4,128]{2,1,0:T(4,128)}), f32[32,4,128]{2,1,0:T(4,128)S(1)}, u32[]{:S(2)}, u32[]{:S(2)}) async-start(f32[32,4,128]{2,1,0:T(4,128)} %bitcast.47), calls=%async_computation | async-start | bytes 131072 | tf_op jit(solution)/shard_map/all_to_all | solution.py:484
  11.4 21.4 %collective-permute-start = (f32[8,2,16,240]{3,2,1,0:T(8,128)S(1)}, f32[8,2,16,240]{3,2,1,0:T(8,128)S(1)}, u32[]{:S(2)}, u32[]{:S(2)}) collective-permute-start(f32[8,2,16,240]{3,2,1,0:T(8,128)S(1)} %bitcast.40), channel_id=1, source_target_pairs={{0,1},{1,2},{2,3},{3,0},{4,5},{5,6},{6,7},{7,4},{8,9},{9,10},{10,1... | collective-permute-start | bytes 737288 | tf_op jit(solution)/shard_map/ppermute | solution.py:497
  13.2 20.8 %collective-permute-start.1 = (f32[8,2,16,240]{3,2,1,0:T(8,128)S(1)}, f32[8,2,16,240]{3,2,1,0:T(8,128)S(1)}, u32[]{:S(2)}, u32[]{:S(2)}) collective-permute-start(f32[8,2,16,240]{3,2,1,0:T(8,128)S(1)} %bitcast.41), channel_id=1, source_target_pairs={{0,2},{1,3},{2,0},{3,1},{4,6},{5,7},{6,4},{7,5},{8,10},{9,11},{10,... | collective-permute-start | bytes 737288 | tf_op jit(solution)/shard_map/ppermute | solution.py:497
  15.6 18.4 %collective-permute-start.2 = (f32[8,2,16,240]{3,2,1,0:T(8,128)S(1)}, f32[8,2,16,240]{3,2,1,0:T(8,128)S(1)}, u32[]{:S(2)}, u32[]{:S(2)}) collective-permute-start(f32[8,2,16,240]{3,2,1,0:T(8,128)S(1)} %bitcast.42), channel_id=1, source_target_pairs={{0,3},{1,0},{2,1},{3,2},{4,7},{5,4},{6,5},{7,6},{8,11},{9,8},{10,9... | collective-permute-start | bytes 737288 | tf_op jit(solution)/shard_map/ppermute | solution.py:497
  19.2 0.8 copy-start.1
  32.8 18.2 %copy-start.7 = (f32[8,2,16,240]{3,2,1,0:T(8,128)}, f32[8,2,16,240]{3,2,1,0:T(8,128)S(1)}, u32[]{:S(2)}) copy-start(f32[8,2,16,240]{3,2,1,0:T(8,128)S(1)} %collective-permute-done.rest_1_) | copy-start | bytes 737284
  34.0 17.0 %copy-start.8 = (f32[8,2,16,240]{3,2,1,0:T(8,128)}, f32[8,2,16,240]{3,2,1,0:T(8,128)S(1)}, u32[]{:S(2)}) copy-start(f32[8,2,16,240]{3,2,1,0:T(8,128)S(1)} %collective-permute-done.1.rest_2_) | copy-start | bytes 737284
  34.0 17.0 %copy-start.9 = (f32[8,2,16,240]{3,2,1,0:T(8,128)}, f32[8,2,16,240]{3,2,1,0:T(8,128)S(1)}, u32[]{:S(2)}) copy-start(f32[8,2,16,240]{3,2,1,0:T(8,128)S(1)} %collective-permute-done.2.rest_3_) | copy-start | bytes 737284
  34.0 17.0 %all-to-all-start.1 = ((f32[32,8,128]{2,1,0:T(8,128)}), f32[32,8,128]{2,1,0:T(8,128)S(1)}, u32[]{:S(2)}, u32[]{:S(2)}) async-start(f32[32,8,128]{2,1,0:T(8,128)} %bitcast.46), calls=%async_computation.1 | async-start | bytes 262144 | tf_op jit(solution)/shard_map/all_to_all | solution.py:484
  43.9 27.1 %collective-permute-start.3 = (f32[1,16,8,2,240]{4,1,3,2,0:T(8,128)S(1)}, f32[1,16,8,2,240]{4,1,3,2,0:T(8,128)S(1)}, u32[]{:S(2)}, u32[]{:S(2)}) collective-permute-start(f32[1,16,8,2,240]{4,1,3,2,0:T(8,128)S(1)} %copy.26), channel_id=1, source_target_pairs={{0,4},{4,8},{8,12},{12,16},{16,20},{20,24},{24,28},{1,5},{5,9},{9,... | collective-permute-start | bytes 737288 | tf_op jit(solution)/shard_map/ppermute | solution.py:528
  46.0 25.0 %collective-permute-start.4 = (f32[1,16,8,2,240]{4,1,3,2,0:T(8,128)S(1)}, f32[1,16,8,2,240]{4,1,3,2,0:T(8,128)S(1)}, u32[]{:S(2)}, u32[]{:S(2)}) collective-permute-start(f32[1,16,8,2,240]{4,1,3,2,0:T(8,128)S(1)} %copy.26), channel_id=1, source_target_pairs={{4,0},{8,4},{12,8},{16,12},{20,16},{24,20},{28,24},{5,1},{9,5},{13... | collective-permute-start | bytes 737288 | tf_op jit(solution)/shard_map/ppermute | solution.py:529
  51.1 0.7 copy-start.6
  71.0 33.3 %copy-start.5 = (f32[8,2,16,240]{3,2,1,0:T(8,128)S(1)}, f32[8,2,16,240]{3,2,1,0:T(8,128)}, u32[]{:S(2)}) copy-start(f32[8,2,16,240]{3,2,1,0:T(8,128)} %get-tuple-element.49) | copy-start | bytes 737284
  71.0 12.9 %all-to-all-start.2 = ((f32[32,8,128]{2,1,0:T(8,128)}), f32[32,8,128]{2,1,0:T(8,128)S(1)}, u32[]{:S(2)}, u32[]{:S(2)}) async-start(f32[32,8,128]{2,1,0:T(8,128)} %bitcast.44), calls=%async_computation.2 | async-start | bytes 262144 | tf_op jit(solution)/shard_map/all_to_all | solution.py:484
  75.3 28.3 %collective-permute-start.5 = (f32[8,2,16,240]{3,2,1,0:T(8,128)}, f32[8,2,16,240]{3,2,1,0:T(8,128)S(1)}, u32[]{:S(2)}, u32[]{:S(2)}) collective-permute-start(f32[8,2,16,240]{3,2,1,0:T(8,128)} %get-tuple-element.46), channel_id=1, source_target_pairs={{0,3},{1,0},{2,1},{3,2},{4,7},{5,4},{6,5},{7,6},{8,11},{9,8},{10,9... | collective-permute-start | bytes 737288 | tf_op jit(solution)/shard_map/ppermute | solution.py:562
  79.0 25.4 %collective-permute-start.6 = (f32[8,2,16,240]{3,2,1,0:T(8,128)}, f32[8,2,16,240]{3,2,1,0:T(8,128)S(1)}, u32[]{:S(2)}, u32[]{:S(2)}) collective-permute-start(f32[8,2,16,240]{3,2,1,0:T(8,128)} %get-tuple-element.47), channel_id=1, source_target_pairs={{0,2},{1,3},{2,0},{3,1},{4,6},{5,7},{6,4},{7,5},{8,10},{9,11},{10,... | collective-permute-start | bytes 737288 | tf_op jit(solution)/shard_map/ppermute | solution.py:562
  79.0 25.4 %collective-permute-start.7 = (f32[8,2,16,240]{3,2,1,0:T(8,128)}, f32[8,2,16,240]{3,2,1,0:T(8,128)S(1)}, u32[]{:S(2)}, u32[]{:S(2)}) collective-permute-start(f32[8,2,16,240]{3,2,1,0:T(8,128)} %get-tuple-element.48), channel_id=1, source_target_pairs={{0,1},{1,2},{2,3},{3,0},{4,5},{5,6},{6,7},{7,4},{8,9},{9,10},{10,1... | collective-permute-start | bytes 737288 | tf_op jit(solution)/shard_map/ppermute | solution.py:562
  83.9 0.7 copy-start.2

commit v6 on v5

--- a/solution.py
+++ b/solution.py
@@ -16,6 +16,7 @@
 SMEM = pl.BlockSpec(memory_space=pltpu.SMEM)
 ANY = pl.BlockSpec(memory_space=pl.ANY)
 CHUNK = 16
+PAIR = 2
 
 
 def iota(shape, dim):
@@ -130,7 +131,7 @@
     ]
 
 
-def each_slot(n, visit, carry, jb):
+def each_slot(n, visit, carry, jb, group):
     per_block = LANES // n
     unroll = min(n, 32)
     for q in range(per_block):
@@ -138,8 +139,9 @@
 
         def step(g, inner):
             first = g * unroll
-            for u in range(unroll):
-                inner = visit(inner, j, first + u, u, q * n + first)
+            for u in range(0, unroll, group):
+                slots = [(j, first + v, q * n + first + v) for v in range(u, u + group)]
+                inner = visit(inner, slots)
             return inner
 
         if n == unroll:
@@ -183,16 +185,17 @@
         for copy in copies[x]:
             copy.wait()
 
-        def visit(acc, j, src, u, first):
+        def visit(acc, slots):
+            ((j, src, lane),) = slots
             w = w_s[pl.ds(j * n + src, 1), :]
             window = held[pl.ds(base_ref[j, src], 4)]
             prod = window[0:2] * w[:, :LANES] + window[2:4] * w[:, LANES:]
             return jnp.where(
-                lane3 == first + u, jnp.sum(prod, axis=2, keepdims=True), acc
+                lane3 == lane, jnp.sum(prod, axis=2, keepdims=True), acc
             )
 
         def block(jb, carry):
-            acc = each_slot(n, visit, jnp.zeros((2, facets, LANES), f32), jb)
+            acc = each_slot(n, visit, jnp.zeros((2, facets, LANES), f32), jb, 1)
             for t in range(2):
                 blocks[jb, pl.ds((2 * t + x) * facets, facets), :] = acc[t]
             return carry
@@ -218,7 +221,7 @@
     gain_refs = rest[:group_count]
     out_refs = rest[group_count : 2 * group_count]
     send_ref = rest[2 * group_count]
-    gains, spec, a_s, b_s, m_s, e_s, glr_hi, glr_lo, gm_hi, gm_lo = rest[
+    gains, spec, a_s, b_s, m_s, p_s, e_s, glr_hi, glr_lo, gm_hi, gm_lo = rest[
         2 * group_count + 1 :
     ]
     facets, _, group, channels = gain_refs[0].shape
@@ -285,19 +288,18 @@
             a_re, a_im, b_re, b_im, m_re, m_im = load(f, at)
             p_re = a_re * b_re + a_im * b_im
             p_im = a_im * b_re - a_re * b_im
+            p_s[f, at, :half] = p_re
+            p_s[f, at, half:] = p_im
             e_s[at, :half] += p_re * m_re - p_im * m_im
             e_s[at, half:] += p_re * m_im + p_im * m_re
 
     e_s[...] = -vis_ref[...].astype(f32)
     gather(0)
 
-    def forward(f, carry):
-        gather(f + 1)
+    for f in range(facets):
+        if f + 1 < facets:
+            gather(f + 1)
         predict(f)
-        return carry
-
-    lax.fori_loop(0, facets - 1, forward, 0)
-    predict(facets - 1)
     e_s[...] = e_s[...] * cols[:, 4:5]
 
     block = min(rows, 128)
@@ -317,38 +319,60 @@
 
     re_lanes, im_lanes = slice(0, half), slice(half, wide)
 
+    def vector_part(f, c, i):
+        at = pl.ds(c * block + i * CHUNK, CHUNK)
+        left = pl.ds(2 * c * block + i * CHUNK, CHUNK)
+        right = pl.ds((2 * c + 1) * block + i * CHUNK, CHUNK)
+        e_re, e_im = e_s[at, :half], e_s[at, half:]
+        a_re, a_im, b_re, b_im, m_re, m_im = load(f, at)
+        p_re, p_im = p_s[f, at, :half], p_s[f, at, half:]
+        t_re = e_re * m_re + e_im * m_im
+        t_im = e_im * m_re - e_re * m_im
+        put(glr_hi, glr_lo, left, re_lanes, t_re * b_re - t_im * b_im)
+        put(glr_hi, glr_lo, left, im_lanes, t_re * b_im + t_im * b_re)
+        put(glr_hi, glr_lo, right, re_lanes, t_re * a_re + t_im * a_im)
+        put(glr_hi, glr_lo, right, im_lanes, t_re * a_im - t_im * a_re)
+        put(gm_hi, gm_lo, at, re_lanes, e_re * p_re + e_im * p_im)
+        put(gm_hi, gm_lo, at, im_lanes, e_im * p_re - e_re * p_im)
+
+    def matmul_parts(f, c, sums, parts):
+        both = pl.ds(2 * c * block, 2 * block)
+        here = pl.ds(c * block, block)
+
+        def station(x, ref):
+            def run():
+                term = mm(to_station[c], ref[both, x * half : (x + 1) * half])
+                sums[x] = term if sums[x] is None else sums[x] + term
+
+            return run
+
+        def plane_sum(ref):
+            def run():
+                term = mm_nt(ref[here, :], spec[f, :planes, :])
+                parts[c] = term if parts[c] is None else parts[c] + term
+
+            return run
+
+        return [
+            station(0, glr_hi), station(1, glr_hi), station(0, glr_lo),
+            station(1, glr_lo), plane_sum(gm_hi), plane_sum(gm_lo),
+        ]
+
     def grads(f, grad_degrid):
-        summed = jnp.zeros((stations, wide), f32)
-        table = spec[f, :planes, :]
-        parts = []
+        sums, parts, waiting = [None, None], [None] * block_count, []
         for c in range(block_count):
             for i in range(block // CHUNK):
-                at = pl.ds(c * block + i * CHUNK, CHUNK)
-                left = pl.ds(2 * c * block + i * CHUNK, CHUNK)
-                right = pl.ds((2 * c + 1) * block + i * CHUNK, CHUNK)
-                e_re, e_im = e_s[at, :half], e_s[at, half:]
-                a_re, a_im, b_re, b_im, m_re, m_im = load(f, at)
-                t_re = e_re * m_re + e_im * m_im
-                t_im = e_im * m_re - e_re * m_im
-                p_re = a_re * b_re + a_im * b_im
-                p_im = a_im * b_re - a_re * b_im
-                put(glr_hi, glr_lo, left, re_lanes, t_re * b_re - t_im * b_im)
-                put(glr_hi, glr_lo, left, im_lanes, t_re * b_im + t_im * b_re)
-                put(glr_hi, glr_lo, right, re_lanes, t_re * a_re + t_im * a_im)
-                put(glr_hi, glr_lo, right, im_lanes, t_re * a_im - t_im * a_re)
-                put(gm_hi, gm_lo, at, re_lanes, e_re * p_re + e_im * p_im)
-                put(gm_hi, gm_lo, at, im_lanes, e_im * p_re - e_re * p_im)
-            both = pl.ds(2 * c * block, 2 * block)
-            here = pl.ds(c * block, block)
-            summed = summed + (
-                mm(to_station[c], glr_hi[both, :]) + mm(to_station[c], glr_lo[both, :])
-            )
-            parts.append(mm_nt(gm_hi[here, :], table) + mm_nt(gm_lo[here, :], table))
+                vector_part(f, c, i)
+                if waiting:
+                    waiting.pop(0)()
+            for run in waiting:
+                run()
+            waiting = matmul_parts(f, c, sums, parts)
+        for run in waiting:
+            run()
         for k in range(group_count):
             for x in range(2):
-                out_refs[k][f, x] = summed[
-                    k * group : (k + 1) * group, x * half : x * half + channels
-                ]
+                out_refs[k][f, x] = sums[x][k * group : (k + 1) * group, :channels]
         return grad_degrid + jnp.concatenate(parts, axis=0)
 
     grad_degrid = lax.fori_loop(0, facets, grads, jnp.zeros((rows, planes), f32))
@@ -403,18 +427,36 @@
                 [blocks[jb, pl.ds((2 * t + x) * facets, facets), :] for t in range(2)]
             )
 
-            def visit(inner, j, src, u, first):
-                at = pl.ds(base_ref[j, src], 4)
-                w = w_ref[pl.ds(j * n + src, 1), :]
-                value = jnp.sum(
-                    jnp.where(lane3 == first + u, values, 0.0), axis=2, keepdims=True
-                )
-                held[at] = held[at] + jnp.concatenate(
-                    [value * w[:, :LANES], value * w[:, LANES:]], axis=0
-                )
+            def visit(inner, slots):
+                starts, windows, adds = [], [], []
+                for j, src, lane in slots:
+                    starts.append(base_ref[j, src])
+                    windows.append(held[pl.ds(starts[-1], 4)])
+                for at, (j, src, lane) in enumerate(slots):
+                    w = w_ref[pl.ds(j * n + src, 1), :]
+                    low, high = w[:, :LANES], w[:, LANES:]
+                    value = jnp.sum(
+                        jnp.where(lane3 == lane, values, 0.0), axis=2, keepdims=True
+                    )
+                    window = windows[at] + jnp.concatenate(
+                        [value * low, value * high], axis=0
+                    )
+                    for start, early_value, early_low, early_high in adds:
+                        same = jnp.where(start == starts[at], 1.0, 0.0)
+                        after = jnp.where(start + 2 == starts[at], 1.0, 0.0)
+                        before = jnp.where(start == starts[at] + 2, 1.0, 0.0)
+                        shared_low = early_low * same + early_high * after
+                        shared_high = early_high * same + early_low * before
+                        window = window + jnp.concatenate(
+                            [early_value * shared_low, early_value * shared_high], axis=0
+                        )
+                    windows[at] = window
+                    adds.append((starts[at], value, low, high))
+                for start, window in zip(starts, windows):
+                    held[pl.ds(start, 4)] = window
                 return inner
 
-            return each_slot(n, visit, carry, jb)
+            return each_slot(n, visit, carry, jb, PAIR)
 
         lax.fori_loop(0, block_count, block, 0)
         for f in range(facets):
@@ -489,15 +531,20 @@
         .transpose(0, 2, 1, 3)
         .reshape(pairs, terms * tiles, LANES)
     )
-    send, gain_turned = lax.optimization_barrier((send, gain_turned))
+    def turn_gains(x, k):
+        return lax.ppermute(
+            x, "bl", [(i, (i + k) % group_count) for i in range(group_count)]
+        )
+
+    near = range(1, group_count // 2 + 1)
+    far = range(group_count // 2 + 1, group_count)
+    send, gain_turned, gain_here = lax.optimization_barrier(
+        (send, gain_turned, gain_field)
+    )
     received = exchange(send)
-    gathered = [gain_turned]
-    for k in range(1, group_count):
-        gathered.append(
-            lax.ppermute(
-                gain_turned, "bl", [(i, (i + k) % group_count) for i in range(group_count)]
-            )
-        )
+    early = [turn_gains(gain_turned, k) for k in near]
+    early.append(lax.ppermute(gain_here, "tm", [(i, i + 1) for i in range(time_count - 1)]))
+    early.append(lax.ppermute(gain_here, "tm", [(i + 1, i) for i in range(time_count - 1)]))
     base = received.reshape(n, lines * LANES)[:, (taps + 1) * cap : (taps + 2) * cap]
     base = jnp.clip(base.T.astype(i32), 0, tiles - 2) * terms
     slot_lines = n * cap * planes // LANES
@@ -522,11 +569,10 @@
         cost_estimate=cost(10**8, 7 * 10**7),
         name="degrid",
     )(base, received, sky)
-    values, *gathered = lax.optimization_barrier((values, *gathered))
-    values, gain_here = lax.optimization_barrier((values, gain_field))
+    values, gain_turned, *early = lax.optimization_barrier((values, gain_turned, *early))
+    *early, below, above = early
     back = exchange(values)
-    below = lax.ppermute(gain_here, "tm", [(i, i + 1) for i in range(time_count - 1)])
-    above = lax.ppermute(gain_here, "tm", [(i + 1, i) for i in range(time_count - 1)])
+    gathered = [gain_turned, *early, *(turn_gains(gain_turned, k) for k in far)]
 
     vis_wide = jnp.pad(visibilities, ((0, 0), (0, 0), (0, half - channels))).reshape(
         rows, wide
@@ -544,6 +590,7 @@
             pltpu.VMEM((facets, rows, wide), f32),
             pltpu.VMEM((facets, rows, wide), f32),
             pltpu.VMEM((facets, rows, wide), f32),
+            pltpu.VMEM((facets, rows, wide), f32),
             pltpu.VMEM((rows, wide), f32),
             pltpu.VMEM((2 * rows, wide), bf16),
             pltpu.VMEM((2 * rows, wide), bf16),
@@ -556,7 +603,6 @@
     )(row_table, col_table, vis_wide, back, *gathered)
 
     *parts, send_grad = outs
-    send_grad, below, above = lax.optimization_barrier((send_grad, below, above))
     got = exchange(send_grad)
     for k in range(1, group_count):
         parts[k] = lax.ppermute(

time: 107 us -> 104 us (0.972)
  Pallas kernels: 53.4 us -> 48.4 us
  waiting for transfers between devices: 11.7 us -> 13.7 us
    all_to_all x3, waiting for transfers between devices: 9.75 us -> 3.87 us  [exchange(): x = lax.all_to_all(x, both, split_axis=0, concat_axis=0, tiled=True)]
    ppermute x3, waiting for transfers between devices: 1.21 us -> 6.49 us  [turn_gains(): lax.ppermute(x, 'bl', [(i, (i + k) % group_count) for i in range(group_co...]
    pallas_call x1, Pallas kernels: 19 us -> 16.4 us  [body(): pl.pallas_call(functools.partial(scatter_kernel, n, cap), out_shape=jax.S...]
    ppermute x3, waiting for transfers between devices: 0.75 us -> 3.33 us  [body(): lax.ppermute(parts[k], 'bl', [(i, (i - k) % group_count) for i in range(g...]
    pallas_call x1, Pallas kernels: 19.3 us -> 16.9 us  [body(): pl.pallas_call(functools.partial(rows_kernel, n, cap, group_count), out_s...]
    ppermute x3, starting transfers between devices: 5.65 us -> 7.91 us  [turn_gains(): lax.ppermute(x, 'bl', [(i, (i + k) % group_count) for i in range(group_co...]
    all_to_all x3, starting transfers between devices: 20.2 us -> 18.5 us  [exchange(): x = lax.all_to_all(x, both, split_axis=0, concat_axis=0, tiled=True)]
  transfers between devices with their start and end apart: 11 -> 11, of which waited for: 5 -> 4; matrix products, arithmetic and copies ran while one was open for 2% -> 3% of each run, Pallas kernels for 48% -> 28%
where the time goes in v6:
time: 104 us; the launch traced here: 103 us
  Pallas kernels  48.4 us (47%)
  starting transfers between devices  34 us (33%)
  waiting for transfers between devices  13.7 us (13%)
  local copies, waits for them, and re-layouts  5.75 us (6%)
    all_to_all x3, starting transfers between devices, exchange(): x = lax.all_to_all(x, both, split_axis=0, concat_axis=0, tiled=True)  18.5 us
    pallas_call x1, Pallas kernels, body(): pl.pallas_call(functools.partial(rows_kernel, n, cap, group_count), out_s...  16.9 us
    pallas_call x1, Pallas kernels, body(): pl.pallas_call(functools.partial(scatter_kernel, n, cap), out_shape=jax.S...  16.4 us
    pallas_call x1, Pallas kernels, body(): pl.pallas_call(functools.partial(degrid_kernel, n, cap, taps), out_shape=...  12.8 us
    ppermute x3, starting transfers between devices, turn_gains(): lax.ppermute(x, 'bl', [(i, (i + k) % group_count) for i in range(group_co...  7.91 us
    ppermute x3, waiting for transfers between devices, turn_gains(): lax.ppermute(x, 'bl', [(i, (i + k) % group_count) for i in range(group_co...  6.49 us
    ppermute x3, starting transfers between devices, body(): lax.ppermute(parts[k], 'bl', [(i, (i - k) % group_count) for i in range(g...  4.75 us
    all_to_all x3, waiting for transfers between devices, exchange(): x = lax.all_to_all(x, both, split_axis=0, concat_axis=0, tiled=True)  3.87 us
  transfers between devices with their start and end apart: 11, of which 4 were waited for; matrix products, arithmetic and copies ran while one was open for 3% of the time, Pallas kernels for 28%

profile of v6, /device:TPU:0, one launch (start us, length us, event | category | flops | bytes accessed | tf_op | source)
XLA Modules:
  0.0 103.5 jit_solution(1220079099819917352)
XLA Ops:
  0.6 0.0 copy-start.3
  0.6 1.2 %copy.35 = f32[1,16,8,2,240]{4,1,3,2,0:T(8,128)S(1)} copy(f32[1,16,8,2,240]{4,3,2,1,0:T(2,128)} %param.16) | data formatting | bytes 491520 | tf_op args[7]
  1.8 0.0 copy-start.4
  1.8 2.2 %slots.1 = (f32[128,128]{1,0:T(8,128)}, f32[8,512]{1,0:T(8,128)}, f32[512,8]{1,0:T(8,128)}) custom-call(s32[1]{0:T(128)} %bitcast.shift_ref, s32[1,512]{1,0:T(1,128)} %bitcast.48, s32[1,512]{1,0:T(1,128)} %bitcast.49, f32[8,512]{1,0:T(8,128)} %taps_ref.1, s32[2,512]{1,0:T(2,128)} %pairs_ref.1, f32[1,512]{1,0:T(1,128)} %bitcast.50, s32[1,512]{1,0:T(1,128)} %bitcast.51), custom_call_target="tpu_custom_call" | custom-call | flops 1000000000 | bytes 1000000 | tf_op jit(solution)/shard_map/slots/pallas_call | solution.py:502
  4.0 7.3 %all-to-all-start = ((f32[32,4,128]{2,1,0:T(4,128)}), f32[32,4,128]{2,1,0:T(4,128)S(1)}, u32[]{:S(2)}, u32[]{:S(2)}) async-start(f32[32,4,128]{2,1,0:T(4,128)} %bitcast.47), calls=%async_computation | async-start | bytes 131072 | tf_op jit(solution)/shard_map/all_to_all | solution.py:526
  11.3 1.8 %collective-permute-start = (f32[8,2,16,240]{3,2,1,0:T(8,128)S(1)}, f32[8,2,16,240]{3,2,1,0:T(8,128)S(1)}, u32[]{:S(2)}, u32[]{:S(2)}) collective-permute-start(f32[8,2,16,240]{3,2,1,0:T(8,128)S(1)} %bitcast.40), channel_id=1, source_target_pairs={{0,1},{1,2},{2,3},{3,0},{4,5},{5,6},{6,7},{7,4},{8,9},{9,10},{10,1... | collective-permute-start | bytes 737288 | tf_op jit(solution)/shard_map/ppermute | solution.py:535
  13.2 2.4 %collective-permute-start.1 = (f32[8,2,16,240]{3,2,1,0:T(8,128)S(1)}, f32[8,2,16,240]{3,2,1,0:T(8,128)S(1)}, u32[]{:S(2)}, u32[]{:S(2)}) collective-permute-start(f32[8,2,16,240]{3,2,1,0:T(8,128)S(1)} %bitcast.41), channel_id=1, source_target_pairs={{0,2},{1,3},{2,0},{3,1},{4,6},{5,7},{6,4},{7,5},{8,10},{9,11},{10,... | collective-permute-start | bytes 737288 | tf_op jit(solution)/shard_map/ppermute | solution.py:535
  15.6 1.1 %copy.26 = f32[1,16,8,2,240]{4,1,3,2,0:T(8,128)S(1)} copy(f32[1,16,8,2,240]{4,3,2,1,0:T(2,128)} %param.16) | data formatting | bytes 491520 | tf_op jit(solution)/shard_map/optimization_barrier | solution.py:541
  16.7 1.5 %collective-permute-start.2 = (f32[1,16,8,2,240]{4,1,3,2,0:T(8,128)S(1)}, f32[1,16,8,2,240]{4,1,3,2,0:T(8,128)S(1)}, u32[]{:S(2)}, u32[]{:S(2)}) collective-permute-start(f32[1,16,8,2,240]{4,1,3,2,0:T(8,128)S(1)} %copy.26), channel_id=1, source_target_pairs={{0,4},{4,8},{8,12},{12,16},{16,20},{20,24},{24,28},{1,5},{5,9},{9,... | collective-permute-start | bytes 737288 | tf_op jit(solution)/shard_map/ppermute | solution.py:546
  18.2 1.3 %collective-permute-start.3 = (f32[1,16,8,2,240]{4,1,3,2,0:T(8,128)S(1)}, f32[1,16,8,2,240]{4,1,3,2,0:T(8,128)S(1)}, u32[]{:S(2)}, u32[]{:S(2)}) collective-permute-start(f32[1,16,8,2,240]{4,1,3,2,0:T(8,128)S(1)} %copy.26), channel_id=1, source_target_pairs={{4,0},{8,4},{12,8},{16,12},{20,16},{24,20},{28,24},{5,1},{9,5},{13... | collective-permute-start | bytes 737288 | tf_op jit(solution)/shard_map/ppermute | solution.py:547
  19.5 0.0 all-to-all-done
  19.5 0.0 copy-start.1
  19.5 0.1 copy.23
  19.7 0.6 fusion.2.base_ref
  20.3 0.0 copy-done.1
  20.3 12.8 %degrid.1 = (f32[256,128]{1,0:T(8,128)}, f32[1024,256]{1,0:T(8,128)}) custom-call(s32[32,32]{1,0:T(8,128)} %fusion.2.base_ref, f32[128,128]{1,0:T(8,128)} %bitcast.37, f32[16,2048,128]{2,1,0:T(8,128)} %bitcast.35), custom_call_target="tpu_custom_call" | custom-call | flops 100000000 | bytes 70000000 | tf_op jit(solution)/shard_map/degrid/pallas_call | solution.py:552
  33.1 0.0 collective-permute-done.rest_1_
  33.1 0.0 copy-start.7
  33.1 0.6 collective-permute-done.1.rest_2_
  33.8 0.0 copy-start.8
  33.8 0.0 collective-permute-done.2
  33.8 0.0 collective-permute-done.3
  33.8 5.8 %all-to-all-start.1 = ((f32[32,8,128]{2,1,0:T(8,128)}), f32[32,8,128]{2,1,0:T(8,128)S(1)}, u32[]{:S(2)}, u32[]{:S(2)}) async-start(f32[32,8,128]{2,1,0:T(8,128)} %bitcast.45), calls=%async_computation.1 | async-start | bytes 262144 | tf_op jit(solution)/shard_map/all_to_all | solution.py:526
  39.6 3.7 %collective-permute-start.4 = (f32[8,2,16,240]{3,2,1,0:T(8,128)S(1)}, f32[8,2,16,240]{3,2,1,0:T(8,128)S(1)}, u32[]{:S(2)}, u32[]{:S(2)}) collective-permute-start(f32[8,2,16,240]{3,2,1,0:T(8,128)S(1)} %bitcast.42), channel_id=1, source_target_pairs={{0,3},{1,0},{2,1},{3,2},{4,7},{5,4},{6,5},{7,6},{8,11},{9,8},{10,9... | collective-permute-start | bytes 737288 | tf_op jit(solution)/shard_map/ppermute | solution.py:535
  43.2 0.0 copy-done.3
  43.3 1.0 copy.32.vis_ref
  44.3 5.9 %collective-permute-done.4.rest_3_ = f32[8,2,16,240]{3,2,1,0:T(8,128)S(1)} collective-permute-done((f32[8,2,16,240]{3,2,1,0:T(8,128)S(1)}, f32[8,2,16,240]{3,2,1,0:T(8,128)S(1)}, u32[]{:S(2)}, u32[]{:S(2)}) %collective-permute-start.4) | collective-permute-done | bytes 245792 | tf_op jit(solution)/shard_map/ppermute | solution.py:535
  50.2 0.0 all-to-all-done.1
  50.2 0.0 copy-done.4
  50.2 0.0 copy-done.7
  50.2 0.0 copy-done.8
  50.2 0.7 copy-done.9
  50.9 0.1 copy-done.6
  50.9 16.9 %rowgrads.1 = (f32[8,2,16,240]{3,2,1,0:T(8,128)}, f32[8,2,16,240]{3,2,1,0:T(8,128)}, f32[8,2,16,240]{3,2,1,0:T(8,128)}, f32[8,2,16,240]{3,2,1,0:T(8,128)}, f32[256,128]{1,0:T(8,128)}) custom-call(f32[8,512]{1,0:T(8,128)} %get-tuple-element.28.rows_ref, f32[512,8]{1,0:T(8,128)} %get-tuple-element.29.cols_ref, bf16[512,512]{1,0:T(8,128)(2,1)} %copy.32.vis_ref, ...), custom_call_target="tpu_custom_call" | custom-call | flops 20000000000 | bytes 10000000 | tf_op jit(solution)/shard_map/rowgrads/pallas_call | solution.py:581
  67.8 5.5 %all-to-all-start.2 = ((f32[32,8,128]{2,1,0:T(8,128)}), f32[32,8,128]{2,1,0:T(8,128)S(1)}, u32[]{:S(2)}, u32[]{:S(2)}) async-start(f32[32,8,128]{2,1,0:T(8,128)} %bitcast.44), calls=%async_computation.2 | async-start | bytes 262144 | tf_op jit(solution)/shard_map/all_to_all | solution.py:526
  73.3 3.7 %collective-permute-start.5 = (f32[8,2,16,240]{3,2,1,0:T(8,128)}, f32[8,2,16,240]{3,2,1,0:T(8,128)S(1)}, u32[]{:S(2)}, u32[]{:S(2)}) collective-permute-start(f32[8,2,16,240]{3,2,1,0:T(8,128)} %get-tuple-element.40), channel_id=1, source_target_pairs={{0,3},{1,0},{2,1},{3,2},{4,7},{5,4},{6,5},{7,6},{8,11},{9,8},{10,9... | collective-permute-start | bytes 737288 | tf_op jit(solution)/shard_map/ppermute | solution.py:608
  76.9 0.0 collective-permute-start.6
  76.9 1.1 %collective-permute-start.7 = (f32[8,2,16,240]{3,2,1,0:T(8,128)}, f32[8,2,16,240]{3,2,1,0:T(8,128)S(1)}, u32[]{:S(2)}, u32[]{:S(2)}) collective-permute-start(f32[8,2,16,240]{3,2,1,0:T(8,128)} %get-tuple-element.42), channel_id=1, source_target_pairs={{0,1},{1,2},{2,3},{3,0},{4,5},{5,6},{6,7},{7,4},{8,9},{9,10},{10,1... | collective-permute-start | bytes 737288 | tf_op jit(solution)/shard_map/ppermute | solution.py:608
  78.0 3.9 %all-to-all-done.2 = f32[32,8,128]{2,1,0:T(8,128)S(1)} async-done(((f32[32,8,128]{2,1,0:T(8,128)}), f32[32,8,128]{2,1,0:T(8,128)S(1)}, u32[]{:S(2)}, u32[]{:S(2)}) %all-to-all-start.2) | async-done | bytes 131104 | tf_op jit(solution)/shard_map/all_to_all | solution.py:526
  81.9 0.7 copy-done.2
  82.6 16.4 %scatter.1 = f32[16,2048,128]{2,1,0:T(8,128)} custom-call(s32[32,32]{1,0:T(8,128)} %fusion.2.base_ref, f32[256,128]{1,0:T(8,128)} %bitcast.38, f32[1024,256]{1,0:T(8,128)} %get-tuple-element.38.w_ref), custom_call_target="tpu_custom_call" | custom-call | flops 100000000 | bytes 100000000 | tf_op jit(solution)/shard_map/scatter/pallas_call | solution.py:611
  99.0 0.0 collective-permute-done.5
  99.0 3.3 %collective-permute-done.6 = f32[8,2,16,240]{3,2,1,0:T(8,128)S(1)} collective-permute-done((f32[8,2,16,240]{3,2,1,0:T(8,128)}, f32[8,2,16,240]{3,2,1,0:T(8,128)S(1)}, u32[]{:S(2)}, u32[]{:S(2)}) %collective-permute-start.6) | collective-permute-done | bytes 245792 | tf_op jit(solution)/shard_map/ppermute | solution.py:608
  102.3 0.0 collective-permute-done.7
  102.3 0.0 copy-done
  102.3 0.0 copy-done.5
  102.3 0.2 bitcast_add_fusion
  102.6 0.9 copy.31
  (6 shorter events, 0.0 us)
Async XLA Ops:
  0.6 42.6 %copy-start.3 = (bf16[512,2,240]{0,2,1:T(8,128)(2,1)S(1)}, bf16[512,2,240]{0,2,1:T(8,128)(2,1)}, u32[]{:S(2)}) copy-start(bf16[512,2,240]{0,2,1:T(8,128)(2,1)} %param.9) | copy-start | bytes 1474564
  1.8 48.4 %copy-start.4 = (f32[1,16,8,2,240]{4,1,3,2,0:T(8,128)}, f32[1,16,8,2,240]{4,1,3,2,0:T(8,128)S(1)}, u32[]{:S(2)}) copy-start(f32[1,16,8,2,240]{4,1,3,2,0:T(8,128)S(1)} %copy.35) | copy-start | bytes 737284
  4.0 15.5 %all-to-all-start = ((f32[32,4,128]{2,1,0:T(4,128)}), f32[32,4,128]{2,1,0:T(4,128)S(1)}, u32[]{:S(2)}, u32[]{:S(2)}) async-start(f32[32,4,128]{2,1,0:T(4,128)} %bitcast.47), calls=%async_computation | async-start | bytes 131072 | tf_op jit(solution)/shard_map/all_to_all | solution.py:526
  11.3 21.8 %collective-permute-start = (f32[8,2,16,240]{3,2,1,0:T(8,128)S(1)}, f32[8,2,16,240]{3,2,1,0:T(8,128)S(1)}, u32[]{:S(2)}, u32[]{:S(2)}) collective-permute-start(f32[8,2,16,240]{3,2,1,0:T(8,128)S(1)} %bitcast.40), channel_id=1, source_target_pairs={{0,1},{1,2},{2,3},{3,0},{4,5},{5,6},{6,7},{7,4},{8,9},{9,10},{10,1... | collective-permute-start | bytes 737288 | tf_op jit(solution)/shard_map/ppermute | solution.py:535
  13.2 20.6 %collective-permute-start.1 = (f32[8,2,16,240]{3,2,1,0:T(8,128)S(1)}, f32[8,2,16,240]{3,2,1,0:T(8,128)S(1)}, u32[]{:S(2)}, u32[]{:S(2)}) collective-permute-start(f32[8,2,16,240]{3,2,1,0:T(8,128)S(1)} %bitcast.41), channel_id=1, source_target_pairs={{0,2},{1,3},{2,0},{3,1},{4,6},{5,7},{6,4},{7,5},{8,10},{9,11},{10,... | collective-permute-start | bytes 737288 | tf_op jit(solution)/shard_map/ppermute | solution.py:535
  16.7 17.1 %collective-permute-start.2 = (f32[1,16,8,2,240]{4,1,3,2,0:T(8,128)S(1)}, f32[1,16,8,2,240]{4,1,3,2,0:T(8,128)S(1)}, u32[]{:S(2)}, u32[]{:S(2)}) collective-permute-start(f32[1,16,8,2,240]{4,1,3,2,0:T(8,128)S(1)} %copy.26), channel_id=1, source_target_pairs={{0,4},{4,8},{8,12},{12,16},{16,20},{20,24},{24,28},{1,5},{5,9},{9,... | collective-permute-start | bytes 737288 | tf_op jit(solution)/shard_map/ppermute | solution.py:546
  18.2 15.6 %collective-permute-start.3 = (f32[1,16,8,2,240]{4,1,3,2,0:T(8,128)S(1)}, f32[1,16,8,2,240]{4,1,3,2,0:T(8,128)S(1)}, u32[]{:S(2)}, u32[]{:S(2)}) collective-permute-start(f32[1,16,8,2,240]{4,1,3,2,0:T(8,128)S(1)} %copy.26), channel_id=1, source_target_pairs={{4,0},{8,4},{12,8},{16,12},{20,16},{24,20},{28,24},{5,1},{9,5},{13... | collective-permute-start | bytes 737288 | tf_op jit(solution)/shard_map/ppermute | solution.py:547
  19.5 0.8 copy-start.1
  33.1 17.0 %copy-start.7 = (f32[8,2,16,240]{3,2,1,0:T(8,128)}, f32[8,2,16,240]{3,2,1,0:T(8,128)S(1)}, u32[]{:S(2)}) copy-start(f32[8,2,16,240]{3,2,1,0:T(8,128)S(1)} %collective-permute-done.rest_1_) | copy-start | bytes 737284
  33.8 16.4 %copy-start.8 = (f32[8,2,16,240]{3,2,1,0:T(8,128)}, f32[8,2,16,240]{3,2,1,0:T(8,128)S(1)}, u32[]{:S(2)}) copy-start(f32[8,2,16,240]{3,2,1,0:T(8,128)S(1)} %collective-permute-done.1.rest_2_) | copy-start | bytes 737284
  33.8 16.4 %all-to-all-start.1 = ((f32[32,8,128]{2,1,0:T(8,128)}), f32[32,8,128]{2,1,0:T(8,128)S(1)}, u32[]{:S(2)}, u32[]{:S(2)}) async-start(f32[32,8,128]{2,1,0:T(8,128)} %bitcast.45), calls=%async_computation.1 | async-start | bytes 262144 | tf_op jit(solution)/shard_map/all_to_all | solution.py:526
  39.6 10.6 %collective-permute-start.4 = (f32[8,2,16,240]{3,2,1,0:T(8,128)S(1)}, f32[8,2,16,240]{3,2,1,0:T(8,128)S(1)}, u32[]{:S(2)}, u32[]{:S(2)}) collective-permute-start(f32[8,2,16,240]{3,2,1,0:T(8,128)S(1)} %bitcast.42), channel_id=1, source_target_pairs={{0,3},{1,0},{2,1},{3,2},{4,7},{5,4},{6,5},{7,6},{8,11},{9,8},{10,9... | collective-permute-start | bytes 737288 | tf_op jit(solution)/shard_map/ppermute | solution.py:535
  50.2 0.7 copy-start.9
  50.2 0.7 copy-start.6
  67.8 34.5 %copy-start = (f32[1,16,8,2,240]{4,3,2,1,0:T(2,128)S(1)}, f32[1,16,8,2,240]{4,3,2,1,0:T(2,128)}, u32[]{:S(2)}) copy-start(f32[1,16,8,2,240]{4,3,2,1,0:T(2,128)} %param.16) | copy-start | bytes 737284
  67.8 34.5 %copy-start.5 = (f32[8,2,16,240]{3,2,1,0:T(8,128)S(1)}, f32[8,2,16,240]{3,2,1,0:T(8,128)}, u32[]{:S(2)}) copy-start(f32[8,2,16,240]{3,2,1,0:T(8,128)} %get-tuple-element.43) | copy-start | bytes 737284
  67.8 14.1 %all-to-all-start.2 = ((f32[32,8,128]{2,1,0:T(8,128)}), f32[32,8,128]{2,1,0:T(8,128)S(1)}, u32[]{:S(2)}, u32[]{:S(2)}) async-start(f32[32,8,128]{2,1,0:T(8,128)} %bitcast.44), calls=%async_computation.2 | async-start | bytes 262144 | tf_op jit(solution)/shard_map/all_to_all | solution.py:526
  73.3 25.7 %collective-permute-start.5 = (f32[8,2,16,240]{3,2,1,0:T(8,128)}, f32[8,2,16,240]{3,2,1,0:T(8,128)S(1)}, u32[]{:S(2)}, u32[]{:S(2)}) collective-permute-start(f32[8,2,16,240]{3,2,1,0:T(8,128)} %get-tuple-element.40), channel_id=1, source_target_pairs={{0,3},{1,0},{2,1},{3,2},{4,7},{5,4},{6,5},{7,6},{8,11},{9,8},{10,9... | collective-permute-start | bytes 737288 | tf_op jit(solution)/shard_map/ppermute | solution.py:608
  76.9 25.4 %collective-permute-start.6 = (f32[8,2,16,240]{3,2,1,0:T(8,128)}, f32[8,2,16,240]{3,2,1,0:T(8,128)S(1)}, u32[]{:S(2)}, u32[]{:S(2)}) collective-permute-start(f32[8,2,16,240]{3,2,1,0:T(8,128)} %get-tuple-element.41), channel_id=1, source_target_pairs={{0,2},{1,3},{2,0},{3,1},{4,6},{5,7},{6,4},{7,5},{8,10},{9,11},{10,... | collective-permute-start | bytes 737288 | tf_op jit(solution)/shard_map/ppermute | solution.py:608
  76.9 25.4 %collective-permute-start.7 = (f32[8,2,16,240]{3,2,1,0:T(8,128)}, f32[8,2,16,240]{3,2,1,0:T(8,128)S(1)}, u32[]{:S(2)}, u32[]{:S(2)}) collective-permute-start(f32[8,2,16,240]{3,2,1,0:T(8,128)} %get-tuple-element.42), channel_id=1, source_target_pairs={{0,1},{1,2},{2,3},{3,0},{4,5},{5,6},{6,7},{7,4},{8,9},{9,10},{10,1... | collective-permute-start | bytes 737288 | tf_op jit(solution)/shard_map/ppermute | solution.py:608
  81.9 0.7 copy-start.2

commit v7 on v6

--- a/solution.py
+++ b/solution.py
@@ -184,10 +184,11 @@
     for x, held in enumerate(halves):
         for copy in copies[x]:
             copy.wait()
+        rows_of = []
 
         def visit(acc, slots):
             ((j, src, lane),) = slots
-            w = w_s[pl.ds(j * n + src, 1), :]
+            w = rows_of[0][pl.ds(lane, 1), :]
             window = held[pl.ds(base_ref[j, src], 4)]
             prod = window[0:2] * w[:, :LANES] + window[2:4] * w[:, LANES:]
             return jnp.where(
@@ -195,6 +196,7 @@
             )
 
         def block(jb, carry):
+            rows_of[:] = [w_s.at[pl.ds(pl.multiple_of(jb * LANES, LANES), LANES), :]]
             acc = each_slot(n, visit, jnp.zeros((2, facets, LANES), f32), jb, 1)
             for t in range(2):
                 blocks[jb, pl.ds((2 * t + x) * facets, facets), :] = acc[t]
@@ -423,6 +425,7 @@
     for x, held in enumerate(halves):
 
         def block(jb, carry):
+            w_rows = w_ref.at[pl.ds(pl.multiple_of(jb * LANES, LANES), LANES), :]
             values = jnp.stack(
                 [blocks[jb, pl.ds((2 * t + x) * facets, facets), :] for t in range(2)]
             )
@@ -433,7 +436,7 @@
                     starts.append(base_ref[j, src])
                     windows.append(held[pl.ds(starts[-1], 4)])
                 for at, (j, src, lane) in enumerate(slots):
-                    w = w_ref[pl.ds(j * n + src, 1), :]
+                    w = w_rows[pl.ds(lane, 1), :]
                     low, high = w[:, :LANES], w[:, LANES:]
                     value = jnp.sum(
                         jnp.where(lane3 == lane, values, 0.0), axis=2, keepdims=True
@@ -536,15 +539,9 @@
             x, "bl", [(i, (i + k) % group_count) for i in range(group_count)]
         )
 
-    near = range(1, group_count // 2 + 1)
-    far = range(group_count // 2 + 1, group_count)
-    send, gain_turned, gain_here = lax.optimization_barrier(
-        (send, gain_turned, gain_field)
-    )
+    send, gain_first = lax.optimization_barrier((send, gain_turned))
     received = exchange(send)
-    early = [turn_gains(gain_turned, k) for k in near]
-    early.append(lax.ppermute(gain_here, "tm", [(i, i + 1) for i in range(time_count - 1)]))
-    early.append(lax.ppermute(gain_here, "tm", [(i + 1, i) for i in range(time_count - 1)]))
+    gathered = [turn_gains(gain_first, k) for k in range(1, group_count)]
     base = received.reshape(n, lines * LANES)[:, (taps + 1) * cap : (taps + 2) * cap]
     base = jnp.clip(base.T.astype(i32), 0, tiles - 2) * terms
     slot_lines = n * cap * planes // LANES
@@ -569,10 +566,11 @@
         cost_estimate=cost(10**8, 7 * 10**7),
         name="degrid",
     )(base, received, sky)
-    values, gain_turned, *early = lax.optimization_barrier((values, gain_turned, *early))
-    *early, below, above = early
+    values, gain_here = lax.optimization_barrier((values, gain_turned))
     back = exchange(values)
-    gathered = [gain_turned, *early, *(turn_gains(gain_turned, k) for k in far)]
+    below = lax.ppermute(gain_here, "tm", [(i, i + 1) for i in range(time_count - 1)])
+    above = lax.ppermute(gain_here, "tm", [(i + 1, i) for i in range(time_count - 1)])
+    visibilities, *gathered = lax.optimization_barrier((visibilities, *gathered))
 
     vis_wide = jnp.pad(visibilities, ((0, 0), (0, 0), (0, half - channels))).reshape(
         rows, wide
@@ -597,17 +595,18 @@
             pltpu.VMEM((rows, wide), bf16),
             pltpu.VMEM((rows, wide), bf16),
         ],
-        compiler_params=params(),
+        compiler_params=params(52),
         cost_estimate=cost(2 * 10**10, 10**7),
         name="rowgrads",
-    )(row_table, col_table, vis_wide, back, *gathered)
-
-    *parts, send_grad = outs
-    got = exchange(send_grad)
-    for k in range(1, group_count):
-        parts[k] = lax.ppermute(
-            parts[k], "bl", [(i, (i - k) % group_count) for i in range(group_count)]
-        )
+    )(row_table, col_table, vis_wide, back, gain_turned, *gathered)
+
+    own, *parts, send_grad = outs
+    when = lax.axis_index("tm")
+    prior = jnp.where(when > 0, gain_turned - below, 0.0)
+    prior = prior - jnp.where(when < time_count - 1, above - gain_turned, 0.0)
+    own = own + smoothness * prior
+    got, own = lax.optimization_barrier((exchange(send_grad), own))
+    parts = [turn_gains(part, -k) for k, part in enumerate(parts, 1)]
     grid = pl.pallas_call(
         functools.partial(scatter_kernel, n, cap),
         out_shape=jax.ShapeDtypeStruct((pairs, terms * tiles, LANES), f32),
@@ -619,23 +618,19 @@
             pltpu.VMEM((block_count, planes, LANES), f32),
             pltpu.SemaphoreType.DMA((pairs,)),
         ],
-        compiler_params=params(),
-        cost_estimate=cost(10**8, 10**8),
+        compiler_params=params(40),
+        cost_estimate=cost(0, 10**5),
         name="scatter",
     )(base, got, weights)
     grid, *parts = lax.optimization_barrier((grid, *parts))
-    total = parts[0]
-    for part in parts[1:]:
-        total = total + part
+    for part in parts:
+        own = own + part
     grid_gradient = (
         grid.reshape(pairs, tiles, terms, LANES)
         .transpose(0, 2, 1, 3)
         .reshape(sky_grid.shape)
     )
-    when = lax.axis_index("tm")
-    prior = jnp.where(when > 0, gain_field - below, 0.0)
-    prior = prior - jnp.where(when < time_count - 1, above - gain_field, 0.0)
-    gain_gradient = total.transpose(2, 0, 1, 3)[None] + smoothness * prior
+    gain_gradient = own.transpose(2, 0, 1, 3)[None]
     return (gain_gradient, grid_gradient)
 
 

time: 104 us -> 115 us (1.11)
  blocking collectives: 0 us -> 14.8 us
  starting transfers between devices: 34 us -> 19.9 us
  waiting for transfers between devices: 13.7 us -> 26.7 us
  local copies, waits for them, and re-layouts: 5.75 us -> 3.29 us
  Pallas kernels: 48.4 us -> 46.1 us
  other arithmetic: 0.86 us -> 2.87 us
    ppermute x3 -> x6, waiting for transfers between devices: 6.49 us -> 24 us  [turn_gains(): lax.ppermute(x, 'bl', [(i, (i + k) % group_count) for i in range(group_co...]
    all_to_all x0 -> x1, blocking collectives: none -> 14.8 us  [exchange(): x = lax.all_to_all(x, both, split_axis=0, concat_axis=0, tiled=True)]
    all_to_all x3 -> x2, starting transfers between devices: 18.5 us -> 5.36 us  [exchange(): x = lax.all_to_all(x, both, split_axis=0, concat_axis=0, tiled=True)]
    ppermute x3 -> x0, starting transfers between devices: 4.75 us -> none  [body(): lax.ppermute(parts[k], 'bl', [(i, (i - k) % group_count) for i in range(g...]
    ppermute x3 -> x0, waiting for transfers between devices: 3.33 us -> none  [body(): lax.ppermute(parts[k], 'bl', [(i, (i - k) % group_count) for i in range(g...]
    ppermute x1, starting transfers between devices: 1.51 us -> 3.74 us  [body(): lax.ppermute(gain_here, 'tm', [(i, i + 1) for i in range(time_count - 1)])]
    ppermute x3 -> x6, starting transfers between devices: 7.91 us -> 9.48 us  [turn_gains(): lax.ppermute(x, 'bl', [(i, (i + k) % group_count) for i in range(group_co...]
    unnamed x22 -> x20, local copies, waits for them, and re-layouts: 3.48 us -> 2.11 us
  transfers between devices with their start and end apart: 11 -> 10, of which waited for: 4 -> 4; matrix products, arithmetic and copies ran while one was open for 3% -> 2% of each run, Pallas kernels for 28% -> 28%
where the time goes in v7:
time: 115 us; the launch traced here: 114 us
  Pallas kernels  46.1 us (40%)
  waiting for transfers between devices  26.7 us (23%)
  starting transfers between devices  19.9 us (17%)
  blocking collectives  14.8 us (13%)
  local copies, waits for them, and re-layouts  3.29 us (3%)
  other arithmetic  2.87 us (2%)
    ppermute x6, waiting for transfers between devices, turn_gains(): lax.ppermute(x, 'bl', [(i, (i + k) % group_count) for i in range(group_co...  24 us
    pallas_call x1, Pallas kernels, body(): pl.pallas_call(functools.partial(rows_kernel, n, cap, group_count), out_s...  16.8 us
    pallas_call x1, Pallas kernels, body(): pl.pallas_call(functools.partial(scatter_kernel, n, cap), out_shape=jax.S...  15.6 us
    all_to_all x1, blocking collectives, exchange(): x = lax.all_to_all(x, both, split_axis=0, concat_axis=0, tiled=True)  14.8 us
    pallas_call x1, Pallas kernels, body(): pl.pallas_call(functools.partial(degrid_kernel, n, cap, taps), out_shape=...  11.6 us
    ppermute x6, starting transfers between devices, turn_gains(): lax.ppermute(x, 'bl', [(i, (i + k) % group_count) for i in range(group_co...  9.48 us
    all_to_all x2, starting transfers between devices, exchange(): x = lax.all_to_all(x, both, split_axis=0, concat_axis=0, tiled=True)  5.36 us
    ppermute x1, starting transfers between devices, body(): lax.ppermute(gain_here, 'tm', [(i, i + 1) for i in range(time_count - 1)])  3.74 us
  transfers between devices with their start and end apart: 10, of which 4 were waited for; matrix products, arithmetic and copies ran while one was open for 2% of the time, Pallas kernels for 28%

profile of v7, /device:TPU:0, one launch (start us, length us, event | category | flops | bytes accessed | tf_op | source)
XLA Modules:
  0.0 114.3 jit_solution(4529621131820551835)
XLA Ops:
  0.6 0.0 copy-start.6
  0.6 1.2 %copy.28 = f32[1,16,8,2,240]{4,1,3,2,0:T(8,128)S(1)} copy(f32[1,16,8,2,240]{4,3,2,1,0:T(2,128)} %param.16) | data formatting | bytes 491520 | tf_op args[7]
  1.8 2.1 %slots.1 = (f32[128,128]{1,0:T(8,128)}, f32[8,512]{1,0:T(8,128)}, f32[512,8]{1,0:T(8,128)}) custom-call(s32[1]{0:T(128)} %bitcast.shift_ref, s32[1,512]{1,0:T(1,128)} %bitcast.51, s32[1,512]{1,0:T(1,128)} %bitcast.52, f32[8,512]{1,0:T(8,128)} %taps_ref.1, s32[2,512]{1,0:T(2,128)} %pairs_ref.1, f32[1,512]{1,0:T(1,128)} %bitcast.53, s32[1,512]{1,0:T(1,128)} %bitcast.54), custom_call_target="tpu_custom_call" | custom-call | flops 1000000000 | bytes 1000000 | tf_op jit(solution)/shard_map/slots/pallas_call | solution.py:505
  3.9 0.0 copy-start.2
  3.9 0.0 copy-start.3
  3.9 14.8 %all_to_all.15 = f32[32,4,128]{2,1,0:T(4,128)S(1)} all-to-all(f32[32,4,128]{2,1,0:T(4,128)} %bitcast.50), channel_id=1, replica_groups=mesh['tm'=8,'bl'=4] {'tm','bl'}, dimensions={0} | all-to-all | bytes 131072 | tf_op jit(solution)/shard_map/all_to_all | solution.py:529
  18.7 0.0 copy-start.5
  18.7 0.1 copy.20
  18.9 0.6 fusion.2.base_ref
  19.5 0.0 copy-done.5
  19.5 11.6 %degrid.1 = (f32[256,128]{1,0:T(8,128)}, f32[1024,256]{1,0:T(8,128)}) custom-call(s32[32,32]{1,0:T(8,128)} %fusion.2.base_ref, f32[128,128]{1,0:T(8,128)} %bitcast.47, f32[16,2048,128]{2,1,0:T(8,128)} %bitcast.45), custom_call_target="tpu_custom_call" | custom-call | flops 100000000 | bytes 70000000 | tf_op jit(solution)/shard_map/degrid/pallas_call | solution.py:549
  31.1 2.6 %all-to-all-start.1 = ((f32[32,8,128]{2,1,0:T(8,128)}), f32[32,8,128]{2,1,0:T(8,128)S(1)}, u32[]{:S(2)}, u32[]{:S(2)}) async-start(f32[32,8,128]{2,1,0:T(8,128)} %bitcast.49), calls=%async_computation.1 | async-start | bytes 262144 | tf_op jit(solution)/shard_map/all_to_all | solution.py:529
  33.7 3.7 %collective-permute-start.2 = (f32[8,2,16,240]{3,2,1,0:T(8,128)S(1)}, f32[8,2,16,240]{3,2,1,0:T(8,128)S(1)}, u32[]{:S(2)}, u32[]{:S(2)}) collective-permute-start(f32[8,2,16,240]{3,2,1,0:T(8,128)S(1)} %bitcast.37), channel_id=1, source_target_pairs={{0,3},{1,0},{2,1},{3,2},{4,7},{5,4},{6,5},{7,6},{8,11},{9,8},{10,9... | collective-permute-start | bytes 737288 | tf_op jit(solution)/shard_map/ppermute | solution.py:538
  37.3 0.0 collective-permute-start.1
  37.3 1.1 collective-permute-start
  38.4 1.3 %collective-permute-start.4 = (f32[8,2,16,240]{3,2,1,0:T(8,128)S(1)}, f32[8,2,16,240]{3,2,1,0:T(8,128)}, u32[]{:S(2)}, u32[]{:S(2)}) collective-permute-start(f32[8,2,16,240]{3,2,1,0:T(8,128)S(1)} %bitcast.40), channel_id=1, source_target_pairs={{4,0},{8,4},{12,8},{16,12},{20,16},{24,20},{28,24},{5,1},{9,5},{13... | collective-permute-start | bytes 737288 | tf_op jit(solution)/shard_map/ppermute | solution.py:572
  39.7 3.7 %collective-permute-start.3 = (f32[8,2,16,240]{3,2,1,0:T(8,128)S(1)}, f32[8,2,16,240]{3,2,1,0:T(8,128)}, u32[]{:S(2)}, u32[]{:S(2)}) collective-permute-start(f32[8,2,16,240]{3,2,1,0:T(8,128)S(1)} %bitcast.41), channel_id=1, source_target_pairs={{0,4},{4,8},{8,12},{12,16},{16,20},{20,24},{24,28},{1,5},{5,9},{9,... | collective-permute-start | bytes 737288 | tf_op jit(solution)/shard_map/ppermute | solution.py:571
  43.4 0.7 collective-permute-done.2.rest_3_
  44.2 18.5 %collective-permute-done.1.rest_2_ = f32[8,2,16,240]{3,2,1,0:T(8,128)S(1)} collective-permute-done((f32[8,2,16,240]{3,2,1,0:T(8,128)S(1)}, f32[8,2,16,240]{3,2,1,0:T(8,128)S(1)}, u32[]{:S(2)}, u32[]{:S(2)}) %collective-permute-start.1) | collective-permute-done | bytes 245792 | tf_op jit(solution)/shard_map/ppermute | solution.py:538
  62.7 0.0 collective-permute-done.rest_1_
  62.7 0.0 copy-done.6
  62.7 1.0 copy.24.vis_ref
  63.7 0.0 all-to-all-done.1
  63.8 0.0 copy-done.8
  63.8 0.0 copy-done.7
  63.8 0.0 copy-done.2
  63.8 0.0 copy-done.3
  63.8 0.0 copy-start.4
  63.8 0.0 copy-start
  63.8 0.0 copy-start.1
  63.8 16.8 %rowgrads.1 = (f32[8,2,16,240]{3,2,1,0:T(8,128)S(1)}, f32[8,2,16,240]{3,2,1,0:T(8,128)S(1)}, f32[8,2,16,240]{3,2,1,0:T(8,128)S(1)}, f32[8,2,16,240]{3,2,1,0:T(8,128)S(1)}, f32[256,128]{1,0:T(8,128)}) custom-call(f32[8,512]{1,0:T(8,128)S(1)} %copy-done.3, f32[512,8]{1,0:T(8,128)S(1)} %copy-done.2, bf16[512,512]{1,0:T(8,128)(2,1)} %copy.24.vis_ref, ...), custom_call_target="tpu_custom_call" | custom-call | flops 20000000000 | bytes 10000000 | tf_op jit(solution)/shard_map/rowgrads/pallas_call | solution.py:579
  80.6 2.8 %all-to-all-start.2 = ((f32[32,8,128]{2,1,0:T(8,128)}), f32[32,8,128]{2,1,0:T(8,128)S(1)}, u32[]{:S(2)}, u32[]{:S(2)}) async-start(f32[32,8,128]{2,1,0:T(8,128)} %bitcast.18), calls=%async_computation.2 | async-start | bytes 262144 | tf_op jit(solution)/shard_map/all_to_all | solution.py:529
  83.4 3.7 %collective-permute-start.5 = (f32[8,2,16,240]{3,2,1,0:T(8,128)S(1)}, f32[8,2,16,240]{3,2,1,0:T(8,128)S(1)}, u32[]{:S(2)}, u32[]{:S(2)}) collective-permute-start(f32[8,2,16,240]{3,2,1,0:T(8,128)S(1)} %get-tuple-element.43), channel_id=1, source_target_pairs={{0,3},{1,0},{2,1},{3,2},{4,7},{5,4},{6,5},{7,6},{8,11},{9,8},{10,9... | collective-permute-start | bytes 737288 | tf_op jit(solution)/shard_map/ppermute | solution.py:538
  87.0 0.0 collective-permute-start.6
  87.0 1.1 collective-permute-start.7
  88.1 0.0 collective-permute-done.4
  88.1 0.0 collective-permute-done.3
  88.1 0.0 copy-done.4
  88.1 1.2 %multiply_add_fusion = f32[8,2,16,240]{3,2,1,0:T(8,128)S(1)} fusion(f32[8,2,16,240]{3,2,1,0:T(8,128)S(1)} %get-tuple-element.38, f32[8,2,16,240]{3,2,1,0:T(8,128)} %collective-permute-done.4, f32[8,2,16,240]{3,2,1,0:T(8,128)} %collective-permute-done.3, pred[]{:T(512)S(6)} %lt.3, pred[]{:T(512)S(6)} %gt.3, f32[1,16,8,2,240]{4,3,2,1,0:T(2,128)S(1)} %copy-done.4), kind=kLoop, calls=%fused_computation.2 | loop fusion | flops 430080 | bytes 1228802 | tf_op jit(solution)/shard_map/add | solution.py:607
  89.4 2.6 %all-to-all-done.2 = f32[32,8,128]{2,1,0:T(8,128)S(1)} async-done(((f32[32,8,128]{2,1,0:T(8,128)}), f32[32,8,128]{2,1,0:T(8,128)S(1)}, u32[]{:S(2)}, u32[]{:S(2)}) %all-to-all-start.2) | async-done | bytes 131104 | tf_op jit(solution)/shard_map/all_to_all | solution.py:529
  92.0 0.0 copy-done
  92.0 0.0 copy-done.1
  92.0 15.6 %scatter.1 = f32[16,2048,128]{2,1,0:T(8,128)} custom-call(s32[32,32]{1,0:T(8,128)S(1)} %copy-done.1, f32[256,128]{1,0:T(8,128)S(1)} %bitcast.36, f32[1024,256]{1,0:T(8,128)S(1)} %copy-done), custom_call_target="tpu_custom_call" | custom-call | bytes 100000 | tf_op jit(solution)/shard_map/scatter/pallas_call | solution.py:610
  107.6 0.0 collective-permute-done.5
  107.6 4.8 %collective-permute-done.6 = f32[8,2,16,240]{3,2,1,0:T(8,128)S(1)} collective-permute-done((f32[8,2,16,240]{3,2,1,0:T(8,128)S(1)}, f32[8,2,16,240]{3,2,1,0:T(8,128)S(1)}, u32[]{:S(2)}, u32[]{:S(2)}) %collective-permute-start.6) | collective-permute-done | bytes 245792 | tf_op jit(solution)/shard_map/ppermute | solution.py:538
  112.4 0.0 collective-permute-done.7
  112.4 1.0 add_bitcast_fusion
  113.4 0.9 copy.23
  (3 shorter events, 0.0 us)
Async XLA Ops:
  0.6 62.1 %copy-start.6 = (bf16[512,2,240]{0,2,1:T(8,128)(2,1)S(1)}, bf16[512,2,240]{0,2,1:T(8,128)(2,1)}, u32[]{:S(2)}) copy-start(bf16[512,2,240]{0,2,1:T(8,128)(2,1)} %param.9) | copy-start | bytes 1474564
  3.9 59.8 %copy-start.2 = (f32[512,8]{1,0:T(8,128)S(1)}, f32[512,8]{1,0:T(8,128)}, u32[]{:S(2)}) copy-start(f32[512,8]{1,0:T(8,128)} %get-tuple-element.27.cols_ref) | copy-start | bytes 49156
  3.9 59.8 %copy-start.3 = (f32[8,512]{1,0:T(8,128)S(1)}, f32[8,512]{1,0:T(8,128)}, u32[]{:S(2)}) copy-start(f32[8,512]{1,0:T(8,128)} %get-tuple-element.26.rows_ref) | copy-start | bytes 49156
  18.7 0.7 copy-start.5
  31.1 32.7 %all-to-all-start.1 = ((f32[32,8,128]{2,1,0:T(8,128)}), f32[32,8,128]{2,1,0:T(8,128)S(1)}, u32[]{:S(2)}, u32[]{:S(2)}) async-start(f32[32,8,128]{2,1,0:T(8,128)} %bitcast.49), calls=%async_computation.1 | async-start | bytes 262144 | tf_op jit(solution)/shard_map/all_to_all | solution.py:529
  33.7 10.5 %collective-permute-start.2 = (f32[8,2,16,240]{3,2,1,0:T(8,128)S(1)}, f32[8,2,16,240]{3,2,1,0:T(8,128)S(1)}, u32[]{:S(2)}, u32[]{:S(2)}) collective-permute-start(f32[8,2,16,240]{3,2,1,0:T(8,128)S(1)} %bitcast.37), channel_id=1, source_target_pairs={{0,3},{1,0},{2,1},{3,2},{4,7},{5,4},{6,5},{7,6},{8,11},{9,8},{10,9... | collective-permute-start | bytes 737288 | tf_op jit(solution)/shard_map/ppermute | solution.py:538
  37.3 25.4 %collective-permute-start.1 = (f32[8,2,16,240]{3,2,1,0:T(8,128)S(1)}, f32[8,2,16,240]{3,2,1,0:T(8,128)S(1)}, u32[]{:S(2)}, u32[]{:S(2)}) collective-permute-start(f32[8,2,16,240]{3,2,1,0:T(8,128)S(1)} %bitcast.38), channel_id=1, source_target_pairs={{0,2},{1,3},{2,0},{3,1},{4,6},{5,7},{6,4},{7,5},{8,10},{9,11},{10,... | collective-permute-start | bytes 737288 | tf_op jit(solution)/shard_map/ppermute | solution.py:538
  37.3 25.4 %collective-permute-start = (f32[8,2,16,240]{3,2,1,0:T(8,128)S(1)}, f32[8,2,16,240]{3,2,1,0:T(8,128)}, u32[]{:S(2)}, u32[]{:S(2)}) collective-permute-start(f32[8,2,16,240]{3,2,1,0:T(8,128)S(1)} %bitcast.39), channel_id=1, source_target_pairs={{0,1},{1,2},{2,3},{3,0},{4,5},{5,6},{6,7},{7,4},{8,9},{9,10},{10,1... | collective-permute-start | bytes 737288 | tf_op jit(solution)/shard_map/ppermute | solution.py:538
  38.4 49.7 %collective-permute-start.4 = (f32[8,2,16,240]{3,2,1,0:T(8,128)S(1)}, f32[8,2,16,240]{3,2,1,0:T(8,128)}, u32[]{:S(2)}, u32[]{:S(2)}) collective-permute-start(f32[8,2,16,240]{3,2,1,0:T(8,128)S(1)} %bitcast.40), channel_id=1, source_target_pairs={{4,0},{8,4},{12,8},{16,12},{20,16},{24,20},{28,24},{5,1},{9,5},{13... | collective-permute-start | bytes 737288 | tf_op jit(solution)/shard_map/ppermute | solution.py:572
  39.7 48.4 %collective-permute-start.3 = (f32[8,2,16,240]{3,2,1,0:T(8,128)S(1)}, f32[8,2,16,240]{3,2,1,0:T(8,128)}, u32[]{:S(2)}, u32[]{:S(2)}) collective-permute-start(f32[8,2,16,240]{3,2,1,0:T(8,128)S(1)} %bitcast.41), channel_id=1, source_target_pairs={{0,4},{4,8},{8,12},{12,16},{16,20},{20,24},{24,28},{1,5},{5,9},{9,... | collective-permute-start | bytes 737288 | tf_op jit(solution)/shard_map/ppermute | solution.py:571
  44.2 19.6 %copy-start.7 = (f32[8,2,16,240]{3,2,1,0:T(8,128)}, f32[8,2,16,240]{3,2,1,0:T(8,128)S(1)}, u32[]{:S(2)}) copy-start(f32[8,2,16,240]{3,2,1,0:T(8,128)S(1)} %collective-permute-done.2.rest_3_) | copy-start | bytes 737284
  62.7 1.1 copy-start.8
  63.8 24.3 %copy-start.4 = (f32[1,16,8,2,240]{4,3,2,1,0:T(2,128)S(1)}, f32[1,16,8,2,240]{4,3,2,1,0:T(2,128)}, u32[]{:S(2)}) copy-start(f32[1,16,8,2,240]{4,3,2,1,0:T(2,128)} %param.16) | copy-start | bytes 737284
  63.8 28.2 %copy-start = (f32[1024,256]{1,0:T(8,128)S(1)}, f32[1024,256]{1,0:T(8,128)}, u32[]{:S(2)}) copy-start(f32[1024,256]{1,0:T(8,128)} %get-tuple-element.42.w_ref) | copy-start | bytes 3145732
  63.8 28.2 %copy-start.1 = (s32[32,32]{1,0:T(8,128)S(1)}, s32[32,32]{1,0:T(8,128)}, u32[]{:S(2)}) copy-start(s32[32,32]{1,0:T(8,128)} %fusion.2.base_ref) | copy-start | bytes 12292
  80.6 11.4 %all-to-all-start.2 = ((f32[32,8,128]{2,1,0:T(8,128)}), f32[32,8,128]{2,1,0:T(8,128)S(1)}, u32[]{:S(2)}, u32[]{:S(2)}) async-start(f32[32,8,128]{2,1,0:T(8,128)} %bitcast.18), calls=%async_computation.2 | async-start | bytes 262144 | tf_op jit(solution)/shard_map/all_to_all | solution.py:529
  83.4 24.3 %collective-permute-start.5 = (f32[8,2,16,240]{3,2,1,0:T(8,128)S(1)}, f32[8,2,16,240]{3,2,1,0:T(8,128)S(1)}, u32[]{:S(2)}, u32[]{:S(2)}) collective-permute-start(f32[8,2,16,240]{3,2,1,0:T(8,128)S(1)} %get-tuple-element.43), channel_id=1, source_target_pairs={{0,3},{1,0},{2,1},{3,2},{4,7},{5,4},{6,5},{7,6},{8,11},{9,8},{10,9... | collective-permute-start | bytes 737288 | tf_op jit(solution)/shard_map/ppermute | solution.py:538
  87.0 25.4 %collective-permute-start.6 = (f32[8,2,16,240]{3,2,1,0:T(8,128)S(1)}, f32[8,2,16,240]{3,2,1,0:T(8,128)S(1)}, u32[]{:S(2)}, u32[]{:S(2)}) collective-permute-start(f32[8,2,16,240]{3,2,1,0:T(8,128)S(1)} %get-tuple-element.44), channel_id=1, source_target_pairs={{0,2},{1,3},{2,0},{3,1},{4,6},{5,7},{6,4},{7,5},{8,10},{9,11},{10,... | collective-permute-start | bytes 737288 | tf_op jit(solution)/shard_map/ppermute | solution.py:538
  87.0 25.4 %collective-permute-start.7 = (f32[8,2,16,240]{3,2,1,0:T(8,128)S(1)}, f32[8,2,16,240]{3,2,1,0:T(8,128)}, u32[]{:S(2)}, u32[]{:S(2)}) collective-permute-start(f32[8,2,16,240]{3,2,1,0:T(8,128)S(1)} %get-tuple-element.45), channel_id=1, source_target_pairs={{0,1},{1,2},{2,3},{3,0},{4,5},{5,6},{6,7},{7,4},{8,9},{9,10},{10,1... | collective-permute-start | bytes 737288 | tf_op jit(solution)/shard_map/ppermute | solution.py:538

commit v8 on v7

--- a/solution.py
+++ b/solution.py
@@ -220,12 +220,10 @@
     n, cap, group_count,
     rows_ref, cols_ref, vis_ref, back_ref, *rest,
 ):
-    gain_refs = rest[:group_count]
-    out_refs = rest[group_count : 2 * group_count]
-    send_ref = rest[2 * group_count]
-    gains, spec, a_s, b_s, m_s, p_s, e_s, glr_hi, glr_lo, gm_hi, gm_lo = rest[
-        2 * group_count + 1 :
-    ]
+    far = group_count - group_count // 2 - 1
+    gain_refs, rest = rest[: group_count + far], rest[group_count + far :]
+    out_refs, send_ref, rest = rest[:group_count], rest[group_count], rest[group_count + 1 :]
+    gains, spec, a_s, b_s, m_s, p_s, e_s, glr_hi, glr_lo, gm_hi, gm_lo = rest
     facets, _, group, channels = gain_refs[0].shape
     rows = cols_ref.shape[0]
     stations = group * group_count
@@ -239,11 +237,13 @@
 
     gains[...] = jnp.zeros(gains.shape, f32)
     for k in range(group_count):
+        mine = slice(k * group, (k + 1) * group)
         for f in range(facets):
+            ref, at = gain_refs[k], f
+            if f >= ref.shape[0]:
+                ref, at = gain_refs[k + far], f - ref.shape[0]
             for x in range(2):
-                gains[f, k * group : (k + 1) * group, x * half : x * half + channels] = (
-                    gain_refs[k][f, x]
-                )
+                gains[f, mine, x * half : x * half + channels] = ref[at, x]
 
     owner3 = as_bf16(mod(iota((1, 3 * n), 1), n) == owner_col)
     per_line = LANES // planes
@@ -541,7 +541,11 @@
 
     send, gain_first = lax.optimization_barrier((send, gain_turned))
     received = exchange(send)
-    gathered = [turn_gains(gain_first, k) for k in range(1, group_count)]
+    near = range(1, group_count // 2 + 1)
+    far = range(group_count // 2 + 1, group_count)
+    part = facets // 2
+    early = [turn_gains(gain_first, k) for k in near]
+    early += [turn_gains(gain_first[:part], k) for k in far]
     base = received.reshape(n, lines * LANES)[:, (taps + 1) * cap : (taps + 2) * cap]
     base = jnp.clip(base.T.astype(i32), 0, tiles - 2) * terms
     slot_lines = n * cap * planes // LANES
@@ -566,11 +570,12 @@
         cost_estimate=cost(10**8, 7 * 10**7),
         name="degrid",
     )(base, received, sky)
-    values, gain_here = lax.optimization_barrier((values, gain_turned))
+    values, gain_here, *early = lax.optimization_barrier((values, gain_turned, *early))
     back = exchange(values)
     below = lax.ppermute(gain_here, "tm", [(i, i + 1) for i in range(time_count - 1)])
     above = lax.ppermute(gain_here, "tm", [(i + 1, i) for i in range(time_count - 1)])
-    visibilities, *gathered = lax.optimization_barrier((visibilities, *gathered))
+    late = [turn_gains(gain_here[part:], k) for k in far]
+    gathered = [gain_turned, *early, *late]
 
     vis_wide = jnp.pad(visibilities, ((0, 0), (0, 0), (0, half - channels))).reshape(
         rows, wide
@@ -580,7 +585,7 @@
         functools.partial(rows_kernel, n, cap, group_count),
         out_shape=(partial_shape,) * group_count
         + (jax.ShapeDtypeStruct((slot_lines, LANES), f32),),
-        in_specs=[VMEM] * (4 + group_count),
+        in_specs=[VMEM] * (4 + len(gathered)),
         out_specs=(VMEM,) * (group_count + 1),
         scratch_shapes=[
             pltpu.VMEM((facets, stations, wide), f32),
@@ -598,7 +603,7 @@
         compiler_params=params(52),
         cost_estimate=cost(2 * 10**10, 10**7),
         name="rowgrads",
-    )(row_table, col_table, vis_wide, back, gain_turned, *gathered)
+    )(row_table, col_table, vis_wide, back, *gathered)
 
     own, *parts, send_grad = outs
     when = lax.axis_index("tm")

time: 115 us -> 101 us (0.88)
  starting transfers between devices: 19.9 us -> 36.5 us
  waiting for transfers between devices: 26.7 us -> 11.3 us
  blocking collectives: 14.8 us -> 0 us
    ppermute x6 -> x7, waiting for transfers between devices: 24 us -> 7.49 us  [turn_gains(): lax.ppermute(x, 'bl', [(i, (i + k) % group_count) for i in range(group_co...]
    all_to_all x1 -> x0, blocking collectives: 14.8 us -> none  [exchange(): x = lax.all_to_all(x, both, split_axis=0, concat_axis=0, tiled=True)]
    all_to_all x2 -> x3, starting transfers between devices: 5.36 us -> 16.5 us  [exchange(): x = lax.all_to_all(x, both, split_axis=0, concat_axis=0, tiled=True)]
    ppermute x6 -> x7, starting transfers between devices: 9.48 us -> 15 us  [turn_gains(): lax.ppermute(x, 'bl', [(i, (i + k) % group_count) for i in range(group_co...]
    all_to_all x2 -> x3, waiting for transfers between devices: 2.62 us -> 3.82 us  [exchange(): x = lax.all_to_all(x, both, split_axis=0, concat_axis=0, tiled=True)]
  transfers between devices with their start and end apart: 10 -> 12, of which waited for: 4 -> 4; matrix products, arithmetic and copies ran while one was open for 2% -> 3% of each run, Pallas kernels for 28% -> 43%
where the time goes in v8:
time: 101 us
  Pallas kernels  45.9 us (45%)
  starting transfers between devices  36.5 us (36%)
  waiting for transfers between devices  11.3 us (11%)
  local copies, waits for them, and re-layouts  3.32 us (3%)
  other arithmetic  2.96 us (3%)
    pallas_call x1, Pallas kernels, body(): pl.pallas_call(functools.partial(rows_kernel, n, cap, group_count), out_s...  16.8 us
    all_to_all x3, starting transfers between devices, exchange(): x = lax.all_to_all(x, both, split_axis=0, concat_axis=0, tiled=True)  16.5 us
    pallas_call x1, Pallas kernels, body(): pl.pallas_call(functools.partial(scatter_kernel, n, cap), out_shape=jax.S...  15.3 us
    ppermute x7, starting transfers between devices, turn_gains(): lax.ppermute(x, 'bl', [(i, (i + k) % group_count) for i in range(group_co...  15 us
    pallas_call x1, Pallas kernels, body(): pl.pallas_call(functools.partial(degrid_kernel, n, cap, taps), out_shape=...  11.6 us
    ppermute x7, waiting for transfers between devices, turn_gains(): lax.ppermute(x, 'bl', [(i, (i + k) % group_count) for i in range(group_co...  7.49 us
    all_to_all x3, waiting for transfers between devices, exchange(): x = lax.all_to_all(x, both, split_axis=0, concat_axis=0, tiled=True)  3.82 us
    ppermute x1, starting transfers between devices, body(): lax.ppermute(gain_here, 'tm', [(i, i + 1) for i in range(time_count - 1)])  3.73 us
  transfers between devices with their start and end apart: 12, of which 4 were waited for; matrix products, arithmetic and copies ran while one was open for 3% of the time, Pallas kernels for 43%

profile of v8, /device:TPU:0, one launch (start us, length us, event | category | flops | bytes accessed | tf_op | source)
XLA Modules:
  0.0 100.9 jit_solution(1891684685567685166)
XLA Ops:
  0.6 0.0 copy-start.7
  0.6 1.2 %copy.28 = f32[1,16,8,2,240]{4,1,3,2,0:T(8,128)S(1)} copy(f32[1,16,8,2,240]{4,3,2,1,0:T(2,128)} %param.16) | data formatting | bytes 491520 | tf_op args[7]
  1.8 0.0 copy-start.4
  1.8 2.2 %slots.1 = (f32[128,128]{1,0:T(8,128)}, f32[8,512]{1,0:T(8,128)}, f32[512,8]{1,0:T(8,128)}) custom-call(s32[1]{0:T(128)} %bitcast.shift_ref, s32[1,512]{1,0:T(1,128)} %bitcast.52, s32[1,512]{1,0:T(1,128)} %bitcast.53, f32[8,512]{1,0:T(8,128)} %taps_ref.1, s32[2,512]{1,0:T(2,128)} %pairs_ref.1, f32[1,512]{1,0:T(1,128)} %bitcast.54, s32[1,512]{1,0:T(1,128)} %bitcast.55), custom_call_target="tpu_custom_call" | custom-call | flops 1000000000 | bytes 1000000 | tf_op jit(solution)/shard_map/slots/pallas_call | solution.py:505
  4.0 7.3 %all-to-all-start = ((f32[32,4,128]{2,1,0:T(4,128)}), f32[32,4,128]{2,1,0:T(4,128)S(1)}, u32[]{:S(2)}, u32[]{:S(2)}) async-start(f32[32,4,128]{2,1,0:T(4,128)} %bitcast.51), calls=%async_computation | async-start | bytes 131072 | tf_op jit(solution)/shard_map/all_to_all | solution.py:529
  11.3 2.7 %collective-permute-start.1 = (f32[8,2,16,240]{3,2,1,0:T(8,128)S(1)}, f32[8,2,16,240]{3,2,1,0:T(8,128)S(1)}, u32[]{:S(2)}, u32[]{:S(2)}) collective-permute-start(f32[8,2,16,240]{3,2,1,0:T(8,128)S(1)} %bitcast.41), channel_id=1, source_target_pairs={{0,2},{1,3},{2,0},{3,1},{4,6},{5,7},{6,4},{7,5},{8,10},{9,11},{10,... | collective-permute-start | bytes 737288 | tf_op jit(solution)/shard_map/ppermute | solution.py:538
  14.1 1.5 %collective-permute-start = (f32[8,2,16,240]{3,2,1,0:T(8,128)S(1)}, f32[8,2,16,240]{3,2,1,0:T(8,128)S(1)}, u32[]{:S(2)}, u32[]{:S(2)}) collective-permute-start(f32[8,2,16,240]{3,2,1,0:T(8,128)S(1)} %bitcast.42), channel_id=1, source_target_pairs={{0,1},{1,2},{2,3},{3,0},{4,5},{5,6},{6,7},{7,4},{8,9},{9,10},{10,1... | collective-permute-start | bytes 737288 | tf_op jit(solution)/shard_map/ppermute | solution.py:538
  15.6 2.4 %collective-permute-start.2 = (f32[4,2,16,240]{3,2,1,0:T(8,128)S(1)}, f32[4,2,16,240]{3,2,1,0:T(8,128)S(1)}, u32[]{:S(2)}, u32[]{:S(2)}) collective-permute-start(f32[4,2,16,240]{3,2,1,0:T(8,128)S(1)} %slice.10), channel_id=1, source_target_pairs={{0,3},{1,0},{2,1},{3,2},{4,7},{5,4},{6,5},{7,6},{8,11},{9,8},{10,9... | collective-permute-start | bytes 368648 | tf_op jit(solution)/shard_map/ppermute | solution.py:538
  18.0 1.2 %all-to-all-done = f32[32,4,128]{2,1,0:T(4,128)S(1)} async-done(((f32[32,4,128]{2,1,0:T(4,128)}), f32[32,4,128]{2,1,0:T(4,128)S(1)}, u32[]{:S(2)}, u32[]{:S(2)}) %all-to-all-start) | async-done | bytes 65568 | tf_op jit(solution)/shard_map/all_to_all | solution.py:529
  19.2 0.1 copy.20
  19.3 0.6 fusion.2.base_ref
  19.9 0.0 copy-done.6
  19.9 11.6 %degrid.1 = (f32[256,128]{1,0:T(8,128)}, f32[1024,256]{1,0:T(8,128)}) custom-call(s32[32,32]{1,0:T(8,128)} %fusion.2.base_ref, f32[128,128]{1,0:T(8,128)} %bitcast.48, f32[16,2048,128]{2,1,0:T(8,128)} %bitcast.39), custom_call_target="tpu_custom_call" | custom-call | flops 100000000 | bytes 70000000 | tf_op jit(solution)/shard_map/degrid/pallas_call | solution.py:553
  31.6 0.0 collective-permute-done.2.rest_3_
  31.6 2.2 %collective-permute-done.1.rest_2_ = f32[8,2,16,240]{3,2,1,0:T(8,128)S(1)} collective-permute-done((f32[8,2,16,240]{3,2,1,0:T(8,128)S(1)}, f32[8,2,16,240]{3,2,1,0:T(8,128)S(1)}, u32[]{:S(2)}, u32[]{:S(2)}) %collective-permute-start.1) | collective-permute-done | bytes 245792 | tf_op jit(solution)/shard_map/ppermute | solution.py:538
  33.8 0.0 collective-permute-done.rest_1_
  33.9 5.7 %all-to-all-start.1 = ((f32[32,8,128]{2,1,0:T(8,128)}), f32[32,8,128]{2,1,0:T(8,128)S(1)}, u32[]{:S(2)}, u32[]{:S(2)}) async-start(f32[32,8,128]{2,1,0:T(8,128)} %bitcast.50), calls=%async_computation.1 | async-start | bytes 262144 | tf_op jit(solution)/shard_map/all_to_all | solution.py:529
  39.6 3.7 %collective-permute-start.3 = (f32[4,2,16,240]{3,2,1,0:T(8,128)S(1)}, f32[4,2,16,240]{3,2,1,0:T(8,128)S(1)}, u32[]{:S(2)}, u32[]{:S(2)}) collective-permute-start(f32[4,2,16,240]{3,2,1,0:T(8,128)S(1)} %slice.11), channel_id=1, source_target_pairs={{0,3},{1,0},{2,1},{3,2},{4,7},{5,4},{6,5},{7,6},{8,11},{9,8},{10,9... | collective-permute-start | bytes 368648 | tf_op jit(solution)/shard_map/ppermute | solution.py:538
  43.3 0.0 copy-done.8
  43.3 0.0 copy-done.7
  43.3 1.0 %copy.24.vis_ref = bf16[512,512]{1,0:T(8,128)(2,1)} copy(bf16[512,512]{0,1:T(8,128)(2,1)S(1)} %bitcast.40) | data formatting | bytes 1048576 | tf_op jit(solution)/shard_map/reshape | solution.py:580
  44.4 1.3 %collective-permute-start.5 = (f32[8,2,16,240]{3,2,1,0:T(8,128)S(1)}, f32[8,2,16,240]{3,2,1,0:T(8,128)}, u32[]{:S(2)}, u32[]{:S(2)}) collective-permute-start(f32[8,2,16,240]{3,2,1,0:T(8,128)S(1)} %bitcast.45), channel_id=1, source_target_pairs={{4,0},{8,4},{12,8},{16,12},{20,16},{24,20},{28,24},{5,1},{9,5},{13... | collective-permute-start | bytes 737288 | tf_op jit(solution)/shard_map/ppermute | solution.py:576
  45.6 3.7 %collective-permute-start.4 = (f32[8,2,16,240]{3,2,1,0:T(8,128)S(1)}, f32[8,2,16,240]{3,2,1,0:T(8,128)}, u32[]{:S(2)}, u32[]{:S(2)}) collective-permute-start(f32[8,2,16,240]{3,2,1,0:T(8,128)S(1)} %bitcast.46), channel_id=1, source_target_pairs={{0,4},{4,8},{8,12},{12,16},{16,20},{20,24},{24,28},{1,5},{5,9},{9,... | collective-permute-start | bytes 737288 | tf_op jit(solution)/shard_map/ppermute | solution.py:575
  49.4 0.0 collective-permute-done.3.rest_4_
  49.4 0.0 all-to-all-done.1
  49.4 0.0 copy-done.9
  49.4 0.0 copy-done.4
  49.4 0.0 copy-done.2
  49.4 0.0 copy-done.3
  49.4 0.0 copy-start.5
  49.4 0.0 copy-start
  49.5 16.8 %rowgrads.1 = (f32[8,2,16,240]{3,2,1,0:T(8,128)S(1)}, f32[8,2,16,240]{3,2,1,0:T(8,128)S(1)}, f32[8,2,16,240]{3,2,1,0:T(8,128)S(1)}, f32[8,2,16,240]{3,2,1,0:T(8,128)S(1)}, f32[256,128]{1,0:T(8,128)}) custom-call(f32[8,512]{1,0:T(8,128)S(1)} %copy-done.3, f32[512,8]{1,0:T(8,128)S(1)} %copy-done.2, bf16[512,512]{1,0:T(8,128)(2,1)} %copy.24.vis_ref, ...), custom_call_target="tpu_custom_call" | custom-call | flops 20000000000 | bytes 10000000 | tf_op jit(solution)/shard_map/rowgrads/pallas_call | solution.py:584
  66.2 3.4 %all-to-all-start.2 = ((f32[32,8,128]{2,1,0:T(8,128)}), f32[32,8,128]{2,1,0:T(8,128)S(1)}, u32[]{:S(2)}, u32[]{:S(2)}) async-start(f32[32,8,128]{2,1,0:T(8,128)} %bitcast.17), calls=%async_computation.2 | async-start | bytes 262144 | tf_op jit(solution)/shard_map/all_to_all | solution.py:529
  69.7 3.7 %collective-permute-start.6 = (f32[8,2,16,240]{3,2,1,0:T(8,128)S(1)}, f32[8,2,16,240]{3,2,1,0:T(8,128)S(1)}, u32[]{:S(2)}, u32[]{:S(2)}) collective-permute-start(f32[8,2,16,240]{3,2,1,0:T(8,128)S(1)} %get-tuple-element.41), channel_id=1, source_target_pairs={{0,3},{1,0},{2,1},{3,2},{4,7},{5,4},{6,5},{7,6},{8,11},{9,8},{10,9... | collective-permute-start | bytes 737288 | tf_op jit(solution)/shard_map/ppermute | solution.py:538
  73.3 0.0 collective-permute-start.7
  73.4 1.1 %collective-permute-start.8 = (f32[8,2,16,240]{3,2,1,0:T(8,128)S(1)}, f32[8,2,16,240]{3,2,1,0:T(8,128)}, u32[]{:S(2)}, u32[]{:S(2)}) collective-permute-start(f32[8,2,16,240]{3,2,1,0:T(8,128)S(1)} %get-tuple-element.43), channel_id=1, source_target_pairs={{0,1},{1,2},{2,3},{3,0},{4,5},{5,6},{6,7},{7,4},{8,9},{9,10},{10,1... | collective-permute-start | bytes 737288 | tf_op jit(solution)/shard_map/ppermute | solution.py:538
  74.4 0.0 collective-permute-done.5
  74.4 0.0 collective-permute-done.4
  74.4 0.0 copy-done.5
  74.4 1.2 %multiply_add_fusion = f32[8,2,16,240]{3,2,1,0:T(8,128)S(1)} fusion(f32[8,2,16,240]{3,2,1,0:T(8,128)S(1)} %get-tuple-element.37, f32[8,2,16,240]{3,2,1,0:T(8,128)} %collective-permute-done.5, f32[8,2,16,240]{3,2,1,0:T(8,128)} %collective-permute-done.4, pred[]{:T(512)S(6)} %lt.3, pred[]{:T(512)S(6)} %gt.3, f32[1,16,8,2,240]{4,3,2,1,0:T(2,128)S(1)} %copy-done.5), kind=kLoop, calls=%fused_computation.2 | loop fusion | flops 430080 | bytes 1228802 | tf_op jit(solution)/shard_map/add | solution.py:612
  75.7 2.6 %all-to-all-done.2 = f32[32,8,128]{2,1,0:T(8,128)S(1)} async-done(((f32[32,8,128]{2,1,0:T(8,128)}), f32[32,8,128]{2,1,0:T(8,128)S(1)}, u32[]{:S(2)}, u32[]{:S(2)}) %all-to-all-start.2) | async-done | bytes 131104 | tf_op jit(solution)/shard_map/all_to_all | solution.py:529
  78.3 0.0 copy-done.1
  78.3 15.3 %scatter.1 = f32[16,2048,128]{2,1,0:T(8,128)} custom-call(s32[32,32]{1,0:T(8,128)S(1)} %copy-done.1, f32[256,128]{1,0:T(8,128)S(1)} %bitcast.36, f32[1024,256]{1,0:T(8,128)S(1)} %copy-done), custom_call_target="tpu_custom_call" | custom-call | bytes 100000 | tf_op jit(solution)/shard_map/scatter/pallas_call | solution.py:615
  93.6 0.0 collective-permute-done.6
  93.6 5.2 %collective-permute-done.7 = f32[8,2,16,240]{3,2,1,0:T(8,128)} collective-permute-done((f32[8,2,16,240]{3,2,1,0:T(8,128)S(1)}, f32[8,2,16,240]{3,2,1,0:T(8,128)}, u32[]{:S(2)}, u32[]{:S(2)}) %collective-permute-start.7) | collective-permute-done | bytes 245792 | tf_op jit(solution)/shard_map/ppermute | solution.py:538
  98.8 0.0 collective-permute-done.8
  98.8 1.1 %add_bitcast_fusion = f32[1,16,8,2,240]{4,1,3,2,0:T(8,128)S(1)} fusion(f32[8,2,16,240]{3,2,1,0:T(8,128)} %collective-permute-done.8, f32[8,2,16,240]{3,2,1,0:T(8,128)} %collective-permute-done.7, f32[8,2,16,240]{3,2,1,0:T(8,128)S(1)} %multiply_add_fusion, f32[8,2,16,240]{3,2,1,0:T(8,128)S(1)} %collective-permute-done.6), kind=kLoop, calls=%fused_computation.1 | loop fusion | flops 184320 | bytes 1228800 | tf_op jit(solution)/shard_map/broadcast_in_dim | solution.py:638
  99.9 0.9 copy.23
  (10 shorter events, 0.1 us)
Async XLA Ops:
  0.6 42.7 %copy-start.7 = (bf16[512,2,240]{0,2,1:T(8,128)(2,1)S(1)}, bf16[512,2,240]{0,2,1:T(8,128)(2,1)}, u32[]{:S(2)}) copy-start(bf16[512,2,240]{0,2,1:T(8,128)(2,1)} %param.9) | copy-start | bytes 1474564
  1.8 47.6 %copy-start.4 = (f32[1,16,8,2,240]{4,1,3,2,0:T(8,128)}, f32[1,16,8,2,240]{4,1,3,2,0:T(8,128)S(1)}, u32[]{:S(2)}) copy-start(f32[1,16,8,2,240]{4,1,3,2,0:T(8,128)S(1)} %copy.28) | copy-start | bytes 737284
  4.0 45.4 %copy-start.2 = (f32[512,8]{1,0:T(8,128)S(1)}, f32[512,8]{1,0:T(8,128)}, u32[]{:S(2)}) copy-start(f32[512,8]{1,0:T(8,128)} %get-tuple-element.26.cols_ref) | copy-start | bytes 49156
  4.0 45.4 %copy-start.3 = (f32[8,512]{1,0:T(8,128)S(1)}, f32[8,512]{1,0:T(8,128)}, u32[]{:S(2)}) copy-start(f32[8,512]{1,0:T(8,128)} %get-tuple-element.25.rows_ref) | copy-start | bytes 49156
  4.0 15.1 %all-to-all-start = ((f32[32,4,128]{2,1,0:T(4,128)}), f32[32,4,128]{2,1,0:T(4,128)S(1)}, u32[]{:S(2)}, u32[]{:S(2)}) async-start(f32[32,4,128]{2,1,0:T(4,128)} %bitcast.51), calls=%async_computation | async-start | bytes 131072 | tf_op jit(solution)/shard_map/all_to_all | solution.py:529
  11.3 22.5 %collective-permute-start.1 = (f32[8,2,16,240]{3,2,1,0:T(8,128)S(1)}, f32[8,2,16,240]{3,2,1,0:T(8,128)S(1)}, u32[]{:S(2)}, u32[]{:S(2)}) collective-permute-start(f32[8,2,16,240]{3,2,1,0:T(8,128)S(1)} %bitcast.41), channel_id=1, source_target_pairs={{0,2},{1,3},{2,0},{3,1},{4,6},{5,7},{6,4},{7,5},{8,10},{9,11},{10,... | collective-permute-start | bytes 737288 | tf_op jit(solution)/shard_map/ppermute | solution.py:538
  14.1 19.8 %collective-permute-start = (f32[8,2,16,240]{3,2,1,0:T(8,128)S(1)}, f32[8,2,16,240]{3,2,1,0:T(8,128)S(1)}, u32[]{:S(2)}, u32[]{:S(2)}) collective-permute-start(f32[8,2,16,240]{3,2,1,0:T(8,128)S(1)} %bitcast.42), channel_id=1, source_target_pairs={{0,1},{1,2},{2,3},{3,0},{4,5},{5,6},{6,7},{7,4},{8,9},{9,10},{10,1... | collective-permute-start | bytes 737288 | tf_op jit(solution)/shard_map/ppermute | solution.py:538
  15.6 16.0 %collective-permute-start.2 = (f32[4,2,16,240]{3,2,1,0:T(8,128)S(1)}, f32[4,2,16,240]{3,2,1,0:T(8,128)S(1)}, u32[]{:S(2)}, u32[]{:S(2)}) collective-permute-start(f32[4,2,16,240]{3,2,1,0:T(8,128)S(1)} %slice.10), channel_id=1, source_target_pairs={{0,3},{1,0},{2,1},{3,2},{4,7},{5,4},{6,5},{7,6},{8,11},{9,8},{10,9... | collective-permute-start | bytes 368648 | tf_op jit(solution)/shard_map/ppermute | solution.py:538
  19.2 0.8 copy-start.6
  33.8 9.4 %copy-start.8 = (f32[8,2,16,240]{3,2,1,0:T(8,128)}, f32[8,2,16,240]{3,2,1,0:T(8,128)S(1)}, u32[]{:S(2)}) copy-start(f32[8,2,16,240]{3,2,1,0:T(8,128)S(1)} %collective-permute-done.1.rest_2_) | copy-start | bytes 737284
  33.8 15.5 %copy-start.9 = (f32[8,2,16,240]{3,2,1,0:T(8,128)}, f32[8,2,16,240]{3,2,1,0:T(8,128)S(1)}, u32[]{:S(2)}) copy-start(f32[8,2,16,240]{3,2,1,0:T(8,128)S(1)} %collective-permute-done.rest_1_) | copy-start | bytes 737284
  33.9 15.5 %all-to-all-start.1 = ((f32[32,8,128]{2,1,0:T(8,128)}), f32[32,8,128]{2,1,0:T(8,128)S(1)}, u32[]{:S(2)}, u32[]{:S(2)}) async-start(f32[32,8,128]{2,1,0:T(8,128)} %bitcast.50), calls=%async_computation.1 | async-start | bytes 262144 | tf_op jit(solution)/shard_map/all_to_all | solution.py:529
  39.6 9.8 %collective-permute-start.3 = (f32[4,2,16,240]{3,2,1,0:T(8,128)S(1)}, f32[4,2,16,240]{3,2,1,0:T(8,128)S(1)}, u32[]{:S(2)}, u32[]{:S(2)}) collective-permute-start(f32[4,2,16,240]{3,2,1,0:T(8,128)S(1)} %slice.11), channel_id=1, source_target_pairs={{0,3},{1,0},{2,1},{3,2},{4,7},{5,4},{6,5},{7,6},{8,11},{9,8},{10,9... | collective-permute-start | bytes 368648 | tf_op jit(solution)/shard_map/ppermute | solution.py:538
  44.4 30.1 %collective-permute-start.5 = (f32[8,2,16,240]{3,2,1,0:T(8,128)S(1)}, f32[8,2,16,240]{3,2,1,0:T(8,128)}, u32[]{:S(2)}, u32[]{:S(2)}) collective-permute-start(f32[8,2,16,240]{3,2,1,0:T(8,128)S(1)} %bitcast.45), channel_id=1, source_target_pairs={{4,0},{8,4},{12,8},{16,12},{20,16},{24,20},{28,24},{5,1},{9,5},{13... | collective-permute-start | bytes 737288 | tf_op jit(solution)/shard_map/ppermute | solution.py:576
  45.6 28.8 %collective-permute-start.4 = (f32[8,2,16,240]{3,2,1,0:T(8,128)S(1)}, f32[8,2,16,240]{3,2,1,0:T(8,128)}, u32[]{:S(2)}, u32[]{:S(2)}) collective-permute-start(f32[8,2,16,240]{3,2,1,0:T(8,128)S(1)} %bitcast.46), channel_id=1, source_target_pairs={{0,4},{4,8},{8,12},{12,16},{16,20},{20,24},{24,28},{1,5},{5,9},{9,... | collective-permute-start | bytes 737288 | tf_op jit(solution)/shard_map/ppermute | solution.py:575
  49.4 25.0 %copy-start.5 = (f32[1,16,8,2,240]{4,3,2,1,0:T(2,128)S(1)}, f32[1,16,8,2,240]{4,3,2,1,0:T(2,128)}, u32[]{:S(2)}) copy-start(f32[1,16,8,2,240]{4,3,2,1,0:T(2,128)} %param.16) | copy-start | bytes 737284
  49.4 28.9 %copy-start = (f32[1024,256]{1,0:T(8,128)S(1)}, f32[1024,256]{1,0:T(8,128)}, u32[]{:S(2)}) copy-start(f32[1024,256]{1,0:T(8,128)} %get-tuple-element.40.w_ref) | copy-start | bytes 3145732
  49.4 28.9 %copy-start.1 = (s32[32,32]{1,0:T(8,128)S(1)}, s32[32,32]{1,0:T(8,128)}, u32[]{:S(2)}) copy-start(s32[32,32]{1,0:T(8,128)} %fusion.2.base_ref) | copy-start | bytes 12292
  66.2 12.1 %all-to-all-start.2 = ((f32[32,8,128]{2,1,0:T(8,128)}), f32[32,8,128]{2,1,0:T(8,128)S(1)}, u32[]{:S(2)}, u32[]{:S(2)}) async-start(f32[32,8,128]{2,1,0:T(8,128)} %bitcast.17), calls=%async_computation.2 | async-start | bytes 262144 | tf_op jit(solution)/shard_map/all_to_all | solution.py:529
  69.7 23.9 %collective-permute-start.6 = (f32[8,2,16,240]{3,2,1,0:T(8,128)S(1)}, f32[8,2,16,240]{3,2,1,0:T(8,128)S(1)}, u32[]{:S(2)}, u32[]{:S(2)}) collective-permute-start(f32[8,2,16,240]{3,2,1,0:T(8,128)S(1)} %get-tuple-element.41), channel_id=1, source_target_pairs={{0,3},{1,0},{2,1},{3,2},{4,7},{5,4},{6,5},{7,6},{8,11},{9,8},{10,9... | collective-permute-start | bytes 737288 | tf_op jit(solution)/shard_map/ppermute | solution.py:538
  73.3 25.5 %collective-permute-start.7 = (f32[8,2,16,240]{3,2,1,0:T(8,128)S(1)}, f32[8,2,16,240]{3,2,1,0:T(8,128)}, u32[]{:S(2)}, u32[]{:S(2)}) collective-permute-start(f32[8,2,16,240]{3,2,1,0:T(8,128)S(1)} %get-tuple-element.42), channel_id=1, source_target_pairs={{0,2},{1,3},{2,0},{3,1},{4,6},{5,7},{6,4},{7,5},{8,10},{9,11},{10,... | collective-permute-start | bytes 737288 | tf_op jit(solution)/shard_map/ppermute | solution.py:538
  73.4 25.5 %collective-permute-start.8 = (f32[8,2,16,240]{3,2,1,0:T(8,128)S(1)}, f32[8,2,16,240]{3,2,1,0:T(8,128)}, u32[]{:S(2)}, u32[]{:S(2)}) collective-permute-start(f32[8,2,16,240]{3,2,1,0:T(8,128)S(1)} %get-tuple-element.43), channel_id=1, source_target_pairs={{0,1},{1,2},{2,3},{3,0},{4,5},{5,6},{6,7},{7,4},{8,9},{9,10},{10,1... | collective-permute-start | bytes 737288 | tf_op jit(solution)/shard_map/ppermute | solution.py:538

commit v9 on v8

--- a/solution.py
+++ b/solution.py
@@ -272,11 +272,24 @@
     chunks = [pl.ds(i * CHUNK, CHUNK) for i in range(rows // CHUNK)]
 
     def gather(f):
-        table = jnp.concatenate(split(gains[f], 3), axis=0)
-        spec[f] = jnp.where(facet_of == f, value, 0.0).astype(bf16)
-        a_s[f] = mm(first3, table)
-        b_s[f] = mm(second3, table)
-        m_s[f] = mm(d3, spec[f])
+        tables = {}
+
+        def prepare():
+            tables["gains"] = jnp.concatenate(split(gains[f], 3), axis=0)
+            spec[f] = jnp.where(facet_of == f, value, 0.0).astype(bf16)
+
+        def product(ref, left, lanes):
+            def run():
+                right = spec[f, :, lanes] if left is d3 else tables["gains"][:, lanes]
+                ref[f, :, lanes] = mm(left, right)
+
+            return run
+
+        pieces = [prepare]
+        for ref, left in ((a_s, first3), (b_s, second3), (m_s, d3)):
+            for lanes in (slice(0, half), slice(half, wide)):
+                pieces.append(product(ref, left, lanes))
+        return pieces
 
     def load(f, at):
         return (
@@ -285,8 +298,10 @@
             m_s[f, at, :half], m_s[f, at, half:],
         )
 
-    def predict(f):
-        for at in chunks:
+    def predict(f, waiting):
+        for i, at in enumerate(chunks):
+            if waiting and i % 4 == 0:
+                waiting.pop(0)()
             a_re, a_im, b_re, b_im, m_re, m_im = load(f, at)
             p_re = a_re * b_re + a_im * b_im
             p_im = a_im * b_re - a_re * b_im
@@ -296,12 +311,13 @@
             e_s[at, half:] += p_re * m_im + p_im * m_re
 
     e_s[...] = -vis_ref[...].astype(f32)
-    gather(0)
-
+    for run in gather(0):
+        run()
     for f in range(facets):
-        if f + 1 < facets:
-            gather(f + 1)
-        predict(f)
+        waiting = gather(f + 1) if f + 1 < facets else []
+        predict(f, waiting)
+        for run in waiting:
+            run()
     e_s[...] = e_s[...] * cols[:, 4:5]
 
     block = min(rows, 128)
@@ -350,8 +366,7 @@
 
         def plane_sum(ref):
             def run():
-                term = mm_nt(ref[here, :], spec[f, :planes, :])
-                parts[c] = term if parts[c] is None else parts[c] + term
+                parts[c] = parts[c] + mm_nt(ref[here, :], spec[f, :planes, :])
 
             return run
 
@@ -360,24 +375,47 @@
             station(1, glr_lo), plane_sum(gm_hi), plane_sum(gm_lo),
         ]
 
-    def grads(f, grad_degrid):
-        sums, parts, waiting = [None, None], [None] * block_count, []
+    def put_out(f, sums):
+        for k in range(group_count):
+            for x in range(2):
+                out_refs[k][f, x] = sums[x][k * group : (k + 1) * group, :channels]
+
+    last = block_count - 1
+
+    def grads(f, carry):
+        old_sums, parts = list(carry[0]), list(carry[1])
+        before = jnp.maximum(f - 1, 0)
+        sums = [None, None]
+        waiting = matmul_parts(before, last, old_sums, parts)
         for c in range(block_count):
             for i in range(block // CHUNK):
                 vector_part(f, c, i)
+                if c == 0 and i == 0:
+                    continue
                 if waiting:
                     waiting.pop(0)()
             for run in waiting:
                 run()
-            waiting = matmul_parts(f, c, sums, parts)
-        for run in waiting:
-            run()
-        for k in range(group_count):
-            for x in range(2):
-                out_refs[k][f, x] = sums[x][k * group : (k + 1) * group, :channels]
-        return grad_degrid + jnp.concatenate(parts, axis=0)
-
-    grad_degrid = lax.fori_loop(0, facets, grads, jnp.zeros((rows, planes), f32))
+            if c == 0:
+                put_out(before, old_sums)
+            waiting = matmul_parts(f, c, sums, parts) if c < last else []
+        return tuple(sums), tuple(parts)
+
+    tail_wide, tail = pl.ds(2 * last * block, 2 * block), pl.ds(last * block, block)
+    for ref in (glr_hi, glr_lo):
+        ref[tail_wide, :] = jnp.zeros((2 * block, wide), bf16)
+    for ref in (gm_hi, gm_lo):
+        ref[tail, :] = jnp.zeros((block, wide), bf16)
+    no_sum = jnp.zeros((stations, half), f32)
+    no_part = jnp.zeros((block, planes), f32)
+    sums, parts = lax.fori_loop(
+        0, facets, grads, ((no_sum, no_sum), (no_part,) * block_count)
+    )
+    sums, parts = list(sums), list(parts)
+    for run in matmul_parts(facets - 1, last, sums, parts):
+        run()
+    put_out(facets - 1, sums)
+    grad_degrid = jnp.concatenate(parts, axis=0)
     grad3 = jnp.concatenate(split(grad_degrid * term_scale, 3), axis=1)
     spread = as_bf16(
         mod(iota((3 * planes, LANES), 0), planes) == mod(iota((3 * planes, LANES), 1), planes)
@@ -546,6 +584,7 @@
     part = facets // 2
     early = [turn_gains(gain_first, k) for k in near]
     early += [turn_gains(gain_first[:part], k) for k in far]
+    below = lax.ppermute(gain_first, "tm", [(i, i + 1) for i in range(time_count - 1)])
     base = received.reshape(n, lines * LANES)[:, (taps + 1) * cap : (taps + 2) * cap]
     base = jnp.clip(base.T.astype(i32), 0, tiles - 2) * terms
     slot_lines = n * cap * planes // LANES
@@ -570,9 +609,10 @@
         cost_estimate=cost(10**8, 7 * 10**7),
         name="degrid",
     )(base, received, sky)
-    values, gain_here, *early = lax.optimization_barrier((values, gain_turned, *early))
+    values, gain_here, below, *early = lax.optimization_barrier(
+        (values, gain_turned, below, *early)
+    )
     back = exchange(values)
-    below = lax.ppermute(gain_here, "tm", [(i, i + 1) for i in range(time_count - 1)])
     above = lax.ppermute(gain_here, "tm", [(i + 1, i) for i in range(time_count - 1)])
     late = [turn_gains(gain_here[part:], k) for k in far]
     gathered = [gain_turned, *early, *late]

time: 101 us -> 102 us (level)
  waiting for transfers between devices: 11.3 us -> 12.6 us
  starting transfers between devices: 36.5 us -> 35.4 us
    ppermute x1, starting transfers between devices: 3.73 us -> 1.5 us  [body(): lax.ppermute(gain_first, 'tm', [(i, i + 1) for i in range(time_count - 1)])]
    ppermute x7, waiting for transfers between devices: 7.49 us -> 9.09 us  [turn_gains(): lax.ppermute(x, 'bl', [(i, (i + k) % group_count) for i in range(group_co...]
    all_to_all x3, starting transfers between devices: 16.5 us -> 17.6 us  [exchange(): x = lax.all_to_all(x, both, split_axis=0, concat_axis=0, tiled=True)]
    unnamed x22 -> x24, local copies, waits for them, and re-layouts: 2.11 us -> 2.12 us
  transfers between devices with their start and end apart: 12 -> 12, of which waited for: 4 -> 5; matrix products, arithmetic and copies ran while one was open for 3% -> 3% of each run, Pallas kernels for 43% -> 44%
where the time goes in v9:
time: 102 us
  Pallas kernels  46.6 us (46%)
  starting transfers between devices  35.4 us (35%)
  waiting for transfers between devices  12.6 us (12%)
  local copies, waits for them, and re-layouts  3.32 us (3%)
  other arithmetic  2.95 us (3%)
    pallas_call x1, Pallas kernels, body(): pl.pallas_call(functools.partial(rows_kernel, n, cap, group_count), out_s...  17.6 us
    all_to_all x3, starting transfers between devices, exchange(): x = lax.all_to_all(x, both, split_axis=0, concat_axis=0, tiled=True)  17.6 us
    pallas_call x1, Pallas kernels, body(): pl.pallas_call(functools.partial(scatter_kernel, n, cap), out_shape=jax.S...  15.1 us
    ppermute x7, starting transfers between devices, turn_gains(): lax.ppermute(x, 'bl', [(i, (i + k) % group_count) for i in range(group_co...  15 us
    pallas_call x1, Pallas kernels, body(): pl.pallas_call(functools.partial(degrid_kernel, n, cap, taps), out_shape=...  11.7 us
    ppermute x7, waiting for transfers between devices, turn_gains(): lax.ppermute(x, 'bl', [(i, (i + k) % group_count) for i in range(group_co...  9.09 us
    all_to_all x3, waiting for transfers between devices, exchange(): x = lax.all_to_all(x, both, split_axis=0, concat_axis=0, tiled=True)  3.47 us
    pallas_call x1, Pallas kernels, body(): pl.pallas_call(functools.partial(slots_kernel, n, cap, tiles, group, grou...  2.22 us
  transfers between devices with their start and end apart: 12, of which 5 were waited for; matrix products, arithmetic and copies ran while one was open for 3% of the time, Pallas kernels for 44%

profile of v9, /device:TPU:0, one launch (start us, length us, event | category | flops | bytes accessed | tf_op | source)
XLA Modules:
  0.0 101.7 jit_solution(3407962848261654594)
XLA Ops:
  0.6 0.0 copy-start.7
  0.6 1.2 %copy.28 = f32[1,16,8,2,240]{4,1,3,2,0:T(8,128)S(1)} copy(f32[1,16,8,2,240]{4,3,2,1,0:T(2,128)} %param.16) | data formatting | bytes 491520 | tf_op args[7]
  1.8 0.0 copy-start.4
  1.8 2.2 %slots.1 = (f32[128,128]{1,0:T(8,128)}, f32[8,512]{1,0:T(8,128)}, f32[512,8]{1,0:T(8,128)}) custom-call(s32[1]{0:T(128)} %bitcast.shift_ref, s32[1,512]{1,0:T(1,128)} %bitcast.52, s32[1,512]{1,0:T(1,128)} %bitcast.53, f32[8,512]{1,0:T(8,128)} %taps_ref.1, s32[2,512]{1,0:T(2,128)} %pairs_ref.1, f32[1,512]{1,0:T(1,128)} %bitcast.54, s32[1,512]{1,0:T(1,128)} %bitcast.55), custom_call_target="tpu_custom_call" | custom-call | flops 1000000000 | bytes 1000000 | tf_op jit(solution)/shard_map/slots/pallas_call | solution.py:543
  4.0 7.3 %all-to-all-start = ((f32[32,4,128]{2,1,0:T(4,128)}), f32[32,4,128]{2,1,0:T(4,128)S(1)}, u32[]{:S(2)}, u32[]{:S(2)}) async-start(f32[32,4,128]{2,1,0:T(4,128)} %bitcast.51), calls=%async_computation | async-start | bytes 131072 | tf_op jit(solution)/shard_map/all_to_all | solution.py:567
  11.3 2.7 %collective-permute-start.2 = (f32[8,2,16,240]{3,2,1,0:T(8,128)S(1)}, f32[8,2,16,240]{3,2,1,0:T(8,128)S(1)}, u32[]{:S(2)}, u32[]{:S(2)}) collective-permute-start(f32[8,2,16,240]{3,2,1,0:T(8,128)S(1)} %bitcast.41), channel_id=1, source_target_pairs={{0,2},{1,3},{2,0},{3,1},{4,6},{5,7},{6,4},{7,5},{8,10},{9,11},{10,... | collective-permute-start | bytes 737288 | tf_op jit(solution)/shard_map/ppermute | solution.py:576
  14.1 1.5 %collective-permute-start.1 = (f32[8,2,16,240]{3,2,1,0:T(8,128)S(1)}, f32[8,2,16,240]{3,2,1,0:T(8,128)S(1)}, u32[]{:S(2)}, u32[]{:S(2)}) collective-permute-start(f32[8,2,16,240]{3,2,1,0:T(8,128)S(1)} %bitcast.42), channel_id=1, source_target_pairs={{0,1},{1,2},{2,3},{3,0},{4,5},{5,6},{6,7},{7,4},{8,9},{9,10},{10,1... | collective-permute-start | bytes 737288 | tf_op jit(solution)/shard_map/ppermute | solution.py:576
  15.6 1.5 %collective-permute-start = (f32[8,2,16,240]{3,2,1,0:T(8,128)S(1)}, f32[8,2,16,240]{3,2,1,0:T(8,128)S(1)}, u32[]{:S(2)}, u32[]{:S(2)}) collective-permute-start(f32[8,2,16,240]{3,2,1,0:T(8,128)S(1)} %bitcast.43), channel_id=1, source_target_pairs={{0,4},{4,8},{8,12},{12,16},{16,20},{20,24},{24,28},{1,5},{5,9},{9,... | collective-permute-start | bytes 737288 | tf_op jit(solution)/shard_map/ppermute | solution.py:587
  17.1 2.4 %collective-permute-start.3 = (f32[4,2,16,240]{3,2,1,0:T(8,128)S(1)}, f32[4,2,16,240]{3,2,1,0:T(8,128)S(1)}, u32[]{:S(2)}, u32[]{:S(2)}) collective-permute-start(f32[4,2,16,240]{3,2,1,0:T(8,128)S(1)} %slice.10), channel_id=1, source_target_pairs={{0,3},{1,0},{2,1},{3,2},{4,7},{5,4},{6,5},{7,6},{8,11},{9,8},{10,9... | collective-permute-start | bytes 368648 | tf_op jit(solution)/shard_map/ppermute | solution.py:576
  19.5 0.0 all-to-all-done
  19.5 0.1 copy.20
  19.6 0.6 fusion.2.base_ref
  20.2 0.0 copy-done.6
  20.2 11.7 %degrid.1 = (f32[256,128]{1,0:T(8,128)}, f32[1024,256]{1,0:T(8,128)}) custom-call(s32[32,32]{1,0:T(8,128)} %fusion.2.base_ref, f32[128,128]{1,0:T(8,128)} %bitcast.48, f32[16,2048,128]{2,1,0:T(8,128)} %bitcast.39), custom_call_target="tpu_custom_call" | custom-call | flops 100000000 | bytes 70000000 | tf_op jit(solution)/shard_map/degrid/pallas_call | solution.py:592
  31.9 0.0 collective-permute-done.3.rest_3_
  31.9 2.0 %collective-permute-done.2.rest_2_ = f32[8,2,16,240]{3,2,1,0:T(8,128)S(1)} collective-permute-done((f32[8,2,16,240]{3,2,1,0:T(8,128)S(1)}, f32[8,2,16,240]{3,2,1,0:T(8,128)S(1)}, u32[]{:S(2)}, u32[]{:S(2)}) %collective-permute-start.2) | collective-permute-done | bytes 245792 | tf_op jit(solution)/shard_map/ppermute | solution.py:576
  33.9 0.0 collective-permute-done.1.rest_1_
  33.9 0.0 collective-permute-done
  33.9 0.0 copy-start.8
  33.9 5.7 %all-to-all-start.1 = ((f32[32,8,128]{2,1,0:T(8,128)}), f32[32,8,128]{2,1,0:T(8,128)S(1)}, u32[]{:S(2)}, u32[]{:S(2)}) async-start(f32[32,8,128]{2,1,0:T(8,128)} %bitcast.50), calls=%async_computation.1 | async-start | bytes 262144 | tf_op jit(solution)/shard_map/all_to_all | solution.py:567
  39.6 3.7 %collective-permute-start.4 = (f32[4,2,16,240]{3,2,1,0:T(8,128)S(1)}, f32[4,2,16,240]{3,2,1,0:T(8,128)S(1)}, u32[]{:S(2)}, u32[]{:S(2)}) collective-permute-start(f32[4,2,16,240]{3,2,1,0:T(8,128)S(1)} %slice.11), channel_id=1, source_target_pairs={{0,3},{1,0},{2,1},{3,2},{4,7},{5,4},{6,5},{7,6},{8,11},{9,8},{10,9... | collective-permute-start | bytes 368648 | tf_op jit(solution)/shard_map/ppermute | solution.py:576
  43.3 0.0 copy-done.9
  43.3 0.0 copy-done.8
  43.3 0.0 copy-done.7
  43.3 1.0 %copy.24.vis_ref = bf16[512,512]{1,0:T(8,128)(2,1)} copy(bf16[512,512]{0,1:T(8,128)(2,1)S(1)} %bitcast.40) | data formatting | bytes 1048576 | tf_op jit(solution)/shard_map/reshape | solution.py:620
  44.4 1.3 %collective-permute-start.5 = (f32[8,2,16,240]{3,2,1,0:T(8,128)S(1)}, f32[8,2,16,240]{3,2,1,0:T(8,128)}, u32[]{:S(2)}, u32[]{:S(2)}) collective-permute-start(f32[8,2,16,240]{3,2,1,0:T(8,128)S(1)} %bitcast.46), channel_id=1, source_target_pairs={{4,0},{8,4},{12,8},{16,12},{20,16},{24,20},{28,24},{5,1},{9,5},{13... | collective-permute-start | bytes 737288 | tf_op jit(solution)/shard_map/ppermute | solution.py:616
  45.6 1.7 %collective-permute-done.4.rest_4_ = f32[4,2,16,240]{3,2,1,0:T(8,128)S(1)} collective-permute-done((f32[4,2,16,240]{3,2,1,0:T(8,128)S(1)}, f32[4,2,16,240]{3,2,1,0:T(8,128)S(1)}, u32[]{:S(2)}, u32[]{:S(2)}) %collective-permute-start.4) | collective-permute-done | bytes 122912 | tf_op jit(solution)/shard_map/ppermute | solution.py:576
  47.4 0.8 all-to-all-done.1
  48.2 0.0 copy-done.10
  48.2 0.0 copy-done.4
  48.2 0.0 copy-done.2
  48.2 0.0 copy-start.5
  48.3 0.0 copy-start
  48.3 17.6 %rowgrads.1 = (f32[8,2,16,240]{3,2,1,0:T(8,128)S(1)}, f32[8,2,16,240]{3,2,1,0:T(8,128)S(1)}, f32[8,2,16,240]{3,2,1,0:T(8,128)S(1)}, f32[8,2,16,240]{3,2,1,0:T(8,128)S(1)}, f32[256,128]{1,0:T(8,128)}) custom-call(f32[8,512]{1,0:T(8,128)S(1)} %copy-done.3, f32[512,8]{1,0:T(8,128)S(1)} %copy-done.2, bf16[512,512]{1,0:T(8,128)(2,1)} %copy.24.vis_ref, ...), custom_call_target="tpu_custom_call" | custom-call | flops 20000000000 | bytes 10000000 | tf_op jit(solution)/shard_map/rowgrads/pallas_call | solution.py:624
  65.9 4.6 %all-to-all-start.2 = ((f32[32,8,128]{2,1,0:T(8,128)}), f32[32,8,128]{2,1,0:T(8,128)S(1)}, u32[]{:S(2)}, u32[]{:S(2)}) async-start(f32[32,8,128]{2,1,0:T(8,128)} %bitcast.17), calls=%async_computation.2 | async-start | bytes 262144 | tf_op jit(solution)/shard_map/all_to_all | solution.py:567
  70.5 3.7 %collective-permute-start.6 = (f32[8,2,16,240]{3,2,1,0:T(8,128)S(1)}, f32[8,2,16,240]{3,2,1,0:T(8,128)S(1)}, u32[]{:S(2)}, u32[]{:S(2)}) collective-permute-start(f32[8,2,16,240]{3,2,1,0:T(8,128)S(1)} %get-tuple-element.43), channel_id=1, source_target_pairs={{0,3},{1,0},{2,1},{3,2},{4,7},{5,4},{6,5},{7,6},{8,11},{9,8},{10,9... | collective-permute-start | bytes 737288 | tf_op jit(solution)/shard_map/ppermute | solution.py:576
  74.2 0.0 collective-permute-start.7
  74.2 1.1 %collective-permute-start.8 = (f32[8,2,16,240]{3,2,1,0:T(8,128)S(1)}, f32[8,2,16,240]{3,2,1,0:T(8,128)}, u32[]{:S(2)}, u32[]{:S(2)}) collective-permute-start(f32[8,2,16,240]{3,2,1,0:T(8,128)S(1)} %get-tuple-element.45), channel_id=1, source_target_pairs={{0,1},{1,2},{2,3},{3,0},{4,5},{5,6},{6,7},{7,4},{8,9},{9,10},{10,1... | collective-permute-start | bytes 737288 | tf_op jit(solution)/shard_map/ppermute | solution.py:576
  75.3 0.0 collective-permute-done.5
  75.3 1.2 %multiply_add_fusion = f32[8,2,16,240]{3,2,1,0:T(8,128)S(1)} fusion(f32[8,2,16,240]{3,2,1,0:T(8,128)S(1)} %get-tuple-element.38, f32[8,2,16,240]{3,2,1,0:T(8,128)} %collective-permute-done.5, f32[8,2,16,240]{3,2,1,0:T(8,128)} %copy-done.8, pred[]{:T(512)S(6)} %lt.3, pred[]{:T(512)S(6)} %gt.3, f32[1,16,8,2,240]{4,3,2,1,0:T(2,128)S(1)} %copy-done.5), kind=kLoop, calls=%fused_computation.2 | loop fusion | flops 430080 | bytes 1228802 | tf_op jit(solution)/shard_map/add | solution.py:652
  76.5 2.6 %all-to-all-done.2 = f32[32,8,128]{2,1,0:T(8,128)S(1)} async-done(((f32[32,8,128]{2,1,0:T(8,128)}), f32[32,8,128]{2,1,0:T(8,128)S(1)}, u32[]{:S(2)}, u32[]{:S(2)}) %all-to-all-start.2) | async-done | bytes 131104 | tf_op jit(solution)/shard_map/all_to_all | solution.py:567
  79.2 0.0 copy-done
  79.2 15.1 %scatter.1 = f32[16,2048,128]{2,1,0:T(8,128)} custom-call(s32[32,32]{1,0:T(8,128)S(1)} %copy-done.1, f32[256,128]{1,0:T(8,128)S(1)} %bitcast.36, f32[1024,256]{1,0:T(8,128)S(1)} %copy-done), custom_call_target="tpu_custom_call" | custom-call | bytes 100000 | tf_op jit(solution)/shard_map/scatter/pallas_call | solution.py:655
  94.3 0.0 collective-permute-done.6
  94.3 5.4 %collective-permute-done.7 = f32[8,2,16,240]{3,2,1,0:T(8,128)} collective-permute-done((f32[8,2,16,240]{3,2,1,0:T(8,128)S(1)}, f32[8,2,16,240]{3,2,1,0:T(8,128)}, u32[]{:S(2)}, u32[]{:S(2)}) %collective-permute-start.7) | collective-permute-done | bytes 245792 | tf_op jit(solution)/shard_map/ppermute | solution.py:576
  99.7 0.0 collective-permute-done.8
  99.7 1.1 %add_bitcast_fusion = f32[1,16,8,2,240]{4,1,3,2,0:T(8,128)S(1)} fusion(f32[8,2,16,240]{3,2,1,0:T(8,128)} %collective-permute-done.8, f32[8,2,16,240]{3,2,1,0:T(8,128)} %collective-permute-done.7, f32[8,2,16,240]{3,2,1,0:T(8,128)S(1)} %multiply_add_fusion, f32[8,2,16,240]{3,2,1,0:T(8,128)S(1)} %collective-permute-done.6), kind=kLoop, calls=%fused_computation.1 | loop fusion | flops 184320 | bytes 1228800 | tf_op jit(solution)/shard_map/broadcast_in_dim | solution.py:678
  100.8 0.9 copy.23
  (12 shorter events, 0.1 us)
Async XLA Ops:
  0.6 42.7 %copy-start.7 = (bf16[512,2,240]{0,2,1:T(8,128)(2,1)S(1)}, bf16[512,2,240]{0,2,1:T(8,128)(2,1)}, u32[]{:S(2)}) copy-start(bf16[512,2,240]{0,2,1:T(8,128)(2,1)} %param.9) | copy-start | bytes 1474564
  1.8 46.4 %copy-start.4 = (f32[1,16,8,2,240]{4,1,3,2,0:T(8,128)}, f32[1,16,8,2,240]{4,1,3,2,0:T(8,128)S(1)}, u32[]{:S(2)}) copy-start(f32[1,16,8,2,240]{4,1,3,2,0:T(8,128)S(1)} %copy.28) | copy-start | bytes 737284
  4.0 44.2 %copy-start.2 = (f32[512,8]{1,0:T(8,128)S(1)}, f32[512,8]{1,0:T(8,128)}, u32[]{:S(2)}) copy-start(f32[512,8]{1,0:T(8,128)} %get-tuple-element.27.cols_ref) | copy-start | bytes 49156
  4.0 44.2 %copy-start.3 = (f32[8,512]{1,0:T(8,128)S(1)}, f32[8,512]{1,0:T(8,128)}, u32[]{:S(2)}) copy-start(f32[8,512]{1,0:T(8,128)} %get-tuple-element.26.rows_ref) | copy-start | bytes 49156
  4.0 15.4 %all-to-all-start = ((f32[32,4,128]{2,1,0:T(4,128)}), f32[32,4,128]{2,1,0:T(4,128)S(1)}, u32[]{:S(2)}, u32[]{:S(2)}) async-start(f32[32,4,128]{2,1,0:T(4,128)} %bitcast.51), calls=%async_computation | async-start | bytes 131072 | tf_op jit(solution)/shard_map/all_to_all | solution.py:567
  11.3 22.5 %collective-permute-start.2 = (f32[8,2,16,240]{3,2,1,0:T(8,128)S(1)}, f32[8,2,16,240]{3,2,1,0:T(8,128)S(1)}, u32[]{:S(2)}, u32[]{:S(2)}) collective-permute-start(f32[8,2,16,240]{3,2,1,0:T(8,128)S(1)} %bitcast.41), channel_id=1, source_target_pairs={{0,2},{1,3},{2,0},{3,1},{4,6},{5,7},{6,4},{7,5},{8,10},{9,11},{10,... | collective-permute-start | bytes 737288 | tf_op jit(solution)/shard_map/ppermute | solution.py:576
  14.1 19.8 %collective-permute-start.1 = (f32[8,2,16,240]{3,2,1,0:T(8,128)S(1)}, f32[8,2,16,240]{3,2,1,0:T(8,128)S(1)}, u32[]{:S(2)}, u32[]{:S(2)}) collective-permute-start(f32[8,2,16,240]{3,2,1,0:T(8,128)S(1)} %bitcast.42), channel_id=1, source_target_pairs={{0,1},{1,2},{2,3},{3,0},{4,5},{5,6},{6,7},{7,4},{8,9},{9,10},{10,1... | collective-permute-start | bytes 737288 | tf_op jit(solution)/shard_map/ppermute | solution.py:576
  15.6 18.3 %collective-permute-start = (f32[8,2,16,240]{3,2,1,0:T(8,128)S(1)}, f32[8,2,16,240]{3,2,1,0:T(8,128)S(1)}, u32[]{:S(2)}, u32[]{:S(2)}) collective-permute-start(f32[8,2,16,240]{3,2,1,0:T(8,128)S(1)} %bitcast.43), channel_id=1, source_target_pairs={{0,4},{4,8},{8,12},{12,16},{16,20},{20,24},{24,28},{1,5},{5,9},{9,... | collective-permute-start | bytes 737288 | tf_op jit(solution)/shard_map/ppermute | solution.py:587
  17.1 14.8 %collective-permute-start.3 = (f32[4,2,16,240]{3,2,1,0:T(8,128)S(1)}, f32[4,2,16,240]{3,2,1,0:T(8,128)S(1)}, u32[]{:S(2)}, u32[]{:S(2)}) collective-permute-start(f32[4,2,16,240]{3,2,1,0:T(8,128)S(1)} %slice.10), channel_id=1, source_target_pairs={{0,3},{1,0},{2,1},{3,2},{4,7},{5,4},{6,5},{7,6},{8,11},{9,8},{10,9... | collective-permute-start | bytes 368648 | tf_op jit(solution)/shard_map/ppermute | solution.py:576
  19.5 0.7 copy-start.6
  33.9 9.4 %copy-start.9 = (f32[8,2,16,240]{3,2,1,0:T(8,128)}, f32[8,2,16,240]{3,2,1,0:T(8,128)S(1)}, u32[]{:S(2)}) copy-start(f32[8,2,16,240]{3,2,1,0:T(8,128)S(1)} %collective-permute-done.2.rest_2_) | copy-start | bytes 737284
  33.9 14.3 %copy-start.10 = (f32[8,2,16,240]{3,2,1,0:T(8,128)}, f32[8,2,16,240]{3,2,1,0:T(8,128)S(1)}, u32[]{:S(2)}) copy-start(f32[8,2,16,240]{3,2,1,0:T(8,128)S(1)} %collective-permute-done.1.rest_1_) | copy-start | bytes 737284
  33.9 9.4 %copy-start.8 = (f32[8,2,16,240]{3,2,1,0:T(8,128)}, f32[8,2,16,240]{3,2,1,0:T(8,128)S(1)}, u32[]{:S(2)}) copy-start(f32[8,2,16,240]{3,2,1,0:T(8,128)S(1)} %collective-permute-done) | copy-start | bytes 737284
  33.9 14.3 %all-to-all-start.1 = ((f32[32,8,128]{2,1,0:T(8,128)}), f32[32,8,128]{2,1,0:T(8,128)S(1)}, u32[]{:S(2)}, u32[]{:S(2)}) async-start(f32[32,8,128]{2,1,0:T(8,128)} %bitcast.50), calls=%async_computation.1 | async-start | bytes 262144 | tf_op jit(solution)/shard_map/all_to_all | solution.py:567
  39.6 7.8 %collective-permute-start.4 = (f32[4,2,16,240]{3,2,1,0:T(8,128)S(1)}, f32[4,2,16,240]{3,2,1,0:T(8,128)S(1)}, u32[]{:S(2)}, u32[]{:S(2)}) collective-permute-start(f32[4,2,16,240]{3,2,1,0:T(8,128)S(1)} %slice.11), channel_id=1, source_target_pairs={{0,3},{1,0},{2,1},{3,2},{4,7},{5,4},{6,5},{7,6},{8,11},{9,8},{10,9... | collective-permute-start | bytes 368648 | tf_op jit(solution)/shard_map/ppermute | solution.py:576
  44.4 30.9 %collective-permute-start.5 = (f32[8,2,16,240]{3,2,1,0:T(8,128)S(1)}, f32[8,2,16,240]{3,2,1,0:T(8,128)}, u32[]{:S(2)}, u32[]{:S(2)}) collective-permute-start(f32[8,2,16,240]{3,2,1,0:T(8,128)S(1)} %bitcast.46), channel_id=1, source_target_pairs={{4,0},{8,4},{12,8},{16,12},{20,16},{24,20},{28,24},{5,1},{9,5},{13... | collective-permute-start | bytes 737288 | tf_op jit(solution)/shard_map/ppermute | solution.py:616
  48.2 27.1 %copy-start.5 = (f32[1,16,8,2,240]{4,3,2,1,0:T(2,128)S(1)}, f32[1,16,8,2,240]{4,3,2,1,0:T(2,128)}, u32[]{:S(2)}) copy-start(f32[1,16,8,2,240]{4,3,2,1,0:T(2,128)} %param.16) | copy-start | bytes 737284
  48.3 30.9 %copy-start = (f32[1024,256]{1,0:T(8,128)S(1)}, f32[1024,256]{1,0:T(8,128)}, u32[]{:S(2)}) copy-start(f32[1024,256]{1,0:T(8,128)} %get-tuple-element.42.w_ref) | copy-start | bytes 3145732
  48.3 30.9 %copy-start.1 = (s32[32,32]{1,0:T(8,128)S(1)}, s32[32,32]{1,0:T(8,128)}, u32[]{:S(2)}) copy-start(s32[32,32]{1,0:T(8,128)} %fusion.2.base_ref) | copy-start | bytes 12292
  65.9 13.3 %all-to-all-start.2 = ((f32[32,8,128]{2,1,0:T(8,128)}), f32[32,8,128]{2,1,0:T(8,128)S(1)}, u32[]{:S(2)}, u32[]{:S(2)}) async-start(f32[32,8,128]{2,1,0:T(8,128)} %bitcast.17), calls=%async_computation.2 | async-start | bytes 262144 | tf_op jit(solution)/shard_map/all_to_all | solution.py:567
  70.5 23.8 %collective-permute-start.6 = (f32[8,2,16,240]{3,2,1,0:T(8,128)S(1)}, f32[8,2,16,240]{3,2,1,0:T(8,128)S(1)}, u32[]{:S(2)}, u32[]{:S(2)}) collective-permute-start(f32[8,2,16,240]{3,2,1,0:T(8,128)S(1)} %get-tuple-element.43), channel_id=1, source_target_pairs={{0,3},{1,0},{2,1},{3,2},{4,7},{5,4},{6,5},{7,6},{8,11},{9,8},{10,9... | collective-permute-start | bytes 737288 | tf_op jit(solution)/shard_map/ppermute | solution.py:576
  74.2 25.5 %collective-permute-start.7 = (f32[8,2,16,240]{3,2,1,0:T(8,128)S(1)}, f32[8,2,16,240]{3,2,1,0:T(8,128)}, u32[]{:S(2)}, u32[]{:S(2)}) collective-permute-start(f32[8,2,16,240]{3,2,1,0:T(8,128)S(1)} %get-tuple-element.44), channel_id=1, source_target_pairs={{0,2},{1,3},{2,0},{3,1},{4,6},{5,7},{6,4},{7,5},{8,10},{9,11},{10,... | collective-permute-start | bytes 737288 | tf_op jit(solution)/shard_map/ppermute | solution.py:576
  74.2 25.5 %collective-permute-start.8 = (f32[8,2,16,240]{3,2,1,0:T(8,128)S(1)}, f32[8,2,16,240]{3,2,1,0:T(8,128)}, u32[]{:S(2)}, u32[]{:S(2)}) collective-permute-start(f32[8,2,16,240]{3,2,1,0:T(8,128)S(1)} %get-tuple-element.45), channel_id=1, source_target_pairs={{0,1},{1,2},{2,3},{3,0},{4,5},{5,6},{6,7},{7,4},{8,9},{9,10},{10,1... | collective-permute-start | bytes 737288 | tf_op jit(solution)/shard_map/ppermute | solution.py:576

commit v10 on v8

--- a/solution.py
+++ b/solution.py
@@ -543,9 +543,10 @@
     received = exchange(send)
     near = range(1, group_count // 2 + 1)
     far = range(group_count // 2 + 1, group_count)
-    part = facets // 2
+    part = facets * 3 // 4
     early = [turn_gains(gain_first, k) for k in near]
     early += [turn_gains(gain_first[:part], k) for k in far]
+    below = lax.ppermute(gain_first, "tm", [(i, i + 1) for i in range(time_count - 1)])
     base = received.reshape(n, lines * LANES)[:, (taps + 1) * cap : (taps + 2) * cap]
     base = jnp.clip(base.T.astype(i32), 0, tiles - 2) * terms
     slot_lines = n * cap * planes // LANES
@@ -570,11 +571,10 @@
         cost_estimate=cost(10**8, 7 * 10**7),
         name="degrid",
     )(base, received, sky)
-    values, gain_here, *early = lax.optimization_barrier((values, gain_turned, *early))
     back = exchange(values)
-    below = lax.ppermute(gain_here, "tm", [(i, i + 1) for i in range(time_count - 1)])
-    above = lax.ppermute(gain_here, "tm", [(i + 1, i) for i in range(time_count - 1)])
-    late = [turn_gains(gain_here[part:], k) for k in far]
+    gain_late, below, *early = lax.optimization_barrier((gain_first, below, *early))
+    late = [turn_gains(gain_late[part:], k) for k in far]
+    above = lax.ppermute(gain_late, "tm", [(i + 1, i) for i in range(time_count - 1)])
     gathered = [gain_turned, *early, *late]
 
     vis_wide = jnp.pad(visibilities, ((0, 0), (0, 0), (0, half - channels))).reshape(

time: 101 us -> 105 us (1.040)
  waiting for transfers between devices: 11.3 us -> 15.8 us
  starting transfers between devices: 36.5 us -> 35.1 us
    ppermute x7, waiting for transfers between devices: 7.49 us -> 11.1 us  [turn_gains(): lax.ppermute(x, 'bl', [(i, (i + k) % group_count) for i in range(group_co...]
    ppermute x2, starting transfers between devices: 5.01 us -> 2.78 us  [the longest x1 1.5 us: body(): lax.ppermute(gain_first, 'tm', [(i, i + 1) for i in range(time_count - 1)])]
    unnamed x22 -> x24, local copies, waits for them, and re-layouts: 2.11 us -> 2.84 us
  transfers between devices with their start and end apart: 12 -> 12, of which waited for: 4 -> 4; matrix products, arithmetic and copies ran while one was open for 3% -> 3% of each run, Pallas kernels for 43% -> 42%
where the time goes in v10:
time: 105 us; the launch traced here: 104 us
  Pallas kernels  45.6 us (43%)
  starting transfers between devices  35.1 us (33%)
  waiting for transfers between devices  15.8 us (15%)
  local copies, waits for them, and re-layouts  4.05 us (4%)
  other arithmetic  2.95 us (3%)
    pallas_call x1, Pallas kernels, body(): pl.pallas_call(functools.partial(rows_kernel, n, cap, group_count), out_s...  16.8 us
    all_to_all x3, starting transfers between devices, exchange(): x = lax.all_to_all(x, both, split_axis=0, concat_axis=0, tiled=True)  16.3 us
    ppermute x7, starting transfers between devices, turn_gains(): lax.ppermute(x, 'bl', [(i, (i + k) % group_count) for i in range(group_co...  16 us
    pallas_call x1, Pallas kernels, body(): pl.pallas_call(functools.partial(scatter_kernel, n, cap), out_shape=jax.S...  14.9 us
    pallas_call x1, Pallas kernels, body(): pl.pallas_call(functools.partial(degrid_kernel, n, cap, taps), out_shape=...  11.7 us
    ppermute x7, waiting for transfers between devices, turn_gains(): lax.ppermute(x, 'bl', [(i, (i + k) % group_count) for i in range(group_co...  11.1 us
    all_to_all x3, waiting for transfers between devices, exchange(): x = lax.all_to_all(x, both, split_axis=0, concat_axis=0, tiled=True)  4.71 us
    unnamed x24, local copies, waits for them, and re-layouts  2.84 us
  transfers between devices with their start and end apart: 12, of which 4 were waited for; matrix products, arithmetic and copies ran while one was open for 3% of the time, Pallas kernels for 42%

profile of v10, /device:TPU:0, one launch (start us, length us, event | category | flops | bytes accessed | tf_op | source)
XLA Modules:
  0.0 104.3 jit_solution(11405362613199757428)
XLA Ops:
  0.6 0.0 copy-start.7
  0.6 1.2 %copy.28 = f32[1,16,8,2,240]{4,1,3,2,0:T(8,128)S(1)} copy(f32[1,16,8,2,240]{4,3,2,1,0:T(2,128)} %param.16) | data formatting | bytes 491520 | tf_op args[7]
  1.8 0.0 copy-start.4
  1.8 2.2 %slots.1 = (f32[128,128]{1,0:T(8,128)}, f32[8,512]{1,0:T(8,128)}, f32[512,8]{1,0:T(8,128)}) custom-call(s32[1]{0:T(128)} %bitcast.shift_ref, s32[1,512]{1,0:T(1,128)} %bitcast.52, s32[1,512]{1,0:T(1,128)} %bitcast.53, f32[8,512]{1,0:T(8,128)} %taps_ref.1, s32[2,512]{1,0:T(2,128)} %pairs_ref.1, f32[1,512]{1,0:T(1,128)} %bitcast.54, s32[1,512]{1,0:T(1,128)} %bitcast.55), custom_call_target="tpu_custom_call" | custom-call | flops 1000000000 | bytes 1000000 | tf_op jit(solution)/shard_map/slots/pallas_call | solution.py:505
  4.0 7.3 %all-to-all-start = ((f32[32,4,128]{2,1,0:T(4,128)}), f32[32,4,128]{2,1,0:T(4,128)S(1)}, u32[]{:S(2)}, u32[]{:S(2)}) async-start(f32[32,4,128]{2,1,0:T(4,128)} %bitcast.51), calls=%async_computation | async-start | bytes 131072 | tf_op jit(solution)/shard_map/all_to_all | solution.py:529
  11.3 2.7 %collective-permute-start.2 = (f32[8,2,16,240]{3,2,1,0:T(8,128)S(1)}, f32[8,2,16,240]{3,2,1,0:T(8,128)S(1)}, u32[]{:S(2)}, u32[]{:S(2)}) collective-permute-start(f32[8,2,16,240]{3,2,1,0:T(8,128)S(1)} %bitcast.41), channel_id=1, source_target_pairs={{0,2},{1,3},{2,0},{3,1},{4,6},{5,7},{6,4},{7,5},{8,10},{9,11},{10,... | collective-permute-start | bytes 737288 | tf_op jit(solution)/shard_map/ppermute | solution.py:538
  14.1 1.5 %collective-permute-start.1 = (f32[8,2,16,240]{3,2,1,0:T(8,128)S(1)}, f32[8,2,16,240]{3,2,1,0:T(8,128)S(1)}, u32[]{:S(2)}, u32[]{:S(2)}) collective-permute-start(f32[8,2,16,240]{3,2,1,0:T(8,128)S(1)} %bitcast.42), channel_id=1, source_target_pairs={{0,1},{1,2},{2,3},{3,0},{4,5},{5,6},{6,7},{7,4},{8,9},{9,10},{10,1... | collective-permute-start | bytes 737288 | tf_op jit(solution)/shard_map/ppermute | solution.py:538
  15.6 1.5 %collective-permute-start = (f32[8,2,16,240]{3,2,1,0:T(8,128)S(1)}, f32[8,2,16,240]{3,2,1,0:T(8,128)S(1)}, u32[]{:S(2)}, u32[]{:S(2)}) collective-permute-start(f32[8,2,16,240]{3,2,1,0:T(8,128)S(1)} %bitcast.43), channel_id=1, source_target_pairs={{0,4},{4,8},{8,12},{12,16},{16,20},{20,24},{24,28},{1,5},{5,9},{9,... | collective-permute-start | bytes 737288 | tf_op jit(solution)/shard_map/ppermute | solution.py:549
  17.1 2.1 %all-to-all-done = f32[32,4,128]{2,1,0:T(4,128)S(1)} async-done(((f32[32,4,128]{2,1,0:T(4,128)}), f32[32,4,128]{2,1,0:T(4,128)S(1)}, u32[]{:S(2)}, u32[]{:S(2)}) %all-to-all-start) | async-done | bytes 65568 | tf_op jit(solution)/shard_map/all_to_all | solution.py:529
  19.2 0.1 copy.20
  19.3 0.6 fusion.2.base_ref
  19.9 0.0 copy-done.6
  19.9 11.7 %degrid.1 = (f32[256,128]{1,0:T(8,128)}, f32[1024,256]{1,0:T(8,128)}) custom-call(s32[32,32]{1,0:T(8,128)} %fusion.2.base_ref, f32[128,128]{1,0:T(8,128)} %bitcast.48, f32[16,2048,128]{2,1,0:T(8,128)} %bitcast.39), custom_call_target="tpu_custom_call" | custom-call | flops 100000000 | bytes 70000000 | tf_op jit(solution)/shard_map/degrid/pallas_call | solution.py:554
  31.6 3.1 %all-to-all-start.1 = ((f32[32,8,128]{2,1,0:T(8,128)}), f32[32,8,128]{2,1,0:T(8,128)S(1)}, u32[]{:S(2)}, u32[]{:S(2)}) async-start(f32[32,8,128]{2,1,0:T(8,128)} %bitcast.50), calls=%async_computation.1 | async-start | bytes 262144 | tf_op jit(solution)/shard_map/all_to_all | solution.py:529
  34.8 3.7 %collective-permute-start.3 = (f32[6,2,16,240]{3,2,1,0:T(8,128)S(1)}, f32[6,2,16,240]{3,2,1,0:T(8,128)S(1)}, u32[]{:S(2)}, u32[]{:S(2)}) collective-permute-start(f32[6,2,16,240]{3,2,1,0:T(8,128)S(1)} %slice.10), channel_id=1, source_target_pairs={{0,3},{1,0},{2,1},{3,2},{4,7},{5,4},{6,5},{7,6},{8,11},{9,8},{10,9... | collective-permute-start | bytes 552968 | tf_op jit(solution)/shard_map/ppermute | solution.py:538
  38.5 5.5 %collective-permute-done.3.rest_3_ = f32[6,2,16,240]{3,2,1,0:T(8,128)S(1)} collective-permute-done((f32[6,2,16,240]{3,2,1,0:T(8,128)S(1)}, f32[6,2,16,240]{3,2,1,0:T(8,128)S(1)}, u32[]{:S(2)}, u32[]{:S(2)}) %collective-permute-start.3) | collective-permute-done | bytes 184352 | tf_op jit(solution)/shard_map/ppermute | solution.py:538
  43.9 0.0 collective-permute-done.2.rest_2_
  43.9 0.0 collective-permute-done.1.rest_1_
  44.0 0.7 copy-done.9
  44.7 0.0 collective-permute-done
  44.7 3.3 %collective-permute-start.4 = (f32[2,2,16,240]{3,2,1,0:T(8,128)S(1)}, f32[2,2,16,240]{3,2,1,0:T(8,128)S(1)}, u32[]{:S(2)}, u32[]{:S(2)}) collective-permute-start(f32[2,2,16,240]{3,2,1,0:T(8,128)S(1)} %slice.11), channel_id=1, source_target_pairs={{0,3},{1,0},{2,1},{3,2},{4,7},{5,4},{6,5},{7,6},{8,11},{9,8},{10,9... | collective-permute-start | bytes 184328 | tf_op jit(solution)/shard_map/ppermute | solution.py:538
  48.0 0.0 copy-done.10
  48.0 0.0 copy-done.8
  48.0 0.0 copy-done.7
  48.1 1.0 copy.24.vis_ref
  49.1 1.3 %collective-permute-start.5 = (f32[8,2,16,240]{3,2,1,0:T(8,128)S(1)}, f32[8,2,16,240]{3,2,1,0:T(8,128)}, u32[]{:S(2)}, u32[]{:S(2)}) collective-permute-start(f32[8,2,16,240]{3,2,1,0:T(8,128)S(1)} %bitcast.46), channel_id=1, source_target_pairs={{4,0},{8,4},{12,8},{16,12},{20,16},{24,20},{28,24},{5,1},{9,5},{13... | collective-permute-start | bytes 737288 | tf_op jit(solution)/shard_map/ppermute | solution.py:577
  50.4 0.0 collective-permute-done.4.rest_4_
  50.4 0.0 all-to-all-done.1
  50.4 0.0 copy-done.4
  50.4 0.0 copy-done.2
  50.4 0.0 copy-done.3
  50.4 0.0 copy-start.5
  50.4 0.0 copy-start
  50.4 0.0 copy-start.1
  50.5 16.8 %rowgrads.1 = (f32[8,2,16,240]{3,2,1,0:T(8,128)S(1)}, f32[8,2,16,240]{3,2,1,0:T(8,128)S(1)}, f32[8,2,16,240]{3,2,1,0:T(8,128)S(1)}, f32[8,2,16,240]{3,2,1,0:T(8,128)S(1)}, f32[256,128]{1,0:T(8,128)}) custom-call(f32[8,512]{1,0:T(8,128)S(1)} %copy-done.3, f32[512,8]{1,0:T(8,128)S(1)} %copy-done.2, bf16[512,512]{1,0:T(8,128)(2,1)} %copy.24.vis_ref, ...), custom_call_target="tpu_custom_call" | custom-call | flops 20000000000 | bytes 10000000 | tf_op jit(solution)/shard_map/rowgrads/pallas_call | solution.py:584
  67.2 5.9 %all-to-all-start.2 = ((f32[32,8,128]{2,1,0:T(8,128)}), f32[32,8,128]{2,1,0:T(8,128)S(1)}, u32[]{:S(2)}, u32[]{:S(2)}) async-start(f32[32,8,128]{2,1,0:T(8,128)} %bitcast.17), calls=%async_computation.2 | async-start | bytes 262144 | tf_op jit(solution)/shard_map/all_to_all | solution.py:529
  73.1 3.7 %collective-permute-start.6 = (f32[8,2,16,240]{3,2,1,0:T(8,128)S(1)}, f32[8,2,16,240]{3,2,1,0:T(8,128)S(1)}, u32[]{:S(2)}, u32[]{:S(2)}) collective-permute-start(f32[8,2,16,240]{3,2,1,0:T(8,128)S(1)} %get-tuple-element.41), channel_id=1, source_target_pairs={{0,3},{1,0},{2,1},{3,2},{4,7},{5,4},{6,5},{7,6},{8,11},{9,8},{10,9... | collective-permute-start | bytes 737288 | tf_op jit(solution)/shard_map/ppermute | solution.py:538
  76.8 0.0 collective-permute-start.7
  76.8 1.1 %collective-permute-start.8 = (f32[8,2,16,240]{3,2,1,0:T(8,128)S(1)}, f32[8,2,16,240]{3,2,1,0:T(8,128)}, u32[]{:S(2)}, u32[]{:S(2)}) collective-permute-start(f32[8,2,16,240]{3,2,1,0:T(8,128)S(1)} %get-tuple-element.43), channel_id=1, source_target_pairs={{0,1},{1,2},{2,3},{3,0},{4,5},{5,6},{6,7},{7,4},{8,9},{9,10},{10,1... | collective-permute-start | bytes 737288 | tf_op jit(solution)/shard_map/ppermute | solution.py:538
  77.9 0.0 collective-permute-done.5
  77.9 1.2 %multiply_add_fusion = f32[8,2,16,240]{3,2,1,0:T(8,128)S(1)} fusion(f32[8,2,16,240]{3,2,1,0:T(8,128)S(1)} %get-tuple-element.36, f32[8,2,16,240]{3,2,1,0:T(8,128)} %collective-permute-done.5, f32[8,2,16,240]{3,2,1,0:T(8,128)} %copy-done.8, pred[]{:T(512)S(6)} %lt.3, pred[]{:T(512)S(6)} %gt.3, f32[1,16,8,2,240]{4,3,2,1,0:T(2,128)S(1)} %copy-done.5), kind=kLoop, calls=%fused_computation.2 | loop fusion | flops 430080 | bytes 1228802 | tf_op jit(solution)/shard_map/add | solution.py:612
  79.1 2.6 %all-to-all-done.2 = f32[32,8,128]{2,1,0:T(8,128)S(1)} async-done(((f32[32,8,128]{2,1,0:T(8,128)}), f32[32,8,128]{2,1,0:T(8,128)S(1)}, u32[]{:S(2)}, u32[]{:S(2)}) %all-to-all-start.2) | async-done | bytes 131104 | tf_op jit(solution)/shard_map/all_to_all | solution.py:529
  81.7 14.9 %scatter.1 = f32[16,2048,128]{2,1,0:T(8,128)} custom-call(s32[32,32]{1,0:T(8,128)S(1)} %copy-done.1, f32[256,128]{1,0:T(8,128)S(1)} %bitcast.36, f32[1024,256]{1,0:T(8,128)S(1)} %copy-done), custom_call_target="tpu_custom_call" | custom-call | bytes 100000 | tf_op jit(solution)/shard_map/scatter/pallas_call | solution.py:615
  96.7 0.0 collective-permute-done.6
  96.7 5.6 %collective-permute-done.7 = f32[8,2,16,240]{3,2,1,0:T(8,128)} collective-permute-done((f32[8,2,16,240]{3,2,1,0:T(8,128)S(1)}, f32[8,2,16,240]{3,2,1,0:T(8,128)}, u32[]{:S(2)}, u32[]{:S(2)}) %collective-permute-start.7) | collective-permute-done | bytes 245792 | tf_op jit(solution)/shard_map/ppermute | solution.py:538
  102.3 0.0 collective-permute-done.8
  102.3 1.1 %add_bitcast_fusion = f32[1,16,8,2,240]{4,1,3,2,0:T(8,128)S(1)} fusion(f32[8,2,16,240]{3,2,1,0:T(8,128)} %collective-permute-done.8, f32[8,2,16,240]{3,2,1,0:T(8,128)} %collective-permute-done.7, f32[8,2,16,240]{3,2,1,0:T(8,128)S(1)} %multiply_add_fusion, f32[8,2,16,240]{3,2,1,0:T(8,128)S(1)} %collective-permute-done.6), kind=kLoop, calls=%fused_computation.1 | loop fusion | flops 184320 | bytes 1228800 | tf_op jit(solution)/shard_map/broadcast_in_dim | solution.py:638
  103.4 0.9 copy.23
  (12 shorter events, 0.1 us)
Async XLA Ops:
  0.6 47.4 %copy-start.7 = (bf16[512,2,240]{0,2,1:T(8,128)(2,1)S(1)}, bf16[512,2,240]{0,2,1:T(8,128)(2,1)}, u32[]{:S(2)}) copy-start(bf16[512,2,240]{0,2,1:T(8,128)(2,1)} %param.9) | copy-start | bytes 1474564
  1.8 48.6 %copy-start.4 = (f32[1,16,8,2,240]{4,1,3,2,0:T(8,128)}, f32[1,16,8,2,240]{4,1,3,2,0:T(8,128)S(1)}, u32[]{:S(2)}) copy-start(f32[1,16,8,2,240]{4,1,3,2,0:T(8,128)S(1)} %copy.28) | copy-start | bytes 737284
  4.0 46.4 %copy-start.2 = (f32[512,8]{1,0:T(8,128)S(1)}, f32[512,8]{1,0:T(8,128)}, u32[]{:S(2)}) copy-start(f32[512,8]{1,0:T(8,128)} %get-tuple-element.26.cols_ref) | copy-start | bytes 49156
  4.0 46.4 %copy-start.3 = (f32[8,512]{1,0:T(8,128)S(1)}, f32[8,512]{1,0:T(8,128)}, u32[]{:S(2)}) copy-start(f32[8,512]{1,0:T(8,128)} %get-tuple-element.25.rows_ref) | copy-start | bytes 49156
  4.0 15.1 %all-to-all-start = ((f32[32,4,128]{2,1,0:T(4,128)}), f32[32,4,128]{2,1,0:T(4,128)S(1)}, u32[]{:S(2)}, u32[]{:S(2)}) async-start(f32[32,4,128]{2,1,0:T(4,128)} %bitcast.51), calls=%async_computation | async-start | bytes 131072 | tf_op jit(solution)/shard_map/all_to_all | solution.py:529
  11.3 32.6 %collective-permute-start.2 = (f32[8,2,16,240]{3,2,1,0:T(8,128)S(1)}, f32[8,2,16,240]{3,2,1,0:T(8,128)S(1)}, u32[]{:S(2)}, u32[]{:S(2)}) collective-permute-start(f32[8,2,16,240]{3,2,1,0:T(8,128)S(1)} %bitcast.41), channel_id=1, source_target_pairs={{0,2},{1,3},{2,0},{3,1},{4,6},{5,7},{6,4},{7,5},{8,10},{9,11},{10,... | collective-permute-start | bytes 737288 | tf_op jit(solution)/shard_map/ppermute | solution.py:538
  14.1 29.9 %collective-permute-start.1 = (f32[8,2,16,240]{3,2,1,0:T(8,128)S(1)}, f32[8,2,16,240]{3,2,1,0:T(8,128)S(1)}, u32[]{:S(2)}, u32[]{:S(2)}) collective-permute-start(f32[8,2,16,240]{3,2,1,0:T(8,128)S(1)} %bitcast.42), channel_id=1, source_target_pairs={{0,1},{1,2},{2,3},{3,0},{4,5},{5,6},{6,7},{7,4},{8,9},{9,10},{10,1... | collective-permute-start | bytes 737288 | tf_op jit(solution)/shard_map/ppermute | solution.py:538
  15.6 29.1 %collective-permute-start = (f32[8,2,16,240]{3,2,1,0:T(8,128)S(1)}, f32[8,2,16,240]{3,2,1,0:T(8,128)S(1)}, u32[]{:S(2)}, u32[]{:S(2)}) collective-permute-start(f32[8,2,16,240]{3,2,1,0:T(8,128)S(1)} %bitcast.43), channel_id=1, source_target_pairs={{0,4},{4,8},{8,12},{12,16},{16,20},{20,24},{24,28},{1,5},{5,9},{9,... | collective-permute-start | bytes 737288 | tf_op jit(solution)/shard_map/ppermute | solution.py:549
  19.2 0.7 copy-start.6
  31.6 18.7 %all-to-all-start.1 = ((f32[32,8,128]{2,1,0:T(8,128)}), f32[32,8,128]{2,1,0:T(8,128)S(1)}, u32[]{:S(2)}, u32[]{:S(2)}) async-start(f32[32,8,128]{2,1,0:T(8,128)} %bitcast.50), calls=%async_computation.1 | async-start | bytes 262144 | tf_op jit(solution)/shard_map/all_to_all | solution.py:529
  34.8 9.2 %collective-permute-start.3 = (f32[6,2,16,240]{3,2,1,0:T(8,128)S(1)}, f32[6,2,16,240]{3,2,1,0:T(8,128)S(1)}, u32[]{:S(2)}, u32[]{:S(2)}) collective-permute-start(f32[6,2,16,240]{3,2,1,0:T(8,128)S(1)} %slice.10), channel_id=1, source_target_pairs={{0,3},{1,0},{2,1},{3,2},{4,7},{5,4},{6,5},{7,6},{8,11},{9,8},{10,9... | collective-permute-start | bytes 552968 | tf_op jit(solution)/shard_map/ppermute | solution.py:538
  43.9 0.7 copy-start.9
  44.7 3.3 %copy-start.10 = (f32[8,2,16,240]{3,2,1,0:T(8,128)}, f32[8,2,16,240]{3,2,1,0:T(8,128)S(1)}, u32[]{:S(2)}) copy-start(f32[8,2,16,240]{3,2,1,0:T(8,128)S(1)} %collective-permute-done.1.rest_1_) | copy-start | bytes 737284
  44.7 3.3 %copy-start.8 = (f32[8,2,16,240]{3,2,1,0:T(8,128)}, f32[8,2,16,240]{3,2,1,0:T(8,128)S(1)}, u32[]{:S(2)}) copy-start(f32[8,2,16,240]{3,2,1,0:T(8,128)S(1)} %collective-permute-done) | copy-start | bytes 737284
  44.7 5.7 %collective-permute-start.4 = (f32[2,2,16,240]{3,2,1,0:T(8,128)S(1)}, f32[2,2,16,240]{3,2,1,0:T(8,128)S(1)}, u32[]{:S(2)}, u32[]{:S(2)}) collective-permute-start(f32[2,2,16,240]{3,2,1,0:T(8,128)S(1)} %slice.11), channel_id=1, source_target_pairs={{0,3},{1,0},{2,1},{3,2},{4,7},{5,4},{6,5},{7,6},{8,11},{9,8},{10,9... | collective-permute-start | bytes 184328 | tf_op jit(solution)/shard_map/ppermute | solution.py:538
  49.1 28.8 %collective-permute-start.5 = (f32[8,2,16,240]{3,2,1,0:T(8,128)S(1)}, f32[8,2,16,240]{3,2,1,0:T(8,128)}, u32[]{:S(2)}, u32[]{:S(2)}) collective-permute-start(f32[8,2,16,240]{3,2,1,0:T(8,128)S(1)} %bitcast.46), channel_id=1, source_target_pairs={{4,0},{8,4},{12,8},{16,12},{20,16},{24,20},{28,24},{5,1},{9,5},{13... | collective-permute-start | bytes 737288 | tf_op jit(solution)/shard_map/ppermute | solution.py:577
  50.4 27.5 %copy-start.5 = (f32[1,16,8,2,240]{4,3,2,1,0:T(2,128)S(1)}, f32[1,16,8,2,240]{4,3,2,1,0:T(2,128)}, u32[]{:S(2)}) copy-start(f32[1,16,8,2,240]{4,3,2,1,0:T(2,128)} %param.16) | copy-start | bytes 737284
  50.4 31.3 %copy-start = (f32[1024,256]{1,0:T(8,128)S(1)}, f32[1024,256]{1,0:T(8,128)}, u32[]{:S(2)}) copy-start(f32[1024,256]{1,0:T(8,128)} %get-tuple-element.40.w_ref) | copy-start | bytes 3145732
  50.4 31.3 %copy-start.1 = (s32[32,32]{1,0:T(8,128)S(1)}, s32[32,32]{1,0:T(8,128)}, u32[]{:S(2)}) copy-start(s32[32,32]{1,0:T(8,128)} %fusion.2.base_ref) | copy-start | bytes 12292
  67.2 14.5 %all-to-all-start.2 = ((f32[32,8,128]{2,1,0:T(8,128)}), f32[32,8,128]{2,1,0:T(8,128)S(1)}, u32[]{:S(2)}, u32[]{:S(2)}) async-start(f32[32,8,128]{2,1,0:T(8,128)} %bitcast.17), calls=%async_computation.2 | async-start | bytes 262144 | tf_op jit(solution)/shard_map/all_to_all | solution.py:529
  73.1 23.6 %collective-permute-start.6 = (f32[8,2,16,240]{3,2,1,0:T(8,128)S(1)}, f32[8,2,16,240]{3,2,1,0:T(8,128)S(1)}, u32[]{:S(2)}, u32[]{:S(2)}) collective-permute-start(f32[8,2,16,240]{3,2,1,0:T(8,128)S(1)} %get-tuple-element.41), channel_id=1, source_target_pairs={{0,3},{1,0},{2,1},{3,2},{4,7},{5,4},{6,5},{7,6},{8,11},{9,8},{10,9... | collective-permute-start | bytes 737288 | tf_op jit(solution)/shard_map/ppermute | solution.py:538
  76.8 25.5 %collective-permute-start.7 = (f32[8,2,16,240]{3,2,1,0:T(8,128)S(1)}, f32[8,2,16,240]{3,2,1,0:T(8,128)}, u32[]{:S(2)}, u32[]{:S(2)}) collective-permute-start(f32[8,2,16,240]{3,2,1,0:T(8,128)S(1)} %get-tuple-element.42), channel_id=1, source_target_pairs={{0,2},{1,3},{2,0},{3,1},{4,6},{5,7},{6,4},{7,5},{8,10},{9,11},{10,... | collective-permute-start | bytes 737288 | tf_op jit(solution)/shard_map/ppermute | solution.py:538
  76.8 25.5 %collective-permute-start.8 = (f32[8,2,16,240]{3,2,1,0:T(8,128)S(1)}, f32[8,2,16,240]{3,2,1,0:T(8,128)}, u32[]{:S(2)}, u32[]{:S(2)}) collective-permute-start(f32[8,2,16,240]{3,2,1,0:T(8,128)S(1)} %get-tuple-element.43), channel_id=1, source_target_pairs={{0,1},{1,2},{2,3},{3,0},{4,5},{5,6},{6,7},{7,4},{8,9},{9,10},{10,1... | collective-permute-start | bytes 737288 | tf_op jit(solution)/shard_map/ppermute | solution.py:538

commit v11 on v10

--- a/solution.py
+++ b/solution.py
@@ -220,8 +220,7 @@
     n, cap, group_count,
     rows_ref, cols_ref, vis_ref, back_ref, *rest,
 ):
-    far = group_count - group_count // 2 - 1
-    gain_refs, rest = rest[: group_count + far], rest[group_count + far :]
+    gain_refs, rest = rest[:group_count], rest[group_count:]
     out_refs, send_ref, rest = rest[:group_count], rest[group_count], rest[group_count + 1 :]
     gains, spec, a_s, b_s, m_s, p_s, e_s, glr_hi, glr_lo, gm_hi, gm_lo = rest
     facets, _, group, channels = gain_refs[0].shape
@@ -239,11 +238,8 @@
     for k in range(group_count):
         mine = slice(k * group, (k + 1) * group)
         for f in range(facets):
-            ref, at = gain_refs[k], f
-            if f >= ref.shape[0]:
-                ref, at = gain_refs[k + far], f - ref.shape[0]
             for x in range(2):
-                gains[f, mine, x * half : x * half + channels] = ref[at, x]
+                gains[f, mine, x * half : x * half + channels] = gain_refs[k][f, x]
 
     owner3 = as_bf16(mod(iota((1, 3 * n), 1), n) == owner_col)
     per_line = LANES // planes
@@ -543,9 +539,7 @@
     received = exchange(send)
     near = range(1, group_count // 2 + 1)
     far = range(group_count // 2 + 1, group_count)
-    part = facets * 3 // 4
     early = [turn_gains(gain_first, k) for k in near]
-    early += [turn_gains(gain_first[:part], k) for k in far]
     below = lax.ppermute(gain_first, "tm", [(i, i + 1) for i in range(time_count - 1)])
     base = received.reshape(n, lines * LANES)[:, (taps + 1) * cap : (taps + 2) * cap]
     base = jnp.clip(base.T.astype(i32), 0, tiles - 2) * terms
@@ -573,7 +567,7 @@
     )(base, received, sky)
     back = exchange(values)
     gain_late, below, *early = lax.optimization_barrier((gain_first, below, *early))
-    late = [turn_gains(gain_late[part:], k) for k in far]
+    late = [turn_gains(gain_late, k) for k in far]
     above = lax.ppermute(gain_late, "tm", [(i + 1, i) for i in range(time_count - 1)])
     gathered = [gain_turned, *early, *late]
 

time: 105 us -> 99.8 us (0.950)
  starting transfers between devices: 35.1 us -> 31.2 us
    ppermute x7 -> x6, starting transfers between devices: 16 us -> 12.7 us  [turn_gains(): lax.ppermute(x, 'bl', [(i, (i + k) % group_count) for i in range(group_co...]
    ppermute x7 -> x6, waiting for transfers between devices: 11.1 us -> 8.04 us  [turn_gains(): lax.ppermute(x, 'bl', [(i, (i + k) % group_count) for i in range(group_co...]
    all_to_all x3, waiting for transfers between devices: 4.71 us -> 7.23 us  [exchange(): x = lax.all_to_all(x, both, split_axis=0, concat_axis=0, tiled=True)]
  transfers between devices with their start and end apart: 12 -> 11, of which waited for: 4 -> 5; matrix products, arithmetic and copies ran while one was open for 3% -> 3% of each run, Pallas kernels for 42% -> 43%
where the time goes in v11:
time: 99.8 us; the launch traced here: 99.3 us
  Pallas kernels  45.1 us (45%)
  starting transfers between devices  31.2 us (31%)
  waiting for transfers between devices  15.3 us (15%)
  local copies, waits for them, and re-layouts  4.01 us (4%)
  other arithmetic  2.88 us (3%)
    pallas_call x1, Pallas kernels, body(): pl.pallas_call(functools.partial(rows_kernel, n, cap, group_count), out_s...  16.8 us
    all_to_all x3, starting transfers between devices, exchange(): x = lax.all_to_all(x, both, split_axis=0, concat_axis=0, tiled=True)  15.8 us
    pallas_call x1, Pallas kernels, body(): pl.pallas_call(functools.partial(scatter_kernel, n, cap), out_shape=jax.S...  14.3 us
    ppermute x6, starting transfers between devices, turn_gains(): lax.ppermute(x, 'bl', [(i, (i + k) % group_count) for i in range(group_co...  12.7 us
    pallas_call x1, Pallas kernels, body(): pl.pallas_call(functools.partial(degrid_kernel, n, cap, taps), out_shape=...  11.9 us
    ppermute x6, waiting for transfers between devices, turn_gains(): lax.ppermute(x, 'bl', [(i, (i + k) % group_count) for i in range(group_co...  8.04 us
    all_to_all x3, waiting for transfers between devices, exchange(): x = lax.all_to_all(x, both, split_axis=0, concat_axis=0, tiled=True)  7.23 us
    unnamed x24, local copies, waits for them, and re-layouts  2.82 us
  transfers between devices with their start and end apart: 11, of which 5 were waited for; matrix products, arithmetic and copies ran while one was open for 3% of the time, Pallas kernels for 43%

profile of v11, /device:TPU:0, one launch (start us, length us, event | category | flops | bytes accessed | tf_op | source)
XLA Modules:
  0.0 99.3 jit_solution(12822305163125111514)
XLA Ops:
  0.6 0.0 copy-start.6
  0.6 1.2 %copy.28 = f32[1,16,8,2,240]{4,1,3,2,0:T(8,128)S(1)} copy(f32[1,16,8,2,240]{4,3,2,1,0:T(2,128)} %param.16) | data formatting | bytes 491520 | tf_op args[7]
  1.8 2.1 %slots.1 = (f32[128,128]{1,0:T(8,128)}, f32[8,512]{1,0:T(8,128)}, f32[512,8]{1,0:T(8,128)}) custom-call(s32[1]{0:T(128)} %bitcast.shift_ref, s32[1,512]{1,0:T(1,128)} %bitcast.51, s32[1,512]{1,0:T(1,128)} %bitcast.52, f32[8,512]{1,0:T(8,128)} %taps_ref.1, s32[2,512]{1,0:T(2,128)} %pairs_ref.1, f32[1,512]{1,0:T(1,128)} %bitcast.53, s32[1,512]{1,0:T(1,128)} %bitcast.54), custom_call_target="tpu_custom_call" | custom-call | flops 1000000000 | bytes 1000000 | tf_op jit(solution)/shard_map/slots/pallas_call | solution.py:501
  3.9 7.3 %all-to-all-start = ((f32[32,4,128]{2,1,0:T(4,128)}), f32[32,4,128]{2,1,0:T(4,128)S(1)}, u32[]{:S(2)}, u32[]{:S(2)}) async-start(f32[32,4,128]{2,1,0:T(4,128)} %bitcast.50), calls=%async_computation | async-start | bytes 131072 | tf_op jit(solution)/shard_map/all_to_all | solution.py:525
  11.2 2.7 %collective-permute-start.2 = (f32[8,2,16,240]{3,2,1,0:T(8,128)S(1)}, f32[8,2,16,240]{3,2,1,0:T(8,128)S(1)}, u32[]{:S(2)}, u32[]{:S(2)}) collective-permute-start(f32[8,2,16,240]{3,2,1,0:T(8,128)S(1)} %bitcast.37), channel_id=1, source_target_pairs={{0,2},{1,3},{2,0},{3,1},{4,6},{5,7},{6,4},{7,5},{8,10},{9,11},{10,... | collective-permute-start | bytes 737288 | tf_op jit(solution)/shard_map/ppermute | solution.py:534
  14.0 1.5 %collective-permute-start.1 = (f32[8,2,16,240]{3,2,1,0:T(8,128)S(1)}, f32[8,2,16,240]{3,2,1,0:T(8,128)S(1)}, u32[]{:S(2)}, u32[]{:S(2)}) collective-permute-start(f32[8,2,16,240]{3,2,1,0:T(8,128)S(1)} %bitcast.38), channel_id=1, source_target_pairs={{0,1},{1,2},{2,3},{3,0},{4,5},{5,6},{6,7},{7,4},{8,9},{9,10},{10,1... | collective-permute-start | bytes 737288 | tf_op jit(solution)/shard_map/ppermute | solution.py:534
  15.5 1.5 %collective-permute-start = (f32[8,2,16,240]{3,2,1,0:T(8,128)S(1)}, f32[8,2,16,240]{3,2,1,0:T(8,128)S(1)}, u32[]{:S(2)}, u32[]{:S(2)}) collective-permute-start(f32[8,2,16,240]{3,2,1,0:T(8,128)S(1)} %bitcast.39), channel_id=1, source_target_pairs={{0,4},{4,8},{8,12},{12,16},{16,20},{20,24},{24,28},{1,5},{5,9},{9,... | collective-permute-start | bytes 737288 | tf_op jit(solution)/shard_map/ppermute | solution.py:543
  17.0 2.1 %all-to-all-done = f32[32,4,128]{2,1,0:T(4,128)S(1)} async-done(((f32[32,4,128]{2,1,0:T(4,128)}), f32[32,4,128]{2,1,0:T(4,128)S(1)}, u32[]{:S(2)}, u32[]{:S(2)}) %all-to-all-start) | async-done | bytes 65568 | tf_op jit(solution)/shard_map/all_to_all | solution.py:525
  19.1 0.1 copy.20
  19.2 0.6 fusion.2.base_ref
  19.8 0.0 copy-done.5
  19.8 11.9 %degrid.1 = (f32[256,128]{1,0:T(8,128)}, f32[1024,256]{1,0:T(8,128)}) custom-call(s32[32,32]{1,0:T(8,128)} %fusion.2.base_ref, f32[128,128]{1,0:T(8,128)} %bitcast.47, f32[16,2048,128]{2,1,0:T(8,128)} %bitcast.45), custom_call_target="tpu_custom_call" | custom-call | flops 100000000 | bytes 70000000 | tf_op jit(solution)/shard_map/degrid/pallas_call | solution.py:548
  31.7 3.0 %all-to-all-start.1 = ((f32[32,8,128]{2,1,0:T(8,128)}), f32[32,8,128]{2,1,0:T(8,128)S(1)}, u32[]{:S(2)}, u32[]{:S(2)}) async-start(f32[32,8,128]{2,1,0:T(8,128)} %bitcast.49), calls=%async_computation.1 | async-start | bytes 262144 | tf_op jit(solution)/shard_map/all_to_all | solution.py:525
  34.7 0.0 collective-permute-done.2.rest_2_
  34.7 0.0 copy-start.8
  34.7 0.0 collective-permute-done.1.rest_1_
  34.7 0.0 copy-start.9
  34.7 0.0 collective-permute-done
  34.7 0.0 copy-start.7
  34.7 3.7 %collective-permute-start.3 = (f32[8,2,16,240]{3,2,1,0:T(8,128)S(1)}, f32[8,2,16,240]{3,2,1,0:T(8,128)S(1)}, u32[]{:S(2)}, u32[]{:S(2)}) collective-permute-start(f32[8,2,16,240]{3,2,1,0:T(8,128)S(1)} %bitcast.40), channel_id=1, source_target_pairs={{0,3},{1,0},{2,1},{3,2},{4,7},{5,4},{6,5},{7,6},{8,11},{9,8},{10,9... | collective-permute-start | bytes 737288 | tf_op jit(solution)/shard_map/ppermute | solution.py:534
  38.4 0.0 copy-done.9
  38.4 0.0 copy-done.6
  38.5 1.0 %copy.24.vis_ref = bf16[512,512]{1,0:T(8,128)(2,1)} copy(bf16[512,512]{0,1:T(8,128)(2,1)S(1)} %bitcast.46) | data formatting | bytes 1048576 | tf_op jit(solution)/shard_map/reshape | solution.py:574
  39.5 1.3 %collective-permute-start.4 = (f32[8,2,16,240]{3,2,1,0:T(8,128)S(1)}, f32[8,2,16,240]{3,2,1,0:T(8,128)}, u32[]{:S(2)}, u32[]{:S(2)}) collective-permute-start(f32[8,2,16,240]{3,2,1,0:T(8,128)S(1)} %bitcast.41), channel_id=1, source_target_pairs={{4,0},{8,4},{12,8},{16,12},{20,16},{24,20},{28,24},{5,1},{9,5},{13... | collective-permute-start | bytes 737288 | tf_op jit(solution)/shard_map/ppermute | solution.py:571
  40.8 2.5 %all-to-all-done.1 = f32[32,8,128]{2,1,0:T(8,128)S(1)} async-done(((f32[32,8,128]{2,1,0:T(8,128)}), f32[32,8,128]{2,1,0:T(8,128)S(1)}, u32[]{:S(2)}, u32[]{:S(2)}) %all-to-all-start.1) | async-done | bytes 131104 | tf_op jit(solution)/shard_map/all_to_all | solution.py:525
  43.3 2.0 %collective-permute-done.3.rest_3_ = f32[8,2,16,240]{3,2,1,0:T(8,128)S(1)} collective-permute-done((f32[8,2,16,240]{3,2,1,0:T(8,128)S(1)}, f32[8,2,16,240]{3,2,1,0:T(8,128)S(1)}, u32[]{:S(2)}, u32[]{:S(2)}) %collective-permute-start.3) | collective-permute-done | bytes 245792 | tf_op jit(solution)/shard_map/ppermute | solution.py:534
  45.3 0.0 copy-done.7
  45.3 0.7 copy-done.10
  46.0 0.0 copy-done.8
  46.0 0.0 copy-done.2
  46.0 0.0 copy-done.3
  46.0 0.0 copy-start
  46.0 0.0 copy-start.1
  46.0 16.8 %rowgrads.1 = (f32[8,2,16,240]{3,2,1,0:T(8,128)S(1)}, f32[8,2,16,240]{3,2,1,0:T(8,128)S(1)}, f32[8,2,16,240]{3,2,1,0:T(8,128)S(1)}, f32[8,2,16,240]{3,2,1,0:T(8,128)S(1)}, f32[256,128]{1,0:T(8,128)}) custom-call(f32[8,512]{1,0:T(8,128)S(1)} %copy-done.3, f32[512,8]{1,0:T(8,128)S(1)} %copy-done.2, bf16[512,512]{1,0:T(8,128)(2,1)} %copy.24.vis_ref, ...), custom_call_target="tpu_custom_call" | custom-call | flops 20000000000 | bytes 10000000 | tf_op jit(solution)/shard_map/rowgrads/pallas_call | solution.py:578
  62.8 5.5 %all-to-all-start.2 = ((f32[32,8,128]{2,1,0:T(8,128)}), f32[32,8,128]{2,1,0:T(8,128)S(1)}, u32[]{:S(2)}, u32[]{:S(2)}) async-start(f32[32,8,128]{2,1,0:T(8,128)} %bitcast.17), calls=%async_computation.2 | async-start | bytes 262144 | tf_op jit(solution)/shard_map/all_to_all | solution.py:525
  68.3 3.7 %collective-permute-start.5 = (f32[8,2,16,240]{3,2,1,0:T(8,128)S(1)}, f32[8,2,16,240]{3,2,1,0:T(8,128)S(1)}, u32[]{:S(2)}, u32[]{:S(2)}) collective-permute-start(f32[8,2,16,240]{3,2,1,0:T(8,128)S(1)} %get-tuple-element.39), channel_id=1, source_target_pairs={{0,3},{1,0},{2,1},{3,2},{4,7},{5,4},{6,5},{7,6},{8,11},{9,8},{10,9... | collective-permute-start | bytes 737288 | tf_op jit(solution)/shard_map/ppermute | solution.py:534
  72.0 0.0 collective-permute-start.6
  72.0 1.1 %collective-permute-start.7 = (f32[8,2,16,240]{3,2,1,0:T(8,128)S(1)}, f32[8,2,16,240]{3,2,1,0:T(8,128)}, u32[]{:S(2)}, u32[]{:S(2)}) collective-permute-start(f32[8,2,16,240]{3,2,1,0:T(8,128)S(1)} %get-tuple-element.41), channel_id=1, source_target_pairs={{0,1},{1,2},{2,3},{3,0},{4,5},{5,6},{6,7},{7,4},{8,9},{9,10},{10,1... | collective-permute-start | bytes 737288 | tf_op jit(solution)/shard_map/ppermute | solution.py:534
  73.1 0.0 collective-permute-done.4
  73.1 0.0 copy-done.4
  73.1 1.2 %multiply_add_fusion = f32[8,2,16,240]{3,2,1,0:T(8,128)S(1)} fusion(f32[8,2,16,240]{3,2,1,0:T(8,128)S(1)} %get-tuple-element.34, f32[8,2,16,240]{3,2,1,0:T(8,128)} %collective-permute-done.4, f32[8,2,16,240]{3,2,1,0:T(8,128)} %copy-done.7, pred[]{:T(512)S(6)} %lt.3, pred[]{:T(512)S(6)} %gt.3, f32[1,16,8,2,240]{4,3,2,1,0:T(2,128)S(1)} %copy-done.4), kind=kLoop, calls=%fused_computation.2 | loop fusion | flops 430080 | bytes 1228802 | tf_op jit(solution)/shard_map/add | solution.py:606
  74.3 2.6 %all-to-all-done.2 = f32[32,8,128]{2,1,0:T(8,128)S(1)} async-done(((f32[32,8,128]{2,1,0:T(8,128)}), f32[32,8,128]{2,1,0:T(8,128)S(1)}, u32[]{:S(2)}, u32[]{:S(2)}) %all-to-all-start.2) | async-done | bytes 131104 | tf_op jit(solution)/shard_map/all_to_all | solution.py:525
  76.9 14.3 %scatter.1 = f32[16,2048,128]{2,1,0:T(8,128)} custom-call(s32[32,32]{1,0:T(8,128)S(1)} %copy-done.1, f32[256,128]{1,0:T(8,128)S(1)} %bitcast.36, f32[1024,256]{1,0:T(8,128)S(1)} %copy-done), custom_call_target="tpu_custom_call" | custom-call | bytes 100000 | tf_op jit(solution)/shard_map/scatter/pallas_call | solution.py:609
  91.3 0.0 collective-permute-done.5
  91.3 6.1 %collective-permute-done.6 = f32[8,2,16,240]{3,2,1,0:T(8,128)S(1)} collective-permute-done((f32[8,2,16,240]{3,2,1,0:T(8,128)S(1)}, f32[8,2,16,240]{3,2,1,0:T(8,128)S(1)}, u32[]{:S(2)}, u32[]{:S(2)}) %collective-permute-start.6) | collective-permute-done | bytes 245792 | tf_op jit(solution)/shard_map/ppermute | solution.py:534
  97.4 0.0 collective-permute-done.7
  97.4 1.0 %add_bitcast_fusion = f32[1,16,8,2,240]{4,1,3,2,0:T(8,128)S(1)} fusion(f32[8,2,16,240]{3,2,1,0:T(8,128)} %collective-permute-done.7, f32[8,2,16,240]{3,2,1,0:T(8,128)S(1)} %collective-permute-done.6, f32[8,2,16,240]{3,2,1,0:T(8,128)S(1)} %multiply_add_fusion, f32[8,2,16,240]{3,2,1,0:T(8,128)S(1)} %collective-permute-done.5), kind=kLoop, calls=%fused_computation.1 | loop fusion | flops 184320 | bytes 1228800 | tf_op jit(solution)/shard_map/broadcast_in_dim | solution.py:632
  98.4 0.9 copy.23
  (8 shorter events, 0.0 us)
Async XLA Ops:
  0.6 37.8 %copy-start.6 = (bf16[512,2,240]{0,2,1:T(8,128)(2,1)S(1)}, bf16[512,2,240]{0,2,1:T(8,128)(2,1)}, u32[]{:S(2)}) copy-start(bf16[512,2,240]{0,2,1:T(8,128)(2,1)} %param.9) | copy-start | bytes 1474564
  3.9 42.1 %copy-start.2 = (f32[512,8]{1,0:T(8,128)S(1)}, f32[512,8]{1,0:T(8,128)}, u32[]{:S(2)}) copy-start(f32[512,8]{1,0:T(8,128)} %get-tuple-element.25.cols_ref) | copy-start | bytes 49156
  3.9 42.1 %copy-start.3 = (f32[8,512]{1,0:T(8,128)S(1)}, f32[8,512]{1,0:T(8,128)}, u32[]{:S(2)}) copy-start(f32[8,512]{1,0:T(8,128)} %get-tuple-element.24.rows_ref) | copy-start | bytes 49156
  3.9 15.1 %all-to-all-start = ((f32[32,4,128]{2,1,0:T(4,128)}), f32[32,4,128]{2,1,0:T(4,128)S(1)}, u32[]{:S(2)}, u32[]{:S(2)}) async-start(f32[32,4,128]{2,1,0:T(4,128)} %bitcast.50), calls=%async_computation | async-start | bytes 131072 | tf_op jit(solution)/shard_map/all_to_all | solution.py:525
  11.2 23.4 %collective-permute-start.2 = (f32[8,2,16,240]{3,2,1,0:T(8,128)S(1)}, f32[8,2,16,240]{3,2,1,0:T(8,128)S(1)}, u32[]{:S(2)}, u32[]{:S(2)}) collective-permute-start(f32[8,2,16,240]{3,2,1,0:T(8,128)S(1)} %bitcast.37), channel_id=1, source_target_pairs={{0,2},{1,3},{2,0},{3,1},{4,6},{5,7},{6,4},{7,5},{8,10},{9,11},{10,... | collective-permute-start | bytes 737288 | tf_op jit(solution)/shard_map/ppermute | solution.py:534
  14.0 20.7 %collective-permute-start.1 = (f32[8,2,16,240]{3,2,1,0:T(8,128)S(1)}, f32[8,2,16,240]{3,2,1,0:T(8,128)S(1)}, u32[]{:S(2)}, u32[]{:S(2)}) collective-permute-start(f32[8,2,16,240]{3,2,1,0:T(8,128)S(1)} %bitcast.38), channel_id=1, source_target_pairs={{0,1},{1,2},{2,3},{3,0},{4,5},{5,6},{6,7},{7,4},{8,9},{9,10},{10,1... | collective-permute-start | bytes 737288 | tf_op jit(solution)/shard_map/ppermute | solution.py:534
  15.5 19.2 %collective-permute-start = (f32[8,2,16,240]{3,2,1,0:T(8,128)S(1)}, f32[8,2,16,240]{3,2,1,0:T(8,128)S(1)}, u32[]{:S(2)}, u32[]{:S(2)}) collective-permute-start(f32[8,2,16,240]{3,2,1,0:T(8,128)S(1)} %bitcast.39), channel_id=1, source_target_pairs={{0,4},{4,8},{8,12},{12,16},{16,20},{20,24},{24,28},{1,5},{5,9},{9,... | collective-permute-start | bytes 737288 | tf_op jit(solution)/shard_map/ppermute | solution.py:543
  19.1 0.8 copy-start.5
  31.7 11.6 %all-to-all-start.1 = ((f32[32,8,128]{2,1,0:T(8,128)}), f32[32,8,128]{2,1,0:T(8,128)S(1)}, u32[]{:S(2)}, u32[]{:S(2)}) async-start(f32[32,8,128]{2,1,0:T(8,128)} %bitcast.49), calls=%async_computation.1 | async-start | bytes 262144 | tf_op jit(solution)/shard_map/all_to_all | solution.py:525
  34.7 11.3 %copy-start.8 = (f32[8,2,16,240]{3,2,1,0:T(8,128)}, f32[8,2,16,240]{3,2,1,0:T(8,128)S(1)}, u32[]{:S(2)}) copy-start(f32[8,2,16,240]{3,2,1,0:T(8,128)S(1)} %collective-permute-done.2.rest_2_) | copy-start | bytes 737284
  34.7 3.7 %copy-start.9 = (f32[8,2,16,240]{3,2,1,0:T(8,128)}, f32[8,2,16,240]{3,2,1,0:T(8,128)S(1)}, u32[]{:S(2)}) copy-start(f32[8,2,16,240]{3,2,1,0:T(8,128)S(1)} %collective-permute-done.1.rest_1_) | copy-start | bytes 737284
  34.7 10.5 %copy-start.7 = (f32[8,2,16,240]{3,2,1,0:T(8,128)}, f32[8,2,16,240]{3,2,1,0:T(8,128)S(1)}, u32[]{:S(2)}) copy-start(f32[8,2,16,240]{3,2,1,0:T(8,128)S(1)} %collective-permute-done) | copy-start | bytes 737284
  34.7 10.5 %collective-permute-start.3 = (f32[8,2,16,240]{3,2,1,0:T(8,128)S(1)}, f32[8,2,16,240]{3,2,1,0:T(8,128)S(1)}, u32[]{:S(2)}, u32[]{:S(2)}) collective-permute-start(f32[8,2,16,240]{3,2,1,0:T(8,128)S(1)} %bitcast.40), channel_id=1, source_target_pairs={{0,3},{1,0},{2,1},{3,2},{4,7},{5,4},{6,5},{7,6},{8,11},{9,8},{10,9... | collective-permute-start | bytes 737288 | tf_op jit(solution)/shard_map/ppermute | solution.py:534
  39.5 33.6 %collective-permute-start.4 = (f32[8,2,16,240]{3,2,1,0:T(8,128)S(1)}, f32[8,2,16,240]{3,2,1,0:T(8,128)}, u32[]{:S(2)}, u32[]{:S(2)}) collective-permute-start(f32[8,2,16,240]{3,2,1,0:T(8,128)S(1)} %bitcast.41), channel_id=1, source_target_pairs={{4,0},{8,4},{12,8},{16,12},{20,16},{24,20},{28,24},{5,1},{9,5},{13... | collective-permute-start | bytes 737288 | tf_op jit(solution)/shard_map/ppermute | solution.py:571
  45.3 0.7 copy-start.10
  46.0 27.1 %copy-start.4 = (f32[1,16,8,2,240]{4,3,2,1,0:T(2,128)S(1)}, f32[1,16,8,2,240]{4,3,2,1,0:T(2,128)}, u32[]{:S(2)}) copy-start(f32[1,16,8,2,240]{4,3,2,1,0:T(2,128)} %param.16) | copy-start | bytes 737284
  46.0 30.9 %copy-start = (f32[1024,256]{1,0:T(8,128)S(1)}, f32[1024,256]{1,0:T(8,128)}, u32[]{:S(2)}) copy-start(f32[1024,256]{1,0:T(8,128)} %get-tuple-element.38.w_ref) | copy-start | bytes 3145732
  46.0 30.9 %copy-start.1 = (s32[32,32]{1,0:T(8,128)S(1)}, s32[32,32]{1,0:T(8,128)}, u32[]{:S(2)}) copy-start(s32[32,32]{1,0:T(8,128)} %fusion.2.base_ref) | copy-start | bytes 12292
  62.8 14.1 %all-to-all-start.2 = ((f32[32,8,128]{2,1,0:T(8,128)}), f32[32,8,128]{2,1,0:T(8,128)S(1)}, u32[]{:S(2)}, u32[]{:S(2)}) async-start(f32[32,8,128]{2,1,0:T(8,128)} %bitcast.17), calls=%async_computation.2 | async-start | bytes 262144 | tf_op jit(solution)/shard_map/all_to_all | solution.py:525
  68.3 23.0 %collective-permute-start.5 = (f32[8,2,16,240]{3,2,1,0:T(8,128)S(1)}, f32[8,2,16,240]{3,2,1,0:T(8,128)S(1)}, u32[]{:S(2)}, u32[]{:S(2)}) collective-permute-start(f32[8,2,16,240]{3,2,1,0:T(8,128)S(1)} %get-tuple-element.39), channel_id=1, source_target_pairs={{0,3},{1,0},{2,1},{3,2},{4,7},{5,4},{6,5},{7,6},{8,11},{9,8},{10,9... | collective-permute-start | bytes 737288 | tf_op jit(solution)/shard_map/ppermute | solution.py:534
  72.0 25.4 %collective-permute-start.6 = (f32[8,2,16,240]{3,2,1,0:T(8,128)S(1)}, f32[8,2,16,240]{3,2,1,0:T(8,128)S(1)}, u32[]{:S(2)}, u32[]{:S(2)}) collective-permute-start(f32[8,2,16,240]{3,2,1,0:T(8,128)S(1)} %get-tuple-element.40), channel_id=1, source_target_pairs={{0,2},{1,3},{2,0},{3,1},{4,6},{5,7},{6,4},{7,5},{8,10},{9,11},{10,... | collective-permute-start | bytes 737288 | tf_op jit(solution)/shard_map/ppermute | solution.py:534
  72.0 25.4 %collective-permute-start.7 = (f32[8,2,16,240]{3,2,1,0:T(8,128)S(1)}, f32[8,2,16,240]{3,2,1,0:T(8,128)}, u32[]{:S(2)}, u32[]{:S(2)}) collective-permute-start(f32[8,2,16,240]{3,2,1,0:T(8,128)S(1)} %get-tuple-element.41), channel_id=1, source_target_pairs={{0,1},{1,2},{2,3},{3,0},{4,5},{5,6},{6,7},{7,4},{8,9},{9,10},{10,1... | collective-permute-start | bytes 737288 | tf_op jit(solution)/shard_map/ppermute | solution.py:534
